TPU v7x, 32 devices: a whole 2x2x4 slice. The times are simulated.
32 devices in a mesh: dp: 8 (over z, y), row: 2 (over x), col: 2 (over core).
Axes of the slice: x: 2, y: 2, z: 4, core: 2. Of those that a mesh axis runs over, the one named last changes fastest.
Arguments:
- activations: bfloat16 [16384, 2048], P(('dp', 'row'), 'col'), may hold values from -6 to 6
- grad_out: bfloat16 [16384, 2048], P(('dp', 'row'), 'col'), may hold values from -6 to 6
- segments: int32 [8, 2048], P('dp'), may hold values from 0 to 15, never falling along the last dimension, each value on 1 to 1792 neighbouring positions
- first_gain: float32 [2048], P('col'), may hold values from 0.5 to 1.5
- query_weight: bfloat16 [2048, 2048], P('col', 'row'), may hold values from -0.125 to 0.125
- key_weight: bfloat16 [2048, 512], P('col', 'row'), may hold values from -0.125 to 0.125
- value_weight: bfloat16 [2048, 512], P('col', 'row'), may hold values from -0.125 to 0.125
- query_down: bfloat16 [2048, 8], P('col'), may hold values from -0.125 to 0.125
- query_up: bfloat16 [8, 2048], P(None, 'row'), may hold values from -1.5 to 1.5
- key_down: bfloat16 [2048, 8], P('col'), may hold values from -0.125 to 0.125
- key_up: bfloat16 [8, 512], P(None, 'row'), may hold values from -1.5 to 1.5
- value_down: bfloat16 [2048, 8], P('col'), may hold values from -0.125 to 0.125
- value_up: bfloat16 [8, 512], P(None, 'row'), may hold values from -1.5 to 1.5
- query_map: bfloat16 [32, 64, 64], P('row'), may hold values from -0.75 to 0.75
- key_map: bfloat16 [8, 64, 64], P('row'), may hold values from -0.75 to 0.75
- output_weight: bfloat16 [2048, 2048], P('row', 'col'), may hold values from -0.25 to 0.25
- output_down: bfloat16 [2048, 8], P('row'), may hold values from -0.25 to 0.25
- output_up: bfloat16 [8, 2048], P(None, 'col'), may hold values from -1.5 to 1.5
- second_gain: float32 [2048], P('col'), may hold values from 0.5 to 1.5
- gate_weight: bfloat16 [2048, 8192], P('col', 'row'), may hold values from -0.125 to 0.125
- up_weight: bfloat16 [2048, 8192], P('col', 'row'), may hold values from -0.125 to 0.125
- down_weight: bfloat16 [8192, 2048], P('row', 'col'), may hold values from -0.09375 to 0.09375
Outputs:
- result: bfloat16 [16384, 2048], P(('dp', 'row'), 'col')
- grad_activations: float32 [16384, 2048], P(('dp', 'row'), 'col')
- grad_first_gain: float32 [2048], P('col')
- grad_query_weight: float32 [2048, 2048], P(('col', 'dp'), 'row')
- grad_key_weight: float32 [2048, 512], P(('col', 'dp'), 'row')
- grad_value_weight: float32 [2048, 512], P(('col', 'dp'), 'row')
- grad_query_down: float32 [2048, 8], P('col')
- grad_query_up: float32 [8, 2048], P(None, 'row')
- grad_key_down: float32 [2048, 8], P('col')
- grad_key_up: float32 [8, 512], P(None, 'row')
- grad_value_down: float32 [2048, 8], P('col')
- grad_value_up: float32 [8, 512], P(None, 'row')
- grad_query_map: float32 [32, 64, 64], P('row')
- grad_key_map: float32 [8, 64, 64], P('row')
- grad_output_weight: float32 [2048, 2048], P(('row', 'dp'), 'col')
- grad_output_down: float32 [2048, 8], P('row')
- grad_output_up: float32 [8, 2048], P(None, 'col')
- grad_second_gain: float32 [2048], P('col')
- grad_gate_weight: float32 [2048, 8192], P(('col', 'dp'), 'row')
- grad_up_weight: float32 [2048, 8192], P(('col', 'dp'), 'row')
- grad_down_weight: float32 [8192, 2048], P('row', ('col', 'dp'))
Inputs may be any that keep to these rules, and one draw needn't show every extreme that they name: `segments`: in every sequence the document numbers never fall, every number from 0 to 15 is used, each document has 1 to 1792 positions and one has exactly 1792.
All inputs are finite; a program needn't handle non-finite values.
Results may differ from a plain program's by a relative error of at most 0.02.
Values may be sent and summed in bfloat16 or wider, within the bound.
A program may use at most 448 MiB of HBM per device.

v0:
```python
import math

import jax
import jax.numpy as jnp
from jax import lax
from jax.sharding import PartitionSpec as P

D = 2048
HEAD_DIM = 64
WINDOW = 64
BLOCK = 512


norm_eps = 1e-05


def matmul(left, right):
    return jnp.dot(left, right, preferred_element_type=jnp.float32)


def times_transposed(left, right):
    return lax.dot_general(
        left, right, (((1,), (1,)), ((), ())), preferred_element_type=jnp.float32
    )


def inner_rows(left, right):
    return lax.dot_general(
        left, right, (((0,), (0,)), ((), ())), preferred_element_type=jnp.float32
    )


def col_total(values):
    return lax.psum(values, "col")


def gather_rows(values):
    return lax.all_gather(values, "row", axis=0, tiled=True)


def gather_heads(values):
    return lax.all_gather(values, "col", axis=1, tiled=True)


def sum_cols_attention(larger, smaller):
    copies = jnp.tile(smaller, (1, lax.axis_size("col")))
    return (
        lax.psum_scatter(larger, "col", scatter_dimension=1, tiled=True),
        lax.psum_scatter(copies, "col", scatter_dimension=1, tiled=True),
    )


def sum_rows_attention(larger, smaller):
    return (
        lax.psum_scatter(larger, "row", scatter_dimension=0, tiled=True),
        lax.psum_scatter(smaller, "row", scatter_dimension=0, tiled=True),
    )


def sum_rows_mlp(left, right, transposed, row_total):

    def term(first_row, piece_rows):
        if transposed:
            return times_transposed(left, right)
        return matmul(left, right)

    return lax.psum_scatter(
        term(jnp.int32(0), lax.axis_size("row") * row_total), "row", scatter_dimension=0, tiled=True
    )


def by_parts(weight, count):
    return weight.reshape(weight.shape[0], count, weight.shape[1] // count)


def place_slot(values, along, count, where):
    width = values.shape[along]
    full_shape = list(values.shape)
    full_shape[along] = width * count
    return lax.dynamic_update_slice_in_dim(
        jnp.zeros(tuple(full_shape), values.dtype), values, where * width, along
    )


def take_slot(values, along, count, where):
    width = values.shape[along] // count
    return lax.dynamic_slice_in_dim(values, where * width, width, along)


def feature_map(heads, weights):
    before = jnp.einsum("lhd,hde->lhe", heads, weights, precision=lax.Precision.HIGHEST)
    return jnp.concatenate(
        [jax.nn.softmax(before, axis=-1), jax.nn.softmax(-before, axis=-1)], axis=-1
    )


def norm_backward(grad_normed, gain, hat_rows, scale_rows):
    grad_hat = grad_normed * gain
    inner_total = col_total(jnp.sum(grad_hat * hat_rows, axis=1))
    grad_input = scale_rows[:, None] * (grad_hat - hat_rows * (inner_total / D)[:, None])
    return (grad_input, jnp.sum(grad_normed * hat_rows, axis=0))


def pad_front(values):
    return jnp.concatenate([jnp.zeros((WINDOW,) + values.shape[1:], values.dtype), values], axis=0)


def block_masks(query_documents, tile_documents):
    offsets = (
        jnp.arange(BLOCK, dtype=jnp.int32)[:, None]
        + WINDOW
        - jnp.arange(BLOCK + WINDOW, dtype=jnp.int32)[None, :]
    )
    same_doc = query_documents[:, None] == tile_documents[None, :]
    window_mask = same_doc & (offsets >= 0) & (offsets < WINDOW)
    linear_mask = same_doc & (offsets >= WINDOW)
    return (window_mask, linear_mask)


def take_block(arrays, block_index):
    query_heads, query_features, key_pad, value_pad, feature_pad, documents, padded_documents = (
        arrays
    )
    first_row = block_index * BLOCK
    return (
        lax.dynamic_slice_in_dim(query_heads, first_row, BLOCK, 0),
        lax.dynamic_slice_in_dim(query_features, first_row, BLOCK, 0),
        lax.dynamic_slice_in_dim(key_pad, first_row, BLOCK + WINDOW, 0),
        lax.dynamic_slice_in_dim(value_pad, first_row, BLOCK + WINDOW, 0),
        lax.dynamic_slice_in_dim(feature_pad, first_row, BLOCK + WINDOW, 0),
        lax.dynamic_slice_in_dim(documents, first_row, BLOCK, 0),
        lax.dynamic_slice_in_dim(padded_documents, first_row, BLOCK + WINDOW, 0),
    )


def tile_weights(query_block, query_features, key_tile, key_features, window_mask, linear_mask):
    score_scale = 1.0 / math.sqrt(HEAD_DIM)
    scores = (
        jnp.einsum("qgrd,kgd->grqk", query_block, key_tile, preferred_element_type=jnp.float32)
        * score_scale
    )
    linear = jnp.einsum(
        "qgrf,kgf->grqk", query_features, key_features, preferred_element_type=jnp.float32
    )
    exponent = jnp.exp(jnp.where(window_mask, scores, 0.0))
    weights = jnp.where(window_mask, exponent, 0.0) + jnp.where(linear_mask, linear, 0.0)
    return (weights, exponent)


def forward_block(arrays, carried, block_index):
    linear_state, norm_state, last_document = carried
    (
        query_block,
        query_features,
        key_tile,
        value_tile,
        key_features,
        query_documents,
        tile_documents,
    ) = take_block(arrays, block_index)
    window_mask, linear_mask = block_masks(query_documents, tile_documents)
    weights, exponent = tile_weights(
        query_block, query_features, key_tile, key_features, window_mask, linear_mask
    )
    same_flag = (query_documents == last_document).astype(jnp.float32)
    through = jnp.einsum(
        "qgrf,gfd->grqd",
        query_features,
        linear_state.astype(jnp.bfloat16),
        preferred_element_type=jnp.float32,
    )
    normal = jnp.einsum(
        "qgrf,gf->grq",
        query_features.astype(jnp.float32),
        norm_state,
        precision=lax.Precision.HIGHEST,
    )
    totals = jnp.sum(weights, axis=-1) + same_flag * normal
    probabilities = (weights / totals[..., None]).astype(jnp.bfloat16)
    mixed_rows = (
        jnp.einsum("grqk,kgd->grqd", probabilities, value_tile, preferred_element_type=jnp.float32)
        + (same_flag / totals)[..., None] * through
    )
    next_document = tile_documents[BLOCK - 1]
    keep_flag = (last_document == next_document).astype(jnp.float32)
    member = tile_documents[:BLOCK] == next_document
    key_member = jnp.where(
        member[:, None, None], key_features[:BLOCK], jnp.zeros_like(key_features[:BLOCK])
    )
    added_state = jnp.einsum(
        "kgf,kgd->gfd", key_member, value_tile[:BLOCK], preferred_element_type=jnp.float32
    )
    new_state = keep_flag * linear_state + added_state
    new_norm = keep_flag * norm_state + jnp.sum(key_member.astype(jnp.float32), axis=0)
    return (
        (new_state, new_norm, next_document),
        (mixed_rows, linear_state, norm_state, last_document, totals),
    )


def backward_block(arrays, carried, block_inputs):
    grad_next, norm_next = carried
    block_index, linear_state, norm_state, last_document, totals, grad_block = block_inputs
    (
        query_block,
        query_features,
        key_tile,
        value_tile,
        key_features,
        query_documents,
        tile_documents,
    ) = take_block(arrays, block_index)
    window_mask, linear_mask = block_masks(query_documents, tile_documents)
    weights, exponent = tile_weights(
        query_block, query_features, key_tile, key_features, window_mask, linear_mask
    )
    same_flag = (query_documents == last_document).astype(jnp.float32)
    state_low = linear_state.astype(jnp.bfloat16)
    through = jnp.einsum(
        "qgrf,gfd->grqd", query_features, state_low, preferred_element_type=jnp.float32
    )
    ratio_rows = weights / totals[..., None]
    probabilities = ratio_rows.astype(jnp.bfloat16)
    grad_value_tile = jnp.einsum(
        "grqk,qgrd->kgd", probabilities, grad_block, preferred_element_type=jnp.float32
    )
    grad_probs = jnp.einsum(
        "qgrd,kgd->grqk", grad_block, value_tile, preferred_element_type=jnp.float32
    )
    grad_float = jnp.transpose(grad_block, (1, 2, 0, 3)).astype(jnp.float32)
    grad_through = ((same_flag / totals)[..., None] * grad_float).astype(jnp.bfloat16)
    grad_totals = (
        -(
            jnp.sum(grad_probs * ratio_rows, axis=-1)
            + same_flag * jnp.sum(grad_float * through, axis=-1) / totals
        )
        / totals
    )
    grad_weights = grad_probs / totals[..., None] + grad_totals[..., None]
    grad_scores = jnp.where(window_mask, exponent * grad_weights, 0.0).astype(jnp.bfloat16)
    grad_linear = jnp.where(linear_mask, grad_weights, 0.0).astype(jnp.bfloat16)
    score_scale = 1.0 / math.sqrt(HEAD_DIM)
    grad_query = (
        jnp.einsum("grqk,kgd->qgrd", grad_scores, key_tile, preferred_element_type=jnp.float32)
        * score_scale
    )
    grad_key_tile = (
        jnp.einsum("grqk,qgrd->kgd", grad_scores, query_block, preferred_element_type=jnp.float32)
        * score_scale
    )
    flag_totals = same_flag * grad_totals
    grad_query_features = (
        jnp.einsum("grqk,kgf->qgrf", grad_linear, key_features, preferred_element_type=jnp.float32)
        + jnp.einsum("grqd,gfd->qgrf", grad_through, state_low, preferred_element_type=jnp.float32)
        + jnp.transpose(flag_totals, (2, 0, 1))[..., None] * norm_state[None, :, None, :]
    )
    grad_feature_tile = jnp.einsum(
        "grqk,qgrf->kgf", grad_linear, query_features, preferred_element_type=jnp.float32
    )
    grad_state_direct = jnp.einsum(
        "qgrf,grqd->gfd", query_features, grad_through, preferred_element_type=jnp.float32
    )
    grad_norm_direct = jnp.einsum(
        "grq,qgrf->gf",
        flag_totals,
        query_features.astype(jnp.float32),
        precision=lax.Precision.HIGHEST,
    )
    next_document = tile_documents[BLOCK - 1]
    keep_flag = (last_document == next_document).astype(jnp.float32)
    member = (tile_documents[:BLOCK] == next_document)[:, None, None]
    grad_state = (grad_state_direct + keep_flag * grad_next.astype(jnp.float32)).astype(
        jnp.bfloat16
    )
    grad_norm = grad_norm_direct + keep_flag * norm_next
    feature_added = (
        jnp.einsum(
            "kgd,gfd->kgf", value_tile[:BLOCK], grad_next, preferred_element_type=jnp.float32
        )
        + norm_next[None]
    )
    value_added = jnp.einsum(
        "kgf,gfd->kgd", key_features[:BLOCK], grad_next, preferred_element_type=jnp.float32
    )
    grad_feature_tile = grad_feature_tile + jnp.pad(
        jnp.where(member, feature_added, 0.0), ((0, WINDOW), (0, 0), (0, 0))
    )
    grad_value_tile = grad_value_tile + jnp.pad(
        jnp.where(member, value_added, 0.0), ((0, WINDOW), (0, 0), (0, 0))
    )
    return (
        (grad_state, grad_norm),
        (grad_query, grad_query_features, grad_key_tile, grad_value_tile, grad_feature_tile),
    )


def combine_tiles(tiles):
    heads_part = tiles[:, :WINDOW]
    body_part = tiles[:, WINDOW:]
    shifted = jnp.concatenate([heads_part[1:], jnp.zeros_like(heads_part[:1])], axis=0)
    filler = jnp.zeros((tiles.shape[0], BLOCK - WINDOW) + tiles.shape[2:], tiles.dtype)
    body_part = body_part + jnp.concatenate([filler, shifted], axis=1)
    return body_part.reshape((-1,) + tiles.shape[2:])


def on_device(
    activations,
    grad_out,
    segments,
    first_gain,
    query_weight,
    key_weight,
    value_weight,
    query_down,
    query_up,
    key_down,
    key_up,
    value_down,
    value_up,
    query_map,
    key_map,
    output_weight,
    output_down,
    output_up,
    second_gain,
    gate_weight,
    up_weight,
    down_weight,
):
    row_count = lax.axis_size("row")
    col_count = lax.axis_size("col")
    row_index = lax.axis_index("row")
    col_index = lax.axis_index("col")
    slot_count = row_count * col_count
    slot_index = row_index * col_count + col_index
    local_rows = activations.shape[0]
    seq_rows = segments.shape[1]
    feature_cols = activations.shape[1]
    query_part = query_weight.shape[1] // col_count
    key_part = key_weight.shape[1] // col_count
    part_cols = query_part + 2 * key_part
    hidden_cols = gate_weight.shape[1]
    rank_cols = query_down.shape[1]
    head_count = query_map.shape[0] // col_count
    group_count = key_map.shape[0] // col_count
    ratio = head_count // group_count
    feature_width = 2 * HEAD_DIM
    input_float = activations.astype(jnp.float32)
    first_scale = lax.rsqrt(col_total(jnp.sum(input_float * input_float, axis=1)) / D + norm_eps)
    first_hat = input_float * first_scale[:, None]
    first_normed = (first_hat * first_gain).astype(jnp.bfloat16)
    first_gathered = gather_rows(first_normed)
    proj_parts = jnp.concatenate(
        [
            by_parts(query_weight, col_count),
            by_parts(key_weight, col_count),
            by_parts(value_weight, col_count),
        ],
        axis=2,
    ).reshape(feature_cols, col_count * part_cols)
    down_all = jnp.concatenate([query_down, key_down, value_down], axis=1)
    up_dtype = query_up.dtype
    up_parts = jnp.concatenate(
        [
            jnp.concatenate(
                [
                    by_parts(query_up, col_count),
                    jnp.zeros((rank_cols, col_count, 2 * key_part), up_dtype),
                ],
                axis=2,
            ),
            jnp.concatenate(
                [
                    jnp.zeros((rank_cols, col_count, query_part), up_dtype),
                    by_parts(key_up, col_count),
                    jnp.zeros((rank_cols, col_count, key_part), up_dtype),
                ],
                axis=2,
            ),
            jnp.concatenate(
                [
                    jnp.zeros((rank_cols, col_count, query_part + key_part), up_dtype),
                    by_parts(value_up, col_count),
                ],
                axis=2,
            ),
        ],
        axis=0,
    ).reshape(3 * rank_cols, col_count * part_cols)
    up_block = take_slot(up_parts, 1, col_count, col_index)
    proj_sum, adapter_sum = sum_cols_attention(
        matmul(first_gathered, proj_parts), matmul(first_gathered, down_all)
    )
    adapter_low = adapter_sum.astype(jnp.bfloat16)
    projected = (proj_sum + matmul(adapter_low, up_block)).astype(jnp.bfloat16)
    queries = projected[:, :query_part]
    key_rows = projected[:, query_part : query_part + key_part]
    value_rows = projected[:, query_part + key_part :]
    query_map_part = take_slot(query_map, 0, col_count, col_index)
    key_map_part = take_slot(key_map, 0, col_count, col_index)
    query_float = queries.astype(jnp.float32).reshape(seq_rows, head_count, HEAD_DIM)
    key_float = key_rows.astype(jnp.float32).reshape(seq_rows, group_count, HEAD_DIM)
    query_feature_float, query_pullback = jax.vjp(
        feature_map, query_float, query_map_part.astype(jnp.float32)
    )
    key_feature_float, key_pullback = jax.vjp(
        feature_map, key_float, key_map_part.astype(jnp.float32)
    )
    query_features = query_feature_float.astype(jnp.bfloat16).reshape(
        seq_rows, group_count, ratio, feature_width
    )
    key_features = key_feature_float.astype(jnp.bfloat16)
    documents = segments[0]
    padded_documents = jnp.concatenate([jnp.full((WINDOW,), -1, jnp.int32), documents])
    arrays = (
        queries.reshape(seq_rows, group_count, ratio, HEAD_DIM),
        query_features,
        pad_front(key_rows.reshape(seq_rows, group_count, HEAD_DIM)),
        pad_front(value_rows.reshape(seq_rows, group_count, HEAD_DIM)),
        pad_front(key_features),
        documents,
        padded_documents,
    )
    block_count = seq_rows // BLOCK
    block_indices = jnp.arange(block_count, dtype=jnp.int32)

    def forward_step(carried, block_index):
        return forward_block(arrays, carried, block_index)

    start_state = (
        jnp.zeros((group_count, feature_width, HEAD_DIM), jnp.float32),
        jnp.zeros((group_count, feature_width), jnp.float32),
        jnp.int32(-1),
    )
    _, (mixed_blocks, kept_states, kept_norms, kept_lasts, kept_totals) = lax.scan(
        forward_step, start_state, block_indices
    )
    mixed_low = (
        jnp.transpose(mixed_blocks, (0, 3, 1, 2, 4))
        .reshape(seq_rows, query_part)
        .astype(jnp.bfloat16)
    )
    mixed_gathered = gather_heads(mixed_low)
    attended_sum, out_adapter_sum = sum_rows_attention(
        matmul(mixed_gathered, output_weight), matmul(mixed_gathered, output_down)
    )
    out_adapter_low = out_adapter_sum.astype(jnp.bfloat16)
    hidden_state = input_float + (attended_sum + matmul(out_adapter_low, output_up))
    second_scale = lax.rsqrt(col_total(jnp.sum(hidden_state * hidden_state, axis=1)) / D + norm_eps)
    second_hat = hidden_state * second_scale[:, None]
    second_normed = (second_hat * second_gain).astype(jnp.bfloat16)
    second_gathered = gather_rows(second_normed)

    def gather_cols(values):
        return lax.all_gather(values, "col", axis=0, tiled=True)

    def sum_cols_mlp(left, right, transposed, row_total):

        def term(first_row, piece_rows):
            if transposed:
                return times_transposed(left, right)
            return matmul(left, right)

        return lax.psum_scatter(
            term(jnp.int32(0), lax.axis_size("col") * row_total),
            "col",
            scatter_dimension=0,
            tiled=True,
        )

    mlp_rows = seq_rows // col_count
    gate_up_weight = jnp.concatenate([gate_weight, up_weight], axis=1)
    gate_up = sum_cols_mlp(second_gathered, gate_up_weight, False, mlp_rows)
    gate_value = gate_up[:, :hidden_cols]
    up_value = gate_up[:, hidden_cols:]
    gate_silu = jax.nn.silu(gate_value)
    hidden = (gate_silu * up_value).astype(jnp.bfloat16)
    hidden_gathered = gather_cols(hidden)
    mlp_sum = sum_rows_mlp(hidden_gathered, down_weight, False, local_rows)
    result = (hidden_state + mlp_sum).astype(jnp.bfloat16)
    grad_rows = gather_rows(grad_out)
    grad_hidden = sum_cols_mlp(grad_rows, down_weight, True, mlp_rows)
    sigmoid_gate = jax.nn.sigmoid(gate_value)
    grad_up_value = grad_hidden * gate_silu
    grad_gate_value = (
        grad_hidden * up_value * (sigmoid_gate * (1.0 + gate_value * (1.0 - sigmoid_gate)))
    )
    grad_gate_up = jnp.concatenate([grad_gate_value, grad_up_value], axis=1).astype(jnp.bfloat16)
    grad_gate_up_gathered = gather_cols(grad_gate_up)
    grad_gate_up_weight = inner_rows(second_gathered, grad_gate_up_gathered)
    mlp_first = grad_gate_up_weight[:, :hidden_cols]
    mlp_second = grad_gate_up_weight[:, hidden_cols:]
    mlp_third = inner_rows(grad_rows, hidden_gathered)
    grad_second_normed = sum_rows_mlp(grad_gate_up_gathered, gate_up_weight, True, local_rows)
    grad_second_input, grad_second_gain = norm_backward(
        grad_second_normed, second_gain, second_hat, second_scale
    )
    grad_hidden_state = grad_out.astype(jnp.float32) + grad_second_input
    grad_attended = grad_hidden_state.astype(jnp.bfloat16)
    grad_attended_gathered = gather_rows(grad_attended)
    grad_output_weight = inner_rows(mixed_gathered, grad_attended_gathered)
    grad_output_up = inner_rows(out_adapter_low, grad_attended)
    grad_mixed_sum, grad_out_adapter_sum = sum_cols_attention(
        times_transposed(grad_attended_gathered, output_weight),
        times_transposed(grad_attended_gathered, output_up),
    )
    grad_out_adapter = grad_out_adapter_sum.astype(jnp.bfloat16)
    grad_output_down = inner_rows(mixed_low, grad_out_adapter)
    output_down_part = take_slot(output_down, 0, col_count, col_index)
    grad_mixed = (grad_mixed_sum + times_transposed(grad_out_adapter, output_down_part)).astype(
        jnp.bfloat16
    )
    grad_blocks = grad_mixed.reshape(block_count, BLOCK, group_count, ratio, HEAD_DIM)

    def backward_step(carried, block_inputs):
        return backward_block(arrays, carried, block_inputs)

    start_back = (
        jnp.zeros((group_count, feature_width, HEAD_DIM), jnp.bfloat16),
        jnp.zeros((group_count, feature_width), jnp.float32),
    )
    _, (grad_query_blocks, grad_qf_blocks, grad_key_tiles, grad_value_tiles, grad_feature_tiles) = (
        lax.scan(
            backward_step,
            start_back,
            (block_indices, kept_states, kept_norms, kept_lasts, kept_totals, grad_blocks),
            reverse=True,
        )
    )
    grad_query_map_in, grad_query_map = query_pullback(
        grad_qf_blocks.reshape(seq_rows, head_count, feature_width)
    )
    grad_key_map_in, grad_key_map = key_pullback(combine_tiles(grad_feature_tiles))
    grad_query_all = grad_query_blocks.reshape(seq_rows, head_count, HEAD_DIM) + grad_query_map_in
    grad_key_all = combine_tiles(grad_key_tiles) + grad_key_map_in
    grad_value_all = combine_tiles(grad_value_tiles)
    grad_projected = jnp.concatenate(
        [
            grad_query_all.reshape(seq_rows, query_part),
            grad_key_all.reshape(seq_rows, key_part),
            grad_value_all.reshape(seq_rows, key_part),
        ],
        axis=1,
    ).astype(jnp.bfloat16)
    grad_up_local = inner_rows(adapter_low, grad_projected)
    grad_projected_gathered = gather_heads(grad_projected)
    grad_proj_parts = inner_rows(first_gathered, grad_projected_gathered).reshape(
        feature_cols, col_count, part_cols
    )
    grad_first_sum, grad_adapter_sum = sum_rows_attention(
        times_transposed(grad_projected_gathered, proj_parts),
        times_transposed(grad_projected_gathered, up_parts),
    )
    grad_adapter = grad_adapter_sum.astype(jnp.bfloat16)
    grad_down_all = inner_rows(first_normed, grad_adapter)
    grad_first_normed = grad_first_sum + times_transposed(grad_adapter, down_all)
    grad_first_input, grad_first_gain = norm_backward(
        grad_first_normed, first_gain, first_hat, first_scale
    )
    grad_activations = grad_hidden_state + grad_first_input
    reduced = (
        lax.psum_scatter(
            grad_proj_parts[:, :, :query_part]
            .reshape(feature_cols, col_count * query_part)
            .astype(jnp.bfloat16),
            "dp",
            scatter_dimension=0,
            tiled=True,
        ).astype(jnp.float32),
        lax.psum_scatter(
            grad_proj_parts[:, :, query_part : query_part + key_part]
            .reshape(feature_cols, col_count * key_part)
            .astype(jnp.bfloat16),
            "dp",
            scatter_dimension=0,
            tiled=True,
        ).astype(jnp.float32),
        lax.psum_scatter(
            grad_proj_parts[:, :, query_part + key_part :]
            .reshape(feature_cols, col_count * key_part)
            .astype(jnp.bfloat16),
            "dp",
            scatter_dimension=0,
            tiled=True,
        ).astype(jnp.float32),
        lax.psum_scatter(
            grad_output_weight.astype(jnp.bfloat16), "dp", scatter_dimension=0, tiled=True
        ).astype(jnp.float32),
        lax.psum_scatter(
            mlp_first.astype(jnp.bfloat16), "dp", scatter_dimension=0, tiled=True
        ).astype(jnp.float32),
        lax.psum_scatter(
            mlp_second.astype(jnp.bfloat16), "dp", scatter_dimension=0, tiled=True
        ).astype(jnp.float32),
        lax.psum_scatter(
            mlp_third.astype(jnp.bfloat16), "dp", scatter_dimension=0, tiled=True
        ).astype(jnp.float32),
    )
    gate_done, up_done, down_done = (reduced[4], reduced[5], reduced[6])
    small = lax.psum(
        (
            place_slot(grad_first_gain, 0, col_count, col_index),
            place_slot(grad_second_gain, 0, col_count, col_index),
            place_slot(grad_down_all, 0, col_count, col_index),
            place_slot(grad_output_up, 1, col_count, col_index),
            place_slot(grad_query_map, 0, slot_count, slot_index),
            place_slot(grad_key_map, 0, slot_count, slot_index),
            place_slot(grad_up_local[:rank_cols, :query_part], 1, slot_count, slot_index),
            place_slot(
                grad_up_local[rank_cols : 2 * rank_cols, query_part : query_part + key_part],
                1,
                slot_count,
                slot_index,
            ),
            place_slot(
                grad_up_local[2 * rank_cols :, query_part + key_part :], 1, slot_count, slot_index
            ),
            place_slot(grad_output_down, 0, slot_count, slot_index),
        ),
        ("dp", "row", "col"),
    )
    down_reduced = take_slot(small[2], 0, col_count, col_index)
    return (
        result,
        grad_activations,
        take_slot(small[0], 0, col_count, col_index),
        reduced[0],
        reduced[1],
        reduced[2],
        down_reduced[:, :rank_cols],
        take_slot(small[6], 1, row_count, row_index),
        down_reduced[:, rank_cols : 2 * rank_cols],
        take_slot(small[7], 1, row_count, row_index),
        down_reduced[:, 2 * rank_cols :],
        take_slot(small[8], 1, row_count, row_index),
        take_slot(small[4], 0, row_count, row_index),
        take_slot(small[5], 0, row_count, row_index),
        reduced[3],
        take_slot(small[9], 0, row_count, row_index),
        take_slot(small[3], 1, col_count, col_index),
        take_slot(small[1], 0, col_count, col_index),
        gate_done,
        up_done,
        jnp.transpose(down_done),
    )


def solution(mesh):
    placed = (
        P(("dp", "row"), "col"),
        P(("dp", "row"), "col"),
        P("dp", None),
        P("col"),
        P("col", "row"),
        P("col", "row"),
        P("col", "row"),
        P("col", None),
        P(None, "row"),
        P("col", None),
        P(None, "row"),
        P("col", None),
        P(None, "row"),
        P("row", None, None),
        P("row", None, None),
        P("row", "col"),
        P("row", None),
        P(None, "col"),
        P("col"),
        P("col", "row"),
        P("col", "row"),
        P("row", "col"),
    )
    return jax.shard_map(
        on_device,
        mesh=mesh,
        in_specs=placed,
        out_specs=(
            P(("dp", "row"), "col"),
            P(("dp", "row"), "col"),
            P("col"),
            P(("col", "dp"), "row"),
            P(("col", "dp"), "row"),
            P(("col", "dp"), "row"),
            P("col", None),
            P(None, "row"),
            P("col", None),
            P(None, "row"),
            P("col", None),
            P(None, "row"),
            P("row", None, None),
            P("row", None, None),
            P(("row", "dp"), "col"),
            P("row", None),
            P(None, "col"),
            P("col"),
            P(("col", "dp"), "row"),
            P(("col", "dp"), "row"),
            P("row", ("col", "dp")),
        ),
        check_vma=False,
    )
```

profile of v0, /device:TPU:0, one launch (start us, length us, event | category | flops | bytes accessed | tf_op | source)
XLA Modules:
  0.0 2776.1 jit_solution(17435205995297367527)
XLA Ops:
  29.7 45.9 %all-gather.9.cloned.1.call-done = bf16[2048,1024]{1,0:T(8,128)(2,1)} async-done(((bf16[1024,1024]{1,0:T(8,128)(2,1)}), bf16[2048,1024]{1,0:T(8,128)(2,1)}) %all-gather.9.cloned.1.call-update) | async-done | bytes 4194320 | tf_op jit(solution)/shard_map/all_gather | solution.py:38
  79.9 12.3 fusion.206
  93.2 20.7 reduce-scatter.22.cloned.1.call-done
  170.1 146.9 %while.52 = (s32[]{:T(128)}, f32[2,128,64]{1,2,0:T(8,128)S(1)}, f32[2,128]{1,0:T(2,128)S(1)}, s32[]{:T(128)}, bf16[4,2,4,512,64]{3,4,2,1,0:T(8,128)(2,1)}, /*ind...) while((s32[]{:T(128)}, f32[2,128,64]{1,2,0:T(8,128)S(1)}, ...), condition=%wide.region_15.16_spmd.clone, body=%wide.region_12.15_spmd.clone.sunk | while | flops 1320512000 | bytes 64330424 | solution.py:435
  322.6 14.9 all-gather.11.cloned.1.call-done
  352.3 101.5 %reduce-scatter.26.cloned.1.call-done = f32[1024,1024]{1,0:T(8,128)} async-done(((f32[2048,1024]{1,0:T(8,128)}), f32[1024,1024]{1,0:T(8,128)}) %reduce-scatter.26.cloned.1.call-update) | async-done | bytes 4194320 | tf_op jit(solution)/shard_map/reduce_scatter | solution.py:55
  467.3 44.8 %all-gather.17.cloned.1.call-done = bf16[2048,1024]{1,0:T(8,128)(2,1)} async-done(((bf16[1024,1024]{1,0:T(8,128)(2,1)}), bf16[2048,1024]{1,0:T(8,128)(2,1)}) %all-gather.17.cloned.1.call-update) | async-done | bytes 4194320 | tf_op jit(solution)/shard_map/all_gather | solution.py:38
  512.2 25.3 fusion.212
  552.9 18.1 all-gather.13.cloned.1.call-done
  571.1 49.3 %fusion.210 = f32[2048,8192]{1,0:T(8,128)} fusion(bf16[2048,1024]{1,0:T(8,128)(2,1)} %all-gather.13.cloned.1.call-done, bf16[1024,8192]{1,0:T(8,128)(2,1)} %constant_dynamic-update-slice_fusion.4), kind=kOutput, calls=%fused_computation.325 | convolution fusion | flops 34359738368 | bytes 88080384 | tf_op jit(solution)/shard_map/dot_general | solution.py:18
  620.7 84.3 %reduce-scatter.30.cloned.1.call-done = f32[1024,8192]{1,0:T(8,128)} async-done(((f32[2048,8192]{1,0:T(8,128)}), f32[1024,8192]{1,0:T(8,128)}) %reduce-scatter.30.cloned.1.call-update) | async-done | bytes 33554448 | tf_op jit(solution)/shard_map/reduce_scatter | solution.py:464
  704.9 24.0 multiply_convert_fusion.1
  728.9 10.4 pad_maximum_fusion
  739.4 52.5 %all-gather.19.cloned.1.call-done = bf16[2048,8192]{1,0:T(8,128)(2,1)} async-done(((bf16[1024,8192]{1,0:T(8,128)(2,1)}), bf16[2048,8192]{1,0:T(8,128)(2,1)}) %all-gather.19.cloned.1.call-update) | async-done | bytes 33554448 | tf_op jit(solution)/shard_map/all_gather | solution.py:455
  791.9 43.6 %fusion.213 = f32[2048,1024]{1,0:T(8,128)} fusion(bf16[2048,8192]{1,0:T(8,128)(2,1)} %all-gather.19.cloned.1.call-done, bf16[1024,8192]{1,0:T(8,128)(2,1)} %constant_dynamic-update-slice_fusion.4), kind=kOutput, calls=%fused_computation.328 | convolution fusion | flops 34359738368 | bytes 58720256 | tf_op jit(solution)/shard_map/dot_general | solution.py:22
  835.6 100.5 %reduce-scatter.36.cloned.1.call-done = f32[1024,1024]{1,0:T(8,128)} async-done(((f32[2048,1024]{1,0:T(8,128)}), f32[1024,1024]{1,0:T(8,128)}) %reduce-scatter.36.cloned.1.call-update) | async-done | bytes 4194320 | tf_op jit(solution)/shard_map/reduce_scatter | solution.py:67
  950.4 56.8 %all-gather.21.cloned.1.call-done = bf16[2048,1024]{1,0:T(8,128)(2,1)} async-done(((bf16[1024,1024]{1,0:T(8,128)(2,1)}), bf16[2048,1024]{1,0:T(8,128)(2,1)}) %all-gather.21.cloned.1.call-update) | async-done | bytes 4194320 | tf_op jit(solution)/shard_map/all_gather | solution.py:38
  1022.4 16.8 reduce-scatter.38.cloned.1.call-done
  1062.8 484.4 %while.53 = (s32[]{:T(128)}, bf16[2,128,64]{1,2,0:T(8,128)(2,1)S(1)}, f32[2,128]{1,0:T(2,128)S(1)}, f32[4,512,2,4,64]{1,0,4,3,2:T(4,128)}, f32[4,512,2,4,128]{1,...) while((s32[]{:T(128)}, ...), condition=%wide.region_31.32_spmd.clone, body=%wide.region_28.31_spmd.clone.sunk | while | flops 3612846848 | bytes 160752944 | solution.py:523
  1105.3 40.8 %dynamic_update_slice.153 = f32[4,512,2,4,128]{1,0,4,3,2:T(4,128)} dynamic-update-slice(f32[4,512,2,4,128]{1,0,4,3,2:T(4,128)} %get-tuple-element.1294, f32[1,512,2,4,128]{1,0,4,3,2:T(1,128)S(1)} %copy.190, s32[]{:T(128)S(6)} %sub.227, s32[]{:T(128)} %constant.201.clone.1..sunk.1, s32[]{:T(128)} %constant.201.clone.1..sunk.1, s32[]{:T(128)} %constant.201.clone.1..sunk.1, s32[]{:T(128)} %constant.201.clone.1..sunk.1) | dynamic-update-slice | bytes 4194308 | tf_op jit(solution)/shard_map/while/body/jit(dynamic_update_index_in_dim)/dynamic_update_slice | solution.py:523
  1150.8 21.2 dynamic_update_slice.152
  1226.3 40.8 %dynamic_update_slice.153 = f32[4,512,2,4,128]{1,0,4,3,2:T(4,128)} dynamic-update-slice(f32[4,512,2,4,128]{1,0,4,3,2:T(4,128)} %get-tuple-element.1294, f32[1,512,2,4,128]{1,0,4,3,2:T(1,128)S(1)} %copy.190, s32[]{:T(128)S(6)} %sub.227, s32[]{:T(128)} %constant.201.clone.1..sunk.1, s32[]{:T(128)} %constant.201.clone.1..sunk.1, s32[]{:T(128)} %constant.201.clone.1..sunk.1, s32[]{:T(128)} %constant.201.clone.1..sunk.1) | dynamic-update-slice | bytes 4194308 | tf_op jit(solution)/shard_map/while/body/jit(dynamic_update_index_in_dim)/dynamic_update_slice | solution.py:523
  1271.8 21.2 dynamic_update_slice.152
  1347.3 40.8 %dynamic_update_slice.153 = f32[4,512,2,4,128]{1,0,4,3,2:T(4,128)} dynamic-update-slice(f32[4,512,2,4,128]{1,0,4,3,2:T(4,128)} %get-tuple-element.1294, f32[1,512,2,4,128]{1,0,4,3,2:T(1,128)S(1)} %copy.190, s32[]{:T(128)S(6)} %sub.227, s32[]{:T(128)} %constant.201.clone.1..sunk.1, s32[]{:T(128)} %constant.201.clone.1..sunk.1, s32[]{:T(128)} %constant.201.clone.1..sunk.1, s32[]{:T(128)} %constant.201.clone.1..sunk.1) | dynamic-update-slice | bytes 4194308 | tf_op jit(solution)/shard_map/while/body/jit(dynamic_update_index_in_dim)/dynamic_update_slice | solution.py:523
  1392.8 21.2 dynamic_update_slice.152
  1468.4 40.8 %dynamic_update_slice.153 = f32[4,512,2,4,128]{1,0,4,3,2:T(4,128)} dynamic-update-slice(f32[4,512,2,4,128]{1,0,4,3,2:T(4,128)} %get-tuple-element.1294, f32[1,512,2,4,128]{1,0,4,3,2:T(1,128)S(1)} %copy.190, s32[]{:T(128)S(6)} %sub.227, s32[]{:T(128)} %constant.201.clone.1..sunk.1, s32[]{:T(128)} %constant.201.clone.1..sunk.1, s32[]{:T(128)} %constant.201.clone.1..sunk.1, s32[]{:T(128)} %constant.201.clone.1..sunk.1) | dynamic-update-slice | bytes 4194308 | tf_op jit(solution)/shard_map/while/body/jit(dynamic_update_index_in_dim)/dynamic_update_slice | solution.py:523
  1513.8 21.2 dynamic_update_slice.152
  1547.2 10.9 reshape.259
  1601.1 17.5 all-gather.23.cloned.1.call-done
  1623.1 28.2 %all-gather.15.cloned.1.call-done = bf16[2048,4096]{1,0:T(8,128)(2,1)} async-done(((bf16[1024,4096]{1,0:T(8,128)(2,1)}), bf16[2048,4096]{1,0:T(8,128)(2,1)}) %all-gather.15.cloned.1.call-update) | async-done | bytes 16777232 | tf_op jit(solution)/shard_map/all_gather | solution.py:455
  1651.3 24.0 convert_bitcast_fusion
  1675.4 11.3 copy.140
  1686.8 42.7 %convolution_convert_fusion = bf16[1024,8192]{1,0:T(8,128)(2,1)} fusion(bf16[2048,1024]{1,0:T(8,128)(2,1)} %all-gather.13.cloned.1.call-done, bf16[2048,8192]{1,0:T(8,128)(2,1)} %all-gather.19.cloned.1.call-done), kind=kOutput, calls=%fused_computation.180 | convolution fusion | flops 34368126976 | bytes 54525952 | tf_op jit(solution)/shard_map/dot_general | solution.py:28
  1729.5 12.0 fusion.198
  1765.7 11.5 convolution_convert_fusion.1
  1790.6 12.4 fusion.216
  1803.1 24.0 fusion.211
  1840.4 148.7 %reduce-scatter.54.cloned.1.call-done = bf16[128,4096]{1,0:T(8,128)(2,1)} async-done(((bf16[1024,4096]{1,0:T(8,128)(2,1)}), bf16[128,4096]{1,0:T(8,128)(2,1)}) %reduce-scatter.54.cloned.1.call-update) | async-done | bytes 1048592 | tf_op jit(solution)/shard_map/reduce_scatter | solution.py:589
  1991.8 148.9 %reduce-scatter.56.cloned.1.call-done = bf16[128,4096]{1,0:T(8,128)(2,1)} async-done(((bf16[1024,4096]{1,0:T(8,128)(2,1)}), bf16[128,4096]{1,0:T(8,128)(2,1)}) %reduce-scatter.56.cloned.1.call-update) | async-done | bytes 1048592 | tf_op jit(solution)/shard_map/reduce_scatter | solution.py:592
  2143.5 68.0 %reduce-scatter.52.cloned.1.call-done = bf16[128,1024]{1,0:T(8,128)(2,1)} async-done(((bf16[1024,1024]{1,0:T(8,128)(2,1)}), bf16[128,1024]{1,0:T(8,128)(2,1)}) %reduce-scatter.52.cloned.1.call-update) | async-done | bytes 262160 | tf_op jit(solution)/shard_map/reduce_scatter | solution.py:586
  2214.7 139.1 %all-reduce.18.cloned.1.call-done = (f32[2048,24]{0,1:T(8,128)}, f32[8,2048]{1,0:T(8,128)}, f32[32,64,64]{2,1,0:T(8,128)}, f32[8,64,64]{2,1,0:T(8,128)}, f32[2048,8]{0,1:T(8,128)}, /*index=5*/f32[8,2048]{1,0:T(8,128)}) async-done(((f32[2048,24]{0,1:T(8,128)}, f32[8,2048]{1,0:T(8,128)}, f32[32,64,64]{2,1,0:T(8,128)}, f32[8,64,64]{2,1,0:T(8,128)}, f32[2048,8]{0,1:T(8,128)}, /*index=5*/f32[8,2048]{1,0:T(8,128)}), ...) | async-done | bytes 1048592 | tf_op jit(solution)/shard_map/psum | solution.py:600
  2362.8 55.7 %reduce-scatter.48.cloned.1.call-done = bf16[128,256]{1,0:T(8,128)(2,1)} async-done(((bf16[1024,256]{1,0:T(8,128)(2,1)}), bf16[128,256]{1,0:T(8,128)(2,1)}) %reduce-scatter.48.cloned.1.call-update) | async-done | bytes 65552 | tf_op jit(solution)/shard_map/reduce_scatter | solution.py:570
  2420.0 63.7 %reduce-scatter.50.cloned.1.call-done = bf16[128,256]{1,0:T(8,128)(2,1)} async-done(((bf16[1024,256]{1,0:T(8,128)(2,1)}), bf16[128,256]{1,0:T(8,128)(2,1)}) %reduce-scatter.50.cloned.1.call-update) | async-done | bytes 65552 | tf_op jit(solution)/shard_map/reduce_scatter | solution.py:578
  2485.2 69.1 %reduce-scatter.46.cloned.1.call-done = bf16[128,1024]{1,0:T(8,128)(2,1)} async-done(((bf16[1024,1024]{1,0:T(8,128)(2,1)}), bf16[128,1024]{1,0:T(8,128)(2,1)}) %reduce-scatter.46.cloned.1.call-update) | async-done | bytes 262160 | tf_op jit(solution)/shard_map/reduce_scatter | solution.py:562
  2556.1 98.6 %reduce-scatter.42.cloned.1.call-done = f32[1024,1024]{1,0:T(8,128)} async-done(((f32[2048,1024]{1,0:T(8,128)}), f32[1024,1024]{1,0:T(8,128)}) %reduce-scatter.42.cloned.1.call-update) | async-done | bytes 4194320 | tf_op jit(solution)/shard_map/reduce_scatter | solution.py:55
  2660.5 40.5 %all-reduce.14 = (f32[2048]{0:T(1024)S(1)}, f32[8,512]{1,0:T(8,128)S(1)}, f32[8,512]{1,0:T(8,128)S(1)}, f32[2048]{0:T(1024)S(1)}) all-reduce(f32[2048]{0:T(1024)S(1)} %dynamic_update_slice.99, f32[8,512]{1,0:T(8,128)S(1)} %constant_dynamic-update-slice_fusion.7, ...), channel_id=1, replica_groups=mesh['dp'=8,'row'=2,'col'=2] {'dp','row','col'}, use_global_device_ids=true, to_apply=%region_41.42 | all-reduce | flops 12288 | bytes 98304 | tf_op jit(solution)/shard_map/psum | solution.py:600
  2705.8 52.0 %reduce-scatter.32.cloned.1.call-done = f32[1024,1024]{1,0:T(8,128)} async-done(((f32[2048,1024]{1,0:T(8,128)}), f32[1024,1024]{1,0:T(8,128)}) %reduce-scatter.32.cloned.1.call-update) | async-done | bytes 4194320 | tf_op jit(solution)/shard_map/reduce_scatter | solution.py:67
  2757.8 11.2 fusion.143
  (647 shorter events, 682.8 us)
Async XLA Ops:
  7.2 334.0 %copy-start = (bf16[1024,1024]{1,0:T(8,128)(2,1)S(1)}, bf16[1024,1024]{1,0:T(8,128)(2,1)}, u32[]{:S(2)}) copy-start(bf16[1024,1024]{1,0:T(8,128)(2,1)} %param.41) | copy-start | bytes 6291460
  7.2 68.4 %all-gather.9.cloned.1.call-start = ((), (), s32[]{:S(2)}) async-start(), calls=%async_computation.19 | async-start | bytes 6291456 | tf_op jit(solution)/shard_map/all_gather | solution.py:38
  16.1 77.1 %reduce-scatter.24.cloned.1.call-start = ((), (), s32[]{:S(2)}) async-start(), calls=%async_computation.21 | async-start | bytes 589824 | tf_op jit(solution)/shard_map/reduce_scatter | solution.py:49
  29.7 62.5 %copy-start.42 = (bf16[1024,24]{0,1:T(8,128)(2,1)}, bf16[1024,24]{0,1:T(8,128)(2,1)S(1)}, u32[]{:S(2)}) copy-start(bf16[1024,24]{0,1:T(8,128)(2,1)S(1)} %constant_dynamic-update-slice_fusion.1) | copy-start | bytes 147460
  79.8 34.1 %reduce-scatter.22.cloned.1.call-start = ((), (), s32[]{:S(2)}) async-start(), calls=%async_computation.20 | async-start | bytes 18874368 | tf_op jit(solution)/shard_map/reduce_scatter | solution.py:48
  92.2 245.3 %all-gather.11.cloned.1.call-start = ((), (), s32[]{:S(2)}) async-start(), calls=%async_computation.22 | async-start | bytes 6291456 | tf_op jit(solution)/shard_map/all_gather | solution.py:42
  93.1 24.7 copy-start.39
  322.6 29.7 %reduce-scatter.28.cloned.1.call-start = ((), (), s32[]{:S(2)}) async-start(), calls=%async_computation.24 | async-start | bytes 98304 | tf_op jit(solution)/shard_map/reduce_scatter | solution.py:56
  341.1 112.7 %reduce-scatter.26.cloned.1.call-start = ((), (), s32[]{:S(2)}) async-start(), calls=%async_computation.23 | async-start | bytes 12582912 | tf_op jit(solution)/shard_map/reduce_scatter | solution.py:55
  350.3 103.5 %copy-start.64 = (bf16[8,1024]{1,0:T(8,128)(2,1)S(1)}, bf16[8,1024]{1,0:T(8,128)(2,1)}, u32[]{:S(2)}) copy-start(bf16[8,1024]{1,0:T(8,128)(2,1)} %param.43) | copy-start | bytes 49156
  350.3 161.9 %all-gather.17.cloned.1.call-start = ((), (), s32[]{:S(2)}) async-start(), calls=%async_computation.29 | async-start | bytes 6291456 | tf_op jit(solution)/shard_map/all_gather | solution.py:38
  351.1 111.7 %copy-start.70 = (f32[1024]{0:T(1024)S(1)}, f32[1024]{0:T(1024)}, u32[]{:S(2)}) copy-start(f32[1024]{0:T(1024)} %param.44) | copy-start | bytes 12292
  351.1 220.0 %all-gather.13.cloned.1.call-start = ((), (), s32[]{:S(2)}) async-start(), calls=%async_computation.25 | async-start | bytes 6291456 | tf_op jit(solution)/shard_map/all_gather | solution.py:38
  467.3 153.4 %reduce-scatter.34.cloned.1.call-start = ((), (), s32[]{:S(2)}) async-start(), calls=%async_computation.30 | async-start | bytes 50331648 | tf_op jit(solution)/shard_map/reduce_scatter | solution.py:464
  537.4 167.5 %reduce-scatter.30.cloned.1.call-start = ((), (), s32[]{:S(2)}) async-start(), calls=%async_computation.26 | async-start | bytes 100663296 | tf_op jit(solution)/shard_map/reduce_scatter | solution.py:464
  620.4 171.5 %all-gather.19.cloned.1.call-start = ((), (), s32[]{:S(2)}) async-start(), calls=%async_computation.31 | async-start | bytes 50331648 | tf_op jit(solution)/shard_map/all_gather | solution.py:455
  739.3 196.8 %reduce-scatter.36.cloned.1.call-start = ((), (), s32[]{:S(2)}) async-start(), calls=%async_computation.32 | async-start | bytes 12582912 | tf_op jit(solution)/shard_map/reduce_scatter | solution.py:67
  835.5 100.6 %copy-start.61 = (f32[1024]{0:T(1024)S(1)}, f32[1024]{0:T(1024)}, u32[]{:S(2)}) copy-start(f32[1024]{0:T(1024)} %copy-done.60) | copy-start | bytes 12292
  835.5 100.6 %copy-start.71 = (f32[1024]{0:T(1024)S(1)}, f32[1024]{0:T(1024)}, u32[]{:S(2)}) copy-start(f32[1024]{0:T(1024)} %param.44) | copy-start | bytes 12292
  835.6 171.7 %all-gather.21.cloned.1.call-start = ((), (), s32[]{:S(2)}) async-start(), calls=%async_computation.33 | async-start | bytes 6291456 | tf_op jit(solution)/shard_map/all_gather | solution.py:38
  944.7 62.5 %copy-start.65 = (bf16[8,1024]{1,0:T(8,128)(2,1)S(1)}, bf16[8,1024]{1,0:T(8,128)(2,1)}, u32[]{:S(2)}) copy-start(bf16[8,1024]{1,0:T(8,128)(2,1)} %param.43) | copy-start | bytes 49156
  950.3 72.1 %reduce-scatter.40.cloned.1.call-start = ((), (), s32[]{:S(2)}) async-start(), calls=%async_computation.35 | async-start | bytes 196608 | tf_op jit(solution)/shard_map/reduce_scatter | solution.py:49
  1011.3 27.9 %reduce-scatter.38.cloned.1.call-start = ((), (), s32[]{:S(2)}) async-start(), calls=%async_computation.34 | async-start | bytes 12582912 | tf_op jit(solution)/shard_map/reduce_scatter | solution.py:48
  1020.4 598.2 %all-gather.23.cloned.1.call-start = ((), (), s32[]{:S(2)}) async-start(), calls=%async_computation.36 | async-start | bytes 9437184 | tf_op jit(solution)/shard_map/all_gather | solution.py:42
  1150.7 27.1 copy-start.3
  1271.8 27.1 copy-start.3
  1392.7 27.1 copy-start.3
  1513.8 27.1 copy-start.3
  1600.5 50.8 %all-gather.15.cloned.1.call-start = ((), (), s32[]{:S(2)}) async-start(), calls=%async_computation.27 | async-start | bytes 25165824 | tf_op jit(solution)/shard_map/all_gather | solution.py:455
  1601.1 161.5 %reduce-scatter.44.cloned.1.call-start = ((), (), s32[]{:S(2)}) async-start(), calls=%async_computation.38 | async-start | bytes 294912 | tf_op jit(solution)/shard_map/reduce_scatter | solution.py:56
  1623.1 214.0 %reduce-scatter.58.cloned.1.call-start = ((), (), s32[]{:S(2)}) async-start(), calls=%async_computation.45 | async-start | bytes 9437184
  1686.7 302.3 %reduce-scatter.54.cloned.1.call-start = ((), (), s32[]{:S(2)}) async-start(), calls=%async_computation.43 | async-start | bytes 9437184 | tf_op jit(solution)/shard_map/reduce_scatter | solution.py:589
  1741.5 399.2 %reduce-scatter.56.cloned.1.call-start = ((), (), s32[]{:S(2)}) async-start(), calls=%async_computation.44 | async-start | bytes 9437184 | tf_op jit(solution)/shard_map/reduce_scatter | solution.py:592
  1742.3 469.2 %reduce-scatter.52.cloned.1.call-start = ((), (), s32[]{:S(2)}) async-start(), calls=%async_computation.42 | async-start | bytes 2359296 | tf_op jit(solution)/shard_map/reduce_scatter | solution.py:586
  1751.8 602.0 %all-reduce.18.cloned.1.call-start = ((), (), s32[]{:S(2)}) async-start(), calls=%async_computation.46 | async-start | bytes 3407872 | tf_op jit(solution)/shard_map/psum | solution.py:600
  1765.6 652.8 %reduce-scatter.48.cloned.1.call-start = ((), (), s32[]{:S(2)}) async-start(), calls=%async_computation.40 | async-start | bytes 589824 | tf_op jit(solution)/shard_map/reduce_scatter | solution.py:570
  1787.4 696.3 %reduce-scatter.50.cloned.1.call-start = ((), (), s32[]{:S(2)}) async-start(), calls=%async_computation.41 | async-start | bytes 589824 | tf_op jit(solution)/shard_map/reduce_scatter | solution.py:578
  1788.4 765.9 %reduce-scatter.46.cloned.1.call-start = ((), (), s32[]{:S(2)}) async-start(), calls=%async_computation.39 | async-start | bytes 2359296 | tf_op jit(solution)/shard_map/reduce_scatter | solution.py:562
  1790.4 864.4 %reduce-scatter.42.cloned.1.call-start = ((), (), s32[]{:S(2)}) async-start(), calls=%async_computation.37 | async-start | bytes 12582912 | tf_op jit(solution)/shard_map/reduce_scatter | solution.py:55
  1803.0 954.8 %reduce-scatter.32.cloned.1.call-start = ((), (), s32[]{:S(2)}) async-start(), calls=%async_computation.28 | async-start | bytes 12582912 | tf_op jit(solution)/shard_map/reduce_scatter | solution.py:67
  1991.8 662.9 %copy-start.7 = (bf16[1024,1024]{1,0:T(8,128)(2,1)S(1)}, bf16[1024,1024]{1,0:T(8,128)(2,1)}, u32[]{:S(2)}) copy-start(bf16[1024,1024]{1,0:T(8,128)(2,1)} %param.26) | copy-start | bytes 6291460
  1991.8 662.9 %copy-start.41 = (f32[1024,24]{0,1:T(8,128)S(1)}, f32[1024,24]{0,1:T(8,128)}, u32[]{:S(2)}) copy-start(f32[1024,24]{0,1:T(8,128)} %reduce-scatter.44.cloned.1.call-done) | copy-start | bytes 294916
  1991.8 662.9 %copy-start.43 = (bf16[1024,24]{0,1:T(8,128)(2,1)S(1)}, bf16[1024,24]{0,1:T(8,128)(2,1)}, u32[]{:S(2)}) copy-start(bf16[1024,24]{0,1:T(8,128)(2,1)} %copy-done.42) | copy-start | bytes 147460
  1991.8 662.9 %copy-start.74 = (f32[1024]{0:T(1024)S(1)}, f32[1024]{0:T(1024)}, u32[]{:S(2)}) copy-start(f32[1024]{0:T(1024)} %copy-done.73) | copy-start | bytes 12292
  1991.8 662.9 %copy-start.79 = (f32[1024]{0:T(1024)S(1)}, f32[1024]{0:T(1024)}, u32[]{:S(2)}) copy-start(f32[1024]{0:T(1024)} %param.29) | copy-start | bytes 12292
  2556.1 201.7 %copy-start.62 = (f32[1024]{0:T(1024)S(1)}, f32[1024]{0:T(1024)}, u32[]{:S(2)}) copy-start(f32[1024]{0:T(1024)} %copy-done.60) | copy-start | bytes 12292
  2556.1 201.7 %copy-start.72 = (f32[1024]{0:T(1024)S(1)}, f32[1024]{0:T(1024)}, u32[]{:S(2)}) copy-start(f32[1024]{0:T(1024)} %param.44) | copy-start | bytes 12292
  2556.1 201.7 %copy-start.78 = (f32[1024]{0:T(1024)S(1)}, f32[1024]{0:T(1024)}, u32[]{:S(2)}) copy-start(f32[1024]{0:T(1024)} %copy-done.77) | copy-start | bytes 12292
  (90 other events, 560.2 us)
Sparse Core Ops, SparseCore 0:
  16.3 59.3 all-gather.8
  79.9 7.7 reduce-scatter.23
  92.4 21.4 reduce-scatter.21
  322.7 14.8 all-gather.10
  341.2 11.0 reduce-scatter.27
  354.5 99.2 reduce-scatter.25
  455.4 56.7 all-gather.16
  514.3 56.7 all-gather.12
  573.4 45.1 reduce-scatter.33
  620.7 84.1 reduce-scatter.29
  739.4 52.4 all-gather.18
  835.7 100.4 reduce-scatter.35
  950.5 56.7 all-gather.20
  1011.4 7.5 reduce-scatter.39
  1021.2 17.9 reduce-scatter.37
  1600.6 17.9 all-gather.22
  1620.0 31.2 all-gather.14
  1654.0 12.0 reduce-scatter.43
  1686.9 150.2 reduce-scatter.57
  1841.0 147.9 reduce-scatter.53
  1992.7 147.9 reduce-scatter.55
  2144.7 66.7 reduce-scatter.51
  2220.0 133.7 all-reduce.17
  2357.5 60.8 reduce-scatter.47
  2422.7 60.9 reduce-scatter.49
  2487.7 66.6 reduce-scatter.45
  2556.5 98.1 reduce-scatter.41
  2657.1 100.6 reduce-scatter.31
where the time goes:
time: 2790 us; the launch traced here: 2780 us
  waiting for transfers between devices  1460 us (52%)
  matrix products  592 us (21%)
  local copies, waits for them, and re-layouts  456 us (16%)
  other arithmetic  182 us (7%)
  blocking collectives  50.8 us (2%)
    dynamic_update_slice x16, local copies, waits for them, and re-layouts, on_device(): lax.scan(backward_step, start_back, (block_indices, kept_states, kept_nor...  261 us
    reduce_scatter x2, waiting for transfers between devices, sum_rows_attention(): lax.psum_scatter(larger, 'row', scatter_dimension=0, tiled=True)  200 us
    all_gather x4, waiting for transfers between devices, gather_rows(): return lax.all_gather(values, 'row', axis=0, tiled=True)  166 us
    reduce_scatter x2, waiting for transfers between devices, sum_rows_mlp(): lax.psum_scatter(term(jnp.int32(0), lax.axis_size('row') * row_total), 'r...  153 us
    reduce_scatter x1, waiting for transfers between devices, on_device(): lax.psum_scatter(mlp_second.astype(jnp.bfloat16), 'dp', scatter_dimension...  149 us
    reduce_scatter x1, waiting for transfers between devices, on_device(): lax.psum_scatter(mlp_first.astype(jnp.bfloat16), 'dp', scatter_dimension=...  149 us
    psum x1, waiting for transfers between devices, on_device(): lax.psum((place_slot(grad_first_gain, 0, col_count, col_index), place_slo...  139 us
    dot_general x8, matrix products, matmul(): return jnp.dot(left, right, preferred_element_type=jnp.float32)  111 us
  transfers between devices with their start and end apart: 28, of which 24 were waited for; matrix products, arithmetic and copies ran while one was open for 13% of the time, Pallas kernels for 0%

commit v1 on v0

v1 whole, which is shorter than its diff:
```python
import functools
import jax
import jax.numpy as jnp
from jax import lax
from jax.experimental import pallas as pl
from jax.experimental.pallas import tpu as pltpu
from jax.sharding import PartitionSpec as P

HEAD_DIM = 64
WINDOW = 64
BLOCK = 512
SUB = 128
SCALE = 0.125
NSUB = BLOCK // SUB
LANES = 128
MLP_TILE = 512
SUM_TILE = 256
GRAD_TILE = 512
VMEM_LIMIT = 56 * 1024 * 1024
FINISH_ORDER = ("down_own", "down_got", "output", "proj")
norm_eps = 1e-05
F32 = jnp.float32
BF16 = jnp.bfloat16


def dot_nn(left, right):
    return lax.dot_general(left, right, (((1,), (0,)), ((), ())), preferred_element_type=F32)


def dot_nt(left, right):
    return lax.dot_general(left, right, (((1,), (1,)), ((), ())), preferred_element_type=F32)


def softmax_halves(before):
    def soft(values):
        powers = jnp.exp(values - jnp.max(values, axis=0, keepdims=True))
        return powers * (1.0 / jnp.sum(powers, axis=0, keepdims=True))

    return jnp.concatenate([soft(before[:HEAD_DIM]), soft(before[HEAD_DIM:])], axis=0)


def halves_backward(probs, grads):
    def half(p, g):
        return p * (g - jnp.sum(p * g, axis=0, keepdims=True))

    return half(probs[:HEAD_DIM], grads[:HEAD_DIM]) - half(probs[HEAD_DIM:], grads[HEAD_DIM:])


def side_by_side(parts, sub):
    return jnp.concatenate([part[:, sub * SUB : (sub + 1) * SUB] for part in parts], axis=1)


def key_side(kt_ref, vt_ref, kmap_ref, kft_ref, kfr_ref, kr_ref, vr_ref):
    features = softmax_halves(dot_nn(kmap_ref[0], kt_ref[...])).astype(BF16)
    kft_ref[...] = features
    kfr_ref[...] = jnp.transpose(features)
    kr_ref[...] = jnp.transpose(kt_ref[...])
    if vr_ref is not None:
        vr_ref[...] = jnp.transpose(vt_ref[...])


def tile_rows(start_ref, base, sub, ratio):
    low_one = start_ref[0, :, sub * SUB : (sub + 1) * SUB] + (WINDOW - base)
    low = jnp.concatenate([low_one] * ratio, axis=1)
    width = ratio * SUB
    place = sub * SUB + (lax.broadcasted_iota(jnp.int32, (1, width), 1) & (SUB - 1))
    same = jnp.where(low <= -1, 1.0, 0.0)
    return low, place, same


def tile_weights(kfr_ref, kr_ref, base, sub, low, place, q_sub, qf_sub):
    width = q_sub.shape[1]
    first = sub * SUB
    lin_keys = first + SUB
    win_keys = SUB + WINDOW
    link = dot_nn(kfr_ref[pl.ds(base, lin_keys), :], qf_sub)
    score = dot_nn(kr_ref[pl.ds(base + first, win_keys), :], q_sub) * SCALE
    lin_at = lax.broadcasted_iota(jnp.int32, (lin_keys, width), 0)
    win_at = lax.broadcasted_iota(jnp.int32, (win_keys, width), 0) + first
    lin_mask = (lin_at >= low) & (lin_at <= place)
    win_mask = (win_at >= jnp.maximum(low, place + 1)) & (win_at <= place + WINDOW)
    lin = jnp.where(lin_mask, link, 0.0)
    win = jnp.where(win_mask, jnp.exp(score), 0.0)
    return lin, win, lin_mask, win_mask


def member_lanes(base, mark):
    at = lax.broadcasted_iota(jnp.int32, (1, BLOCK), 1) + (base - WINDOW)
    return at >= mark


def forward_kernel(
    mark_ref, start_ref, qt_ref, kt_ref, vt_ref, qmap_ref, kmap_ref, mix_ref, inv_ref,
    kft_ref, kfr_ref, kr_ref, state_ref, norm_ref,
):
    b = pl.program_id(1)
    ratio = qmap_ref.shape[0]
    base = pl.multiple_of(b * BLOCK, BLOCK)

    @pl.when(b == 0)
    def _():
        key_side(kt_ref, vt_ref, kmap_ref, kft_ref, kfr_ref, kr_ref, None)
        state_ref[...] = jnp.zeros_like(state_ref)
        norm_ref[...] = jnp.zeros_like(norm_ref)

    queries = [qt_ref[h * HEAD_DIM : (h + 1) * HEAD_DIM, :] for h in range(ratio)]
    features = [softmax_halves(dot_nn(qmap_ref[h], queries[h])).astype(BF16) for h in range(ratio)]
    state_low = state_ref[...].astype(BF16)
    norm = norm_ref[...]
    for sub in range(NSUB):
        first = sub * SUB
        q_sub = side_by_side(queries, sub)
        qf_sub = side_by_side(features, sub)
        low, place, same = tile_rows(start_ref, base, sub, ratio)
        lin, win, _, _ = tile_weights(kfr_ref, kr_ref, base, sub, low, place, q_sub, qf_sub)
        carried = dot_nn(state_low, qf_sub)
        normal = jnp.sum(qf_sub.astype(F32) * norm, axis=0, keepdims=True)
        total = (
            jnp.sum(lin, axis=0, keepdims=True) + jnp.sum(win, axis=0, keepdims=True) + same * normal
        )
        inverse = 1.0 / total
        mixed = dot_nn(vt_ref[:, pl.ds(base, first + SUB)], lin.astype(BF16))
        mixed += dot_nn(vt_ref[:, pl.ds(base + first, SUB + WINDOW)], win.astype(BF16))
        mixed = ((mixed + same * carried) * inverse).astype(BF16)
        for h in range(ratio):
            lanes = slice(h * SUB, (h + 1) * SUB)
            mix_ref[h * HEAD_DIM : (h + 1) * HEAD_DIM, first : first + SUB] = mixed[:, lanes]
            inv_ref[0, h : h + 1, first : first + SUB] = inverse[:, lanes]

    mark = mark_ref[b + 1]
    keep = jnp.where((mark <= b * BLOCK - WINDOW - 1), 1.0, 0.0)
    tile = kft_ref[:, pl.ds(base, BLOCK)]
    member = jnp.where(member_lanes(base, mark), tile, jnp.zeros_like(tile))
    state_ref[...] = keep * state_ref[...] + dot_nt(vt_ref[:, pl.ds(base, BLOCK)], member)
    norm_ref[...] = keep * norm + jnp.sum(member.astype(F32), axis=1, keepdims=True)


def backward_kernel(
    mark_ref, start_ref, qt_ref, kt_ref, vt_ref, qmap_ref, kmap_ref, dmt_ref, mix_ref, inv_ref,
    qback_ref, kback_ref,
    dqt_ref, dkt_ref, dvt_ref, gqm_ref, gkm_ref,
    kft_ref, kfr_ref, kr_ref, vr_ref, states_ref, statet_ref, norms_ref,
    dk_acc, dkf_acc, dv_acc, dst_ref, dstt_ref, dnorm_ref,
):
    step = pl.program_id(1)
    blocks = pl.num_programs(1)
    count = states_ref.shape[0]
    b = blocks - 1 - step
    ratio = qmap_ref.shape[0]
    base = pl.multiple_of(b * BLOCK, BLOCK)

    @pl.when(step == 0)
    def _():
        key_side(kt_ref, vt_ref, kmap_ref, kft_ref, kfr_ref, kr_ref, vr_ref)
        state = jnp.zeros(statet_ref.shape[1:], F32)
        norm = jnp.zeros(norms_ref.shape[1:], F32)
        statet = jnp.zeros(states_ref.shape[1:], F32)
        for i in range(count):
            statet_ref[i] = state.astype(BF16)
            states_ref[i] = statet.astype(BF16)
            norms_ref[i] = norm
            if i + 1 < count:
                mark = mark_ref[i + 1]
                keep = jnp.where((mark <= i * BLOCK - WINDOW - 1), 1.0, 0.0)
                tile = kft_ref[:, i * BLOCK : (i + 1) * BLOCK]
                member = jnp.where(member_lanes(i * BLOCK, mark), tile, jnp.zeros_like(tile))
                values = vt_ref[:, i * BLOCK : (i + 1) * BLOCK]
                state = keep * state + dot_nt(values, member)
                statet = keep * statet + dot_nt(member, values)
                norm = keep * norm + jnp.sum(member.astype(F32), axis=1, keepdims=True)
        dk_acc[...] = jnp.zeros_like(dk_acc)
        dkf_acc[...] = jnp.zeros_like(dkf_acc)
        dv_acc[...] = jnp.zeros_like(dv_acc)
        dst_ref[...] = jnp.zeros_like(dst_ref)
        dstt_ref[...] = jnp.zeros_like(dstt_ref)
        dnorm_ref[...] = jnp.zeros_like(dnorm_ref)
        gqm_ref[...] = jnp.zeros_like(gqm_ref)

    mark = mark_ref[b + 1]
    keep = jnp.where((mark <= b * BLOCK - WINDOW - 1), 1.0, 0.0)
    tile_lanes = pl.ds(base, BLOCK)
    member = member_lanes(base, mark)
    dst_low = dst_ref[...].astype(BF16)
    dstt_low = dstt_ref[...].astype(BF16)
    dkf_acc[:, tile_lanes] += jnp.where(
        member, dot_nn(dst_low, vt_ref[:, tile_lanes]) + dnorm_ref[...], 0.0
    )
    dv_acc[:, tile_lanes] += jnp.where(member, dot_nn(dstt_low, kft_ref[:, tile_lanes]), 0.0)

    queries = [qt_ref[h * HEAD_DIM : (h + 1) * HEAD_DIM, :] for h in range(ratio)]
    gradients = [dmt_ref[h * HEAD_DIM : (h + 1) * HEAD_DIM, :] for h in range(ratio)]
    mixes = [mix_ref[h * HEAD_DIM : (h + 1) * HEAD_DIM, :] for h in range(ratio)]
    inverses = [inv_ref[0, h : h + 1, :] for h in range(ratio)]
    probabilities = [softmax_halves(dot_nn(qmap_ref[h], queries[h])) for h in range(ratio)]
    features = [p.astype(BF16) for p in probabilities]
    norm = norms_ref[b]
    state_low = states_ref[b]
    dnorm = jnp.zeros((2 * HEAD_DIM, SUB), F32)
    dst = keep * dst_ref[...]
    dstt = keep * dstt_ref[...]
    dq_parts, dpre_parts = [], []
    for sub in range(NSUB):
        first = sub * SUB
        lin_lanes = pl.ds(base, first + SUB)
        win_lanes = pl.ds(base + first, SUB + WINDOW)
        q_sub = side_by_side(queries, sub)
        qf_sub = side_by_side(features, sub)
        dm_sub = side_by_side(gradients, sub)
        inverse = side_by_side(inverses, sub)
        dm_float = dm_sub.astype(F32)
        low, place, same = tile_rows(start_ref, base, sub, ratio)
        lin, win, lin_mask, win_mask = tile_weights(
            kfr_ref, kr_ref, base, sub, low, place, q_sub, qf_sub
        )
        delta = jnp.sum(dm_float * side_by_side(mixes, sub).astype(F32), axis=0, keepdims=True)
        dv_acc[:, lin_lanes] += dot_nt(dm_sub, (lin * inverse).astype(BF16))
        dv_acc[:, win_lanes] += dot_nt(dm_sub, (win * inverse).astype(BF16))
        dlin = (dot_nn(vr_ref[lin_lanes, :], dm_sub) - delta) * inverse
        dwin = (dot_nn(vr_ref[win_lanes, :], dm_sub) - delta) * inverse
        dlink = jnp.where(lin_mask, dlin, 0.0).astype(BF16)
        dscore = (win * dwin).astype(BF16)
        dcarried = (dm_float * (same * inverse)).astype(BF16)
        dtotal = -delta * (same * inverse)
        dk_acc[:, win_lanes] += dot_nt(q_sub, dscore)
        dkf_acc[:, lin_lanes] += dot_nt(qf_sub, dlink)
        dq_parts.append(dot_nn(kt_ref[:, win_lanes], dscore) * SCALE)
        dqf = dot_nn(kft_ref[:, lin_lanes], dlink) + dot_nn(state_low, dcarried) + norm * dtotal
        dst = dst + dot_nt(qf_sub, dcarried)
        dstt = dstt + dot_nt(dcarried, qf_sub)
        weighted = qf_sub.astype(F32) * dtotal
        for h in range(ratio):
            dnorm = dnorm + weighted[:, h * SUB : (h + 1) * SUB]
        dpre_parts.append(halves_backward(side_by_side(probabilities, sub), dqf).astype(BF16))
    dst_ref[...] = dst.astype(BF16).astype(F32)
    dstt_ref[...] = dstt.astype(BF16).astype(F32)
    dnorm_ref[...] = jnp.sum(dnorm, axis=1, keepdims=True) + keep * dnorm_ref[...]
    for h in range(ratio):
        lanes = slice(h * SUB, (h + 1) * SUB)
        dpre = jnp.concatenate([part[:, lanes] for part in dpre_parts], axis=1)
        dq = jnp.concatenate([part[:, lanes] for part in dq_parts], axis=1)
        dq = dq + dot_nn(qback_ref[h], dpre)
        dqt_ref[h * HEAD_DIM : (h + 1) * HEAD_DIM, :] = dq.astype(BF16)
        gqm_ref[h] += dot_nt(queries[h], dpre)

    @pl.when(step == blocks - 1)
    def _():
        key_probs = softmax_halves(dot_nn(kmap_ref[0], kt_ref[...]))
        dpre = halves_backward(key_probs, dkf_acc[...]).astype(BF16)
        dk = dk_acc[...] * SCALE + dot_nn(kback_ref[0], dpre)
        dkt_ref[...] = dk.astype(BF16)
        dvt_ref[...] = dv_acc[...].astype(BF16)
        gkm_ref[0] = dot_nt(kt_ref[...], dpre)


def signed_maps(maps):
    turned = jnp.swapaxes(maps, 1, 2)
    return jnp.concatenate([turned, -turned], axis=1)


def attention_specs(groups, ratio, padded, block_of):
    rows = ratio * HEAD_DIM
    return [
        pl.BlockSpec((1, 1, BLOCK), lambda g, i, *_: (0, 0, block_of(i))),
        pl.BlockSpec((rows, BLOCK), lambda g, i, *_: (g, block_of(i))),
        pl.BlockSpec((HEAD_DIM, padded), lambda g, i, *_: (g, 0)),
        pl.BlockSpec((HEAD_DIM, padded), lambda g, i, *_: (groups + g, 0)),
        pl.BlockSpec((ratio, 2 * HEAD_DIM, HEAD_DIM), lambda g, i, *_: (g, 0, 0)),
        pl.BlockSpec((1, 2 * HEAD_DIM, HEAD_DIM), lambda g, i, *_: (g, 0, 0)),
    ]


def attention_forward(marks, starts, qt, kvt, qmap, kmap):
    length = qt.shape[1]
    padded = kvt.shape[1]
    groups = kmap.shape[0]
    ratio = qmap.shape[0] // groups
    rows = ratio * HEAD_DIM
    blocks = length // BLOCK
    return pl.pallas_call(
        forward_kernel,
        out_shape=(
            jax.ShapeDtypeStruct(qt.shape, BF16),
            jax.ShapeDtypeStruct((groups, ratio, length), F32),
        ),
        grid_spec=pltpu.PrefetchScalarGridSpec(
            num_scalar_prefetch=1,
            grid=(groups, blocks),
            in_specs=attention_specs(groups, ratio, padded, lambda i: i),
            out_specs=[
                pl.BlockSpec((rows, BLOCK), lambda g, i, *_: (g, i)),
                pl.BlockSpec((1, ratio, BLOCK), lambda g, i, *_: (g, 0, i)),
            ],
            scratch_shapes=[
                pltpu.VMEM((2 * HEAD_DIM, padded), BF16),
                pltpu.VMEM((padded, 2 * HEAD_DIM), BF16),
                pltpu.VMEM((padded, HEAD_DIM), BF16),
                pltpu.VMEM((HEAD_DIM, 2 * HEAD_DIM), F32),
                pltpu.VMEM((2 * HEAD_DIM, 1), F32),
            ],
        ),
        compiler_params=pltpu.CompilerParams(
            dimension_semantics=("arbitrary", "arbitrary"), vmem_limit_bytes=48 * 1024 * 1024
        ),
        cost_estimate=pl.CostEstimate(flops=1000, bytes_accessed=1000, transcendentals=0),
        name="attention_forward",
    )(marks, starts, qt, kvt, kvt, signed_maps(qmap), signed_maps(kmap))


def attention_backward(marks, starts, qt, kvt, qmap, kmap, dmt, mixt, inverse):
    length = qt.shape[1]
    padded = kvt.shape[1]
    groups = kmap.shape[0]
    ratio = qmap.shape[0] // groups
    rows = ratio * HEAD_DIM
    blocks = length // BLOCK
    back = lambda i: blocks - 1 - i
    query_spec = pl.BlockSpec((rows, BLOCK), lambda g, i, *_: (g, back(i)))
    key_spec = pl.BlockSpec((HEAD_DIM, padded), lambda g, i, *_: (g, 0))
    return pl.pallas_call(
        backward_kernel,
        out_shape=(
            jax.ShapeDtypeStruct(qt.shape, BF16),
            jax.ShapeDtypeStruct((groups * HEAD_DIM, padded), BF16),
            jax.ShapeDtypeStruct((groups * HEAD_DIM, padded), BF16),
            jax.ShapeDtypeStruct(qmap.shape, F32),
            jax.ShapeDtypeStruct(kmap.shape, F32),
        ),
        grid_spec=pltpu.PrefetchScalarGridSpec(
            num_scalar_prefetch=1,
            grid=(groups, blocks),
            in_specs=attention_specs(groups, ratio, padded, back)
            + [
                query_spec,
                query_spec,
                pl.BlockSpec((1, ratio, BLOCK), lambda g, i, *_: (g, 0, back(i))),
                pl.BlockSpec((ratio, HEAD_DIM, HEAD_DIM), lambda g, i, *_: (g, 0, 0)),
                pl.BlockSpec((1, HEAD_DIM, HEAD_DIM), lambda g, i, *_: (g, 0, 0)),
            ],
            out_specs=[
                query_spec,
                key_spec,
                key_spec,
                pl.BlockSpec((ratio, HEAD_DIM, HEAD_DIM), lambda g, i, *_: (g, 0, 0)),
                pl.BlockSpec((1, HEAD_DIM, HEAD_DIM), lambda g, i, *_: (g, 0, 0)),
            ],
            scratch_shapes=[
                pltpu.VMEM((2 * HEAD_DIM, padded), BF16),
                pltpu.VMEM((padded, 2 * HEAD_DIM), BF16),
                pltpu.VMEM((padded, HEAD_DIM), BF16),
                pltpu.VMEM((padded, HEAD_DIM), BF16),
                pltpu.VMEM((blocks, 2 * HEAD_DIM, HEAD_DIM), BF16),
                pltpu.VMEM((blocks, HEAD_DIM, 2 * HEAD_DIM), BF16),
                pltpu.VMEM((blocks, 2 * HEAD_DIM, 1), F32),
                pltpu.VMEM((HEAD_DIM, padded), F32),
                pltpu.VMEM((2 * HEAD_DIM, padded), F32),
                pltpu.VMEM((HEAD_DIM, padded), F32),
                pltpu.VMEM((2 * HEAD_DIM, HEAD_DIM), F32),
                pltpu.VMEM((HEAD_DIM, 2 * HEAD_DIM), F32),
                pltpu.VMEM((2 * HEAD_DIM, 1), F32),
            ],
        ),
        compiler_params=pltpu.CompilerParams(
            dimension_semantics=("arbitrary", "arbitrary"), vmem_limit_bytes=48 * 1024 * 1024
        ),
        cost_estimate=pl.CostEstimate(flops=1000, bytes_accessed=1000, transcendentals=0),
        name="attention_backward",
    )(
        marks, starts, qt, kvt, kvt, signed_maps(qmap), signed_maps(kmap), dmt, mixt, inverse, qmap, kmap
    )


FREE = pl.CostEstimate(flops=1000, bytes_accessed=1000, transcendentals=0)


def grid_call(kernel, name, grid, out_shape, in_specs, out_specs, scratch=(), aliases=None):
    return pl.pallas_call(
        kernel,
        out_shape=out_shape,
        grid_spec=pltpu.PrefetchScalarGridSpec(
            num_scalar_prefetch=1,
            grid=grid,
            in_specs=in_specs,
            out_specs=out_specs,
            scratch_shapes=list(scratch),
        ),
        input_output_aliases=aliases or {},
        compiler_params=pltpu.CompilerParams(
            dimension_semantics=("arbitrary",) * len(grid), vmem_limit_bytes=VMEM_LIMIT
        ),
        cost_estimate=FREE,
        name=name,
    )


MESH = pl.DeviceIdType.MESH
FAR_CHUNKS = 4


def exchange_kernel(query_cols, key_cols, *refs):
    inputs, grads, query, key, value, gate, up, down, output = refs[:9]
    thin = refs[9:15]
    far, near_other, far_other, grads_other, proj_got, gate_got, up_got, down_got, output_got = (
        refs[15:24]
    )
    thin_got = refs[24:30]
    proj_own, proj_both, output_both = refs[30:33]
    send_sem, recv_sem, local_sem, proj_all, output_all = refs[33:]
    row, col = lax.axis_index("row"), lax.axis_index("col")

    barrier = pltpu.get_barrier_semaphore()
    pl.semaphore_signal(barrier, inc=1, device_id={"row": 1 - row}, device_id_type=MESH)
    pl.semaphore_signal(barrier, inc=1, device_id={"col": 1 - col}, device_id_type=MESH)
    pl.semaphore_wait(barrier, 2)

    copies = []

    def remote(source, target, axis, place):
        n = len(copies)
        copy = pltpu.make_async_remote_copy(
            src_ref=source,
            dst_ref=target,
            send_sem=send_sem.at[n],
            recv_sem=recv_sem.at[n],
            device_id={axis: 1 - place},
            device_id_type=MESH,
        )
        copy.start()
        copies.append(copy)
        return copy

    def columns(ref, index, width):
        return ref.at[:, pl.ds(pl.multiple_of(index * width, width), width)]

    def rows_of(ref, index, height):
        return ref.at[pl.ds(pl.multiple_of(index * height, height), height), :]

    size = inputs.shape[0] // FAR_CHUNKS
    chunks = [pl.ds(i * size, size) for i in range(FAR_CHUNKS)]
    arriving = [remote(inputs.at[at, :], far.at[at, :], "row", row) for at in chunks]
    remote(inputs, near_other, "col", col)
    first = 0
    for weight, width in ((query, query_cols), (key, key_cols), (value, key_cols)):
        remote(
            columns(weight, 1 - col, width), proj_got.at[:, pl.ds(first, width)], "col", col
        )
        first += width
    for source, target in zip(thin, thin_got):
        remote(source, target, "col", col)
    remote(columns(gate, 1 - col, gate_got.shape[1]), gate_got, "col", col)
    remote(columns(up, 1 - col, up_got.shape[1]), up_got, "col", col)
    remote(rows_of(down, 1 - col, down_got.shape[0]), down_got, "col", col)
    remote(rows_of(output, 1 - col, output_got.shape[0]), output_got, "col", col)
    remote(grads, grads_other, "col", col)

    def local(source, target, n):
        copy = pltpu.make_async_copy(source, target, local_sem.at[n])
        copy.start()
        return copy

    whole = proj_own.shape[1]
    height = output_got.shape[0]
    loads, first = [], 0
    for weight, width in ((query, query_cols), (key, key_cols), (value, key_cols)):
        for side in range(2):
            loads.append(
                local(
                    columns(weight, col ^ side, width),
                    proj_all.at[:, pl.ds(side * whole + first, width)],
                    len(loads),
                )
            )
        first += width
    for side in range(2):
        loads.append(
            local(
                rows_of(output, col ^ side, height),
                output_all.at[pl.ds(side * height, height), :],
                len(loads),
            )
        )
    for copy in loads:
        copy.wait()
    stores = [
        local(proj_all.at[:, pl.ds(0, whole)], proj_own, 8),
        local(proj_all, proj_both, 9),
        local(output_all, output_both, 10),
    ]

    for copy, at in zip(arriving, chunks):
        copy.wait_recv()
        remote(far.at[at, :], far_other.at[at, :], "col", col)
    for copy in stores:
        copy.wait()
    for n, copy in enumerate(copies):
        copy.wait_send()
        if n >= FAR_CHUNKS:
            copy.wait_recv()


def exchange(inputs, grads, projections, gate, up, down, output, thin):
    query, key, value = projections
    rows, half = inputs.shape
    query_cols, key_cols = query.shape[1] // 2, key.shape[1] // 2
    columns = query_cols + 2 * key_cols
    like = lambda *shape: jax.ShapeDtypeStruct(shape, BF16)
    outs = [
        like(rows, half),
        like(rows, half),
        like(rows, half),
        like(rows, half),
        like(half, columns),
        like(half, gate.shape[1] // 2),
        like(half, up.shape[1] // 2),
        like(down.shape[0] // 2, half),
        like(output.shape[0] // 2, half),
    ]
    outs += [jax.ShapeDtypeStruct(values.shape, values.dtype) for values in thin]
    outs += [like(half, columns), like(half, 2 * columns), like(output.shape[0], half)]
    copies = 2 * FAR_CHUNKS + 1 + 3 + len(thin) + 5
    return pl.pallas_call(
        functools.partial(exchange_kernel, query_cols, key_cols),
        out_shape=tuple(outs),
        in_specs=[pl.BlockSpec(memory_space=pl.ANY)] * (9 + len(thin)),
        out_specs=tuple([pl.BlockSpec(memory_space=pl.ANY)] * len(outs)),
        scratch_shapes=[
            pltpu.SemaphoreType.DMA((copies,)),
            pltpu.SemaphoreType.DMA((copies,)),
            pltpu.SemaphoreType.DMA((11,)),
            pltpu.VMEM((half, 2 * columns), BF16),
            pltpu.VMEM(output.shape, BF16),
        ],
        compiler_params=pltpu.CompilerParams(
            collective_id=0, has_side_effects=True, vmem_limit_bytes=VMEM_LIMIT
        ),
        cost_estimate=FREE,
        name="exchange",
    )(inputs, grads, query, key, value, gate, up, down, output, *thin)


def hidden_grad_kernel(place_ref, gm_own, go_own, gm_far, go_far, down_own, down_got, out_ref):
    half = gm_own.shape[0]
    out_ref[:half] = (
        dot_nt(gm_own[...], down_own[...]) + dot_nt(go_own[...], down_got[...])
    ).astype(BF16)
    out_ref[half:] = (
        dot_nt(gm_far[...], down_own[...]) + dot_nt(go_far[...], down_got[...])
    ).astype(BF16)


def hidden_grad(place, grads, down_weight, down_got):
    half, width = grads[0].shape
    hidden_cols = down_got.shape[0]
    tiles = hidden_cols // MLP_TILE
    whole = pl.BlockSpec((half, width), lambda i, s: (0, 0))
    return grid_call(
        hidden_grad_kernel,
        "hidden_grad",
        (tiles,),
        jax.ShapeDtypeStruct((2 * half, hidden_cols), BF16),
        [whole] * 4
        + [
            pl.BlockSpec((MLP_TILE, width), lambda i, s: (s[0] * tiles + i, 0)),
            pl.BlockSpec((MLP_TILE, width), lambda i, s: (i, 0)),
        ],
        pl.BlockSpec((2 * half, MLP_TILE), lambda i, s: (0, i)),
    )(place, *grads, down_weight, down_got)


def project_kernel(
    place_ref, mine_ref, other_ref, gain_ref, proj_own, proj_got, down_ref, up_ref, *refs
):
    normed_ref, queries_ref, keys_ref, adapters_ref, scale_ref = refs[-5:]
    half = mine_ref.shape[1]
    mine, other = mine_ref[...].astype(F32), other_ref[...].astype(F32)
    squares = jnp.sum(mine * mine, axis=1, keepdims=True) + jnp.sum(
        other * other, axis=1, keepdims=True
    )
    scale = lax.rsqrt(squares / (2 * half) + norm_eps)
    left = (mine * scale * gain_ref[:, :half]).astype(BF16)
    right = (other * scale * gain_ref[:, half:]).astype(BF16)
    normed_ref[:, :half] = left
    normed_ref[:, half:] = right
    scale_ref[...] = scale
    adapters = (dot_nn(left, down_ref[:half]) + dot_nn(right, down_ref[half:])).astype(BF16)
    adapters_ref[...] = adapters
    sums = dot_nn(left, proj_own[...]) + dot_nn(right, proj_got[...]) + dot_nn(adapters, up_ref[...])
    turned = jnp.transpose(sums.astype(BF16))
    rows = queries_ref.shape[0]
    queries_ref[...] = turned[:rows]
    keys_ref[...] = turned[rows:]


def global_block(local, flip, half_blocks):
    return ((local // half_blocks) ^ flip) * half_blocks + local % half_blocks


def project_block(index, place, mine, other, gain, proj_own, proj_got, down, up, query_part, kept):
    rows, half = mine.shape
    length = 2 * half_rows_of(kept, rows)
    blocks, half_blocks = length // BLOCK, length // BLOCK // 2
    columns = proj_own.shape[1]
    whole = lambda values: pl.BlockSpec(values.shape, lambda i, s: (0, 0))
    lanes = lambda i, s: (0, global_block(index + i, s[1], half_blocks))
    local = lambda i, s: (index + i, 0)
    shapes = (
        jax.ShapeDtypeStruct((length, 2 * half), BF16),
        jax.ShapeDtypeStruct((query_part, length), BF16),
        jax.ShapeDtypeStruct((columns - query_part, length), BF16),
        jax.ShapeDtypeStruct((length, LANES), BF16),
        jax.ShapeDtypeStruct((length, 1), F32),
    )
    return grid_call(
        project_kernel,
        "project_block",
        (rows // BLOCK,),
        shapes,
        [
            pl.BlockSpec((BLOCK, half), lambda i, s: (i, 0)),
            pl.BlockSpec((BLOCK, half), lambda i, s: (i, 0)),
            whole(gain),
            whole(proj_own),
            whole(proj_got),
            whole(down),
            whole(up),
        ]
        + [pl.BlockSpec(memory_space=pl.ANY)] * len(kept),
        [
            pl.BlockSpec((BLOCK, 2 * half), local),
            pl.BlockSpec((query_part, BLOCK), lanes),
            pl.BlockSpec((columns - query_part, BLOCK), lanes),
            pl.BlockSpec((BLOCK, LANES), local),
            pl.BlockSpec((BLOCK, 1), local),
        ],
        aliases={8 + i: i for i in range(len(kept))},
    )(place, mine, other, gain, proj_own, proj_got, down, up, *kept)


def half_rows_of(kept, rows):
    return kept[0].shape[0] // 2 if kept else rows


def mlp_kernel(
    count,
    place_ref,
    in_mine,
    in_other,
    at_mine,
    at_other,
    far_mine,
    far_other,
    adapter_ref,
    up_ref,
    gain_ref,
    gate_own,
    gate_got,
    up_own,
    up_got,
    dh_ref,
    *refs,
):
    hidden_ref, dgate_ref, dup_ref, normed_ref, scale_ref = refs[-1 - count : -1][:5]
    left_ref = refs[-1]
    half = in_mine.shape[1]

    @pl.when(pl.program_id(0) == 0)
    def _():
        def state(inputs, own, far, adapted):
            return inputs[...].astype(F32) + (
                own[...].astype(F32) + far[...].astype(F32) + adapted
            )

        adapter = adapter_ref[...]
        mine = state(in_mine, at_mine, far_mine, dot_nn(adapter, up_ref[:, :half]))
        other = state(in_other, at_other, far_other, dot_nn(adapter, up_ref[:, half:]))
        squares = jnp.sum(mine * mine, axis=1, keepdims=True) + jnp.sum(
            other * other, axis=1, keepdims=True
        )
        scale = lax.rsqrt(squares / (2 * half) + norm_eps)
        scale_ref[...] = scale
        if count == 6:
            refs[-2][...] = mine
        left_ref[:, :half] = (mine * scale * gain_ref[:, :half]).astype(BF16)
        left_ref[:, half:] = (other * scale * gain_ref[:, half:]).astype(BF16)
        normed_ref[...] = left_ref[...]

    left, right = left_ref[:, :half], left_ref[:, half:]
    gate = dot_nn(left, gate_own[...]) + dot_nn(right, gate_got[...])
    up = dot_nn(left, up_own[...]) + dot_nn(right, up_got[...])
    d_hidden = dh_ref[...].astype(F32)
    sig = 1.0 / (1.0 + jnp.exp(-gate))
    silu = gate * sig
    hidden_ref[...] = (silu * up).astype(BF16)
    dup_ref[...] = (d_hidden * silu).astype(BF16)
    dgate_ref[...] = (d_hidden * up * (sig * (1.0 + gate * (1.0 - sig)))).astype(BF16)


def mlp_block(
    index,
    place,
    inputs,
    input_block,
    attended,
    adapter,
    output_up,
    gain,
    gate_weight,
    gate_got,
    up_weight,
    up_got,
    d_hidden,
    kept,
    state_kept,
    with_state,
):
    half, hidden_cols = gate_got.shape
    width = 2 * half
    length = d_hidden.shape[0]
    tiles = hidden_cols // MLP_TILE
    own_spec = pl.BlockSpec((half, MLP_TILE), lambda i, s: (0, s[0] * tiles + i))
    got_spec = pl.BlockSpec((half, MLP_TILE), lambda i, s: (0, i))
    kept_spec = pl.BlockSpec((BLOCK, MLP_TILE), lambda i, s: (index, i))
    here = lambda columns: pl.BlockSpec((BLOCK, columns), lambda i, s: (index, 0))
    whole = lambda values: pl.BlockSpec(values.shape, lambda i, s: (0, 0))
    input_spec = pl.BlockSpec((BLOCK, half), lambda i, s: (input_block, 0))
    block_spec = pl.BlockSpec((BLOCK, half), lambda i, s: (0, 0))
    shapes = (jax.ShapeDtypeStruct((length, hidden_cols), BF16),) * 3 + (
        jax.ShapeDtypeStruct((length, width), BF16),
        jax.ShapeDtypeStruct((length, 1), F32),
    )
    out_specs = [kept_spec] * 3 + [here(width), here(1)]
    aliases = {15 + i: i for i in range(len(kept))}
    passed = tuple(kept)
    if with_state:
        shapes += (jax.ShapeDtypeStruct((length // 2, half), F32),)
        out_specs.append(here(half))
        if state_kept is not None:
            aliases[15 + len(passed)] = 5
            passed += (state_kept,)
    return grid_call(
        functools.partial(mlp_kernel, len(shapes)),
        "mlp_block",
        (tiles,),
        shapes,
        [input_spec, input_spec]
        + [block_spec] * 4
        + [here(adapter.shape[1]), whole(output_up), whole(gain)]
        + [own_spec, got_spec, own_spec, got_spec, kept_spec]
        + [pl.BlockSpec(memory_space=pl.ANY)] * len(passed),
        out_specs,
        [pltpu.VMEM((BLOCK, width), BF16)],
        aliases,
    )(
        place,
        *inputs,
        *attended,
        adapter,
        output_up,
        gain,
        gate_weight,
        gate_got,
        up_weight,
        up_got,
        d_hidden,
        *passed,
    )


def norm_back_kernel(
    count,
    place_ref,
    total_mine,
    total_other,
    normed_ref,
    scale_ref,
    grad_mine,
    grad_other,
    gain_ref,
    out_own,
    out_got,
    up_ref,
    down_ref,
    *refs,
):
    mixed_ref, mine_ref, adapter_ref, gain_sum = refs[-count:][:4]
    half = total_mine.shape[1]
    gain_left, gain_right = gain_ref[:, :half], gain_ref[:, half:]
    d_left, d_right = total_mine[...].astype(F32), total_other[...].astype(F32)
    hat_left = normed_ref[:, :half].astype(F32) * (1.0 / gain_left)
    hat_right = normed_ref[:, half:].astype(F32) * (1.0 / gain_right)
    term = jnp.sum(d_left * hat_left, axis=0, keepdims=True)
    g_left, g_right = d_left * gain_left, d_right * gain_right
    inner = (
        jnp.sum(g_left * hat_left, axis=1, keepdims=True)
        + jnp.sum(g_right * hat_right, axis=1, keepdims=True)
    ) / (2 * half)
    scale = scale_ref[...]
    left = grad_mine[...].astype(F32) + scale * (g_left - hat_left * inner)
    right = grad_other[...].astype(F32) + scale * (g_right - hat_right * inner)
    if count == 5:
        refs[-1][...] = left
    left, right = left.astype(BF16), right.astype(BF16)
    mine_ref[...] = left
    adapter = (dot_nt(left, up_ref[:, :half]) + dot_nt(right, up_ref[:, half:])).astype(BF16)
    adapter_ref[...] = adapter
    mixed_ref[...] = (
        dot_nt(out_own[...], left) + dot_nt(out_got[...], right) + dot_nt(down_ref[...], adapter)
    ).astype(BF16)

    @pl.when(pl.program_id(0) == 0)
    def _():
        gain_sum[...] = term

    @pl.when(pl.program_id(0) > 0)
    def _():
        gain_sum[...] += term


def norm_back(
    index, place, totals, normed, scale, grads, gain, out_own, out_got, up, down, kept, with_state
):
    half_rows, half = totals[0].shape
    length = 2 * half_rows
    half_blocks = half_rows // BLOCK
    heads = out_own.shape[0]
    base = index * half_blocks
    whole = lambda values: pl.BlockSpec(values.shape, lambda i, s: (0, 0))
    near = pl.BlockSpec((BLOCK, half), lambda i, s: (i, 0))
    here = lambda columns: pl.BlockSpec((BLOCK, columns), lambda i, s: (base + i, 0))
    shapes = (
        jax.ShapeDtypeStruct((heads, length), BF16),
        jax.ShapeDtypeStruct((length, half), BF16),
        jax.ShapeDtypeStruct((length, LANES), BF16),
        jax.ShapeDtypeStruct((1, half), F32),
    )
    out_specs = [
        pl.BlockSpec((heads, BLOCK), lambda i, s: (0, global_block(base + i, s[1], half_blocks))),
        here(half),
        here(LANES),
        pl.BlockSpec((1, half), lambda i, s: (0, 0)),
    ]
    if with_state:
        shapes += (jax.ShapeDtypeStruct((half_rows, half), F32),)
        out_specs.append(near)
    return grid_call(
        functools.partial(norm_back_kernel, len(shapes)),
        "norm_back",
        (half_blocks,),
        shapes,
        [near, near, here(2 * half), here(1), near, near]
        + [whole(values) for values in (gain, out_own, out_got, up, down)]
        + [pl.BlockSpec(memory_space=pl.ANY)] * len(kept),
        out_specs,
        aliases={12 + i: i for i in range(len(kept))},
    )(place, *totals, normed, scale, *grads, gain, out_own, out_got, up, down, *kept)


def second_grad_kernel(
    place_ref, dg_ref, du_ref, gate_own, gate_got, up_own, up_got, own_ref, other_ref
):
    own_ref[...] = (dot_nt(dg_ref[...], gate_own[...]) + dot_nt(du_ref[...], up_own[...])).astype(
        BF16
    )
    other_ref[...] = (
        dot_nt(dg_ref[...], gate_got[...]) + dot_nt(du_ref[...], up_got[...])
    ).astype(BF16)


def second_grad(index, place, d_gate, d_up, gate_weight, gate_got, up_weight, up_got):
    half, hidden_cols = gate_got.shape
    tile = min(SUM_TILE, half)
    rows = d_gate.shape[0] // 2
    left = pl.BlockSpec((rows, hidden_cols), lambda i, s: (index, 0))
    own_spec = pl.BlockSpec((tile, hidden_cols), lambda i, s: (i, s[0]))
    got_spec = pl.BlockSpec((tile, hidden_cols), lambda i, s: (i, 0))
    out_spec = pl.BlockSpec((rows, tile), lambda i, s: (0, i))
    return grid_call(
        second_grad_kernel,
        "second_grad",
        (half // tile,),
        (jax.ShapeDtypeStruct((rows, half), BF16),) * 2,
        [left, left, own_spec, got_spec, own_spec, got_spec],
        [out_spec, out_spec],
    )(place, d_gate, d_up, gate_weight, gate_got, up_weight, up_got)


def down_kernel(place_ref, hidden_ref, down_own, down_got, own_ref, other_ref):
    own_ref[...] = dot_nn(hidden_ref[...], down_own[...]).astype(BF16)
    other_ref[...] = dot_nn(hidden_ref[...], down_got[...]).astype(BF16)


def down_product(place, hidden, down_weight, down_got):
    length, hidden_cols = hidden.shape
    half = down_got.shape[1]
    tile = min(SUM_TILE, half)
    out_spec = pl.BlockSpec((length, tile), lambda i, s: (0, i))
    return grid_call(
        down_kernel,
        "down_product",
        (half // tile,),
        (jax.ShapeDtypeStruct((length, half), BF16),) * 2,
        [
            pl.BlockSpec((length, hidden_cols), lambda i, s: (0, 0)),
            pl.BlockSpec((hidden_cols, tile), lambda i, s: (s[0], i)),
            pl.BlockSpec((hidden_cols, tile), lambda i, s: (0, i)),
        ],
        [out_spec, out_spec],
    )(place, hidden, down_weight, down_got)


def weight_grad_kernel(sets, chunks, pieces, turned, right_turned, place_ref, *refs):
    outs = refs[-1 - pieces * sets : -1]
    right_ref, left_ref = refs[-2 - pieces * sets], refs[-1]
    lefts = refs[: -2 - pieces * sets]
    length = left_ref.shape[1]
    rows = left_ref.shape[0] // sets
    count = rows // LANES

    @pl.when(pl.program_id(0) == 0)
    def _():
        for p in range(sets * count):
            lanes = slice(p * LANES, (p + 1) * LANES)
            if turned:
                left_ref[lanes, :] = lefts[p][...]
            else:
                size = length // chunks
                for i in range(chunks):
                    left_ref[lanes, i * size : (i + 1) * size] = jnp.transpose(
                        lefts[p * chunks + i][...]
                    )

    for which in range(sets):
        left = left_ref[which * rows : (which + 1) * rows, :]
        sums = (dot_nt if right_turned else dot_nn)(left, right_ref[...])
        size = rows // pieces
        for i in range(pieces):
            outs[pieces * which + i][...] = sums[i * size : (i + 1) * size].astype(BF16)


def weight_grad(places, sets, right, pieces=2, turned=False, right_turned=False):
    chunks = len(sets[0][0])
    length = sets[0][0][0].shape[1] if turned else sum(c.shape[0] for c in sets[0][0])
    count = (places.shape[0] - 2) // len(sets)
    columns = right.shape[0] if right_turned else right.shape[1]
    tile = min(GRAD_TILE, columns)
    in_specs, operands = [], []
    for n, (lefts, base) in enumerate(sets):
        for p in range(count):
            at = 2 + n * count + p
            for left in lefts:
                if turned:
                    spec = pl.BlockSpec((LANES, length), lambda j, s, at=at: (s[at], 0))
                else:
                    spec = pl.BlockSpec(
                        (left.shape[0], LANES), lambda j, s, at=at, base=base: (0, base + s[at])
                    )
                in_specs.append(spec)
                operands.append(left)
    if right_turned:
        in_specs.append(pl.BlockSpec((tile, length), lambda j, s: (j, 0)))
    else:
        in_specs.append(pl.BlockSpec((length, tile), lambda j, s: (0, j)))
    size = count * LANES // pieces
    out_spec = pl.BlockSpec((size, tile), lambda j, s: (0, j))
    return grid_call(
        functools.partial(weight_grad_kernel, len(sets), chunks, pieces, turned, right_turned),
        "weight_grad",
        (columns // tile,),
        (jax.ShapeDtypeStruct((size, columns), BF16),) * (pieces * len(sets)),
        in_specs,
        [out_spec] * (pieces * len(sets)),
        [pltpu.VMEM((len(sets) * count * LANES, length), BF16)],
    )(places, *operands, right)


def after(value, *others):
    return lax.optimization_barrier((value,) + others)[0]


def swap(values, axis):
    return lax.ppermute(values, axis, [(0, 1), (1, 0)])


def part(values, index, count, axis):
    width = values.shape[axis] // count
    return lax.dynamic_slice_in_dim(values, index * width, width, axis)


def contract(left, right, left_dim, right_dim):
    return lax.dot_general(
        left, right, (((left_dim,), (right_dim,)), ((), ())), preferred_element_type=F32
    )


def exchange_order(bits, first):
    return [(first + k) % bits for k in range(bits)]


def relative_index(position, order):
    bits = len(order)
    return sum(((position >> (bits - 1 - k)) & 1) << order[k] for k in range(bits))


def relative_blocks(values, axis, device, order):
    count = 1 << len(order)
    return jnp.concatenate(
        [part(values, device ^ relative_index(p, order), count, axis) for p in range(count)],
        axis=axis,
    )


class Reduction:
    def __init__(self, keep, send, size, order):
        self.keep, self.size, self.order, self.step = keep, size, order, 0
        self.launch(send)

    def launch(self, send):
        bit = 1 << self.order[self.step]
        self.got = lax.ppermute(send, "dp", [(i, i ^ bit) for i in range(self.size)])

    def combine(self):
        got = self.got
        self.step += 1
        if self.step == len(self.order):
            self.keep = self.keep.astype(F32) + got.astype(F32)
            return self.keep
        half = self.keep.shape[0] // 2
        sums = (
            (self.keep[rows].astype(F32) + got[rows].astype(F32)).astype(BF16)
            for rows in (slice(0, half), slice(half, 2 * half))
        )
        self.keep, send = sums
        self.launch(send)
        return self.keep

    @property
    def done(self):
        return self.step == len(self.order)


def total_over(values, size, bits):
    for k in range(bits):
        values = values + lax.ppermute(values, "dp", [(i, i ^ (1 << k)) for i in range(size)])
    return values


def ordered(own, other, index, axis):
    return jnp.where(
        index == 0,
        jnp.concatenate([own, other], axis=axis),
        jnp.concatenate([other, own], axis=axis),
    )


def on_device(
    activations,
    grad_out,
    segments,
    first_gain,
    query_weight,
    key_weight,
    value_weight,
    query_down,
    query_up,
    key_down,
    key_up,
    value_down,
    value_up,
    query_map,
    key_map,
    output_weight,
    output_down,
    output_up,
    second_gain,
    gate_weight,
    up_weight,
    down_weight,
):
    size = lax.axis_size("dp")
    bits = size.bit_length() - 1
    device = lax.axis_index("dp")
    row = lax.axis_index("row")
    col = lax.axis_index("col")
    seq_rows = segments.shape[1]
    half_rows, feature_cols = activations.shape
    width = 2 * feature_cols
    blocks = seq_rows // BLOCK
    half_blocks = blocks // 2
    rank = query_down.shape[1]
    query_part = query_weight.shape[1] // 2
    key_part = key_weight.shape[1] // 2
    part_cols = query_part + 2 * key_part
    order = exchange_order(bits, 0)
    turned_order = exchange_order(bits, 1)

    def other_half(values, axis):
        return jnp.roll(values, values.shape[axis] // 2, axis)

    def sequence_order(values, axis):
        return jnp.where(row == 0, values, other_half(values, axis))

    def rows_of(index):
        return slice(index * BLOCK, (index + 1) * BLOCK)

    lane_blocks = feature_cols // LANES
    direct = lane_blocks == size

    def block_order(which, rows_of_pair=False):
        if not direct:
            return [jnp.int32(p) for p in range(lane_blocks)]
        blocks_of = [device ^ relative_index(p, which) for p in range(size)]
        if rows_of_pair:
            return [((b // (size // 2)) ^ col) * (size // 2) + b % (size // 2) for b in blocks_of]
        return blocks_of

    def places(*orders, rows_of_pair=False):
        entries = [col, row]
        for which in orders:
            entries += block_order(which, rows_of_pair)
        return jnp.stack([jnp.asarray(v, jnp.int32) for v in entries])

    place = places(order)

    def grads_of(sets, right, orders, right_turned=False):
        if not direct:
            sets = [
                (
                    [
                        relative_blocks(
                            left[:, base * LANES : base * LANES + feature_cols], 1, device, which
                        )
                        for left in lefts
                    ],
                    0,
                )
                for (lefts, base), which in zip(sets, orders)
            ]
        outs = weight_grad(places(*orders), sets, right, 2, False, right_turned)
        return [outs[2 * n : 2 * n + 2] for n in range(len(sets))]

    def ups(index):
        zeros_key = jnp.zeros((rank, key_part), BF16)
        zeros_query = jnp.zeros((rank, query_part), BF16)
        return jnp.concatenate(
            [
                jnp.concatenate([part(query_up, index, 2, 1), zeros_key, zeros_key], axis=1),
                jnp.concatenate([zeros_query, part(key_up, index, 2, 1), zeros_key], axis=1),
                jnp.concatenate([zeros_query, zeros_key, part(value_up, index, 2, 1)], axis=1),
            ],
            axis=0,
        )

    (
        inputs_far,
        inputs_other,
        inputs_far_other,
        grads_other,
        proj_got,
        gate_got,
        up_got,
        mlp_down_got,
        output_got,
        first_gain_got,
        second_gain_got,
        query_down_got,
        key_down_got,
        value_down_got,
        output_up_got,
        proj_own,
        proj_native,
        output_native,
    ) = exchange(
        activations,
        grad_out,
        (query_weight, key_weight, value_weight),
        gate_weight,
        up_weight,
        down_weight,
        output_weight,
        (first_gain, second_gain, query_down, key_down, value_down, output_up),
    )
    grads_far = swap(after(grad_out, inputs_far), "row")
    up_own = ups(col)
    up_native = jnp.concatenate([up_own, ups(1 - col)], axis=1)
    down_own = jnp.concatenate([query_down, key_down, value_down], axis=1)
    down_got = jnp.concatenate([query_down_got, key_down_got, value_down_got], axis=1)
    down_full = jnp.concatenate([down_own, down_got], axis=0)
    down_full = jnp.pad(down_full, ((0, 0), (0, LANES - 3 * rank)))
    up_padded = jnp.pad(up_own, ((0, LANES - 3 * rank), (0, 0)))
    gain_full = jnp.concatenate([first_gain, first_gain_got])[None]
    second_gain_full = jnp.concatenate([second_gain, second_gain_got])[None]
    output_up_full = jnp.concatenate([output_up, output_up_got], axis=1)
    output_up_full = jnp.pad(output_up_full, ((0, LANES - rank), (0, 0)))
    output_rows_own = part(output_weight, col, 2, 0)
    output_down_own = part(output_down, col, 2, 0)
    output_down_native = jnp.concatenate(
        [output_down_own, part(output_down, 1 - col, 2, 0)], axis=0
    )
    output_down_padded = jnp.pad(output_down_own, ((0, 0), (0, LANES - rank)))
    query_map_own = part(query_map, col, 2, 0)
    key_map_own = part(key_map, col, 2, 0)

    documents = segments[0]
    starts = jnp.sum((documents[None, :] < documents[:, None]).astype(jnp.int32), axis=1)
    marks = jnp.concatenate(
        [jnp.full((1,), seq_rows, jnp.int32), starts[BLOCK - WINDOW - 1 :: BLOCK]]
    )
    starts = starts.reshape(1, 1, seq_rows)

    def project(index, mine, other, kept):
        return project_block(
            index,
            place,
            mine,
            other,
            gain_full,
            proj_own,
            proj_got,
            down_full,
            up_padded,
            query_part,
            kept,
        )

    kept = project(0, activations, inputs_other, ())
    kept = project(half_blocks, inputs_far, inputs_far_other, kept)
    normed_first, queries, keys_values, adapters, first_scale = kept
    keys_values = jnp.pad(keys_values, ((0, 0), (WINDOW, WINDOW)))
    mixed, inverse = attention_forward(
        marks, starts, queries, keys_values, query_map_own, key_map_own
    )

    mixed, grads_far = lax.optimization_barrier((mixed, grads_far))
    mixed_local = sequence_order(mixed, 1)
    mixed_pair = jnp.concatenate([mixed_local, swap(mixed_local, "col")], axis=0)
    adapter_sum = contract(mixed_pair, output_down_native, 0, 0)
    adapter_far = swap(other_half(adapter_sum, 0), "row")
    grads_far_other = swap(after(grads_far, mixed), "col")
    send_order = [(b + half_blocks) % blocks for b in range(blocks)]
    attended, attended_far = [None] * blocks, [None] * blocks
    pair = after(mixed_pair, grads_far)
    for b in send_order:
        attended[b] = contract(pair[:, rows_of(b)], output_native, 0, 0).astype(BF16)
        attended_far[send_order[b]] = swap(after(attended[b], adapter_far), "row")
        pair = after(pair, attended[b])
    out_adapter = (adapter_sum + adapter_far).astype(BF16)
    adapter_padded = jnp.pad(out_adapter, ((0, 0), (0, LANES - rank)))
    attended_other = [swap(attended[0], "col")] + [None] * (blocks - 1)
    d_hidden = hidden_grad(
        place,
        [after(grad_out, *attended, adapter_padded), grads_other, grads_far, grads_far_other],
        down_weight,
        mlp_down_got,
    )

    clock = (d_hidden,)
    kept, state = (), None
    for b in range(blocks):
        far = after(attended_far[b], *clock)
        far_other = swap(far, "col")
        if b + 1 < blocks:
            attended_other[b + 1] = swap(after(attended[b + 1], far), "col")
        inputs = (
            (activations, inputs_other)
            if b < half_blocks
            else (inputs_far, inputs_far_other)
        )
        outs = mlp_block(
            b,
            place,
            inputs,
            b % half_blocks,
            (attended[b], attended_other[b], far, far_other),
            adapter_padded,
            output_up_full,
            second_gain_full,
            gate_weight,
            gate_got,
            up_weight,
            up_got,
            d_hidden,
            kept,
            state,
            b < half_blocks,
        )
        kept = outs[:5]
        state = outs[5] if b < half_blocks else state
        clock = (kept[0],)
    hidden, d_gate, d_up, second_normed, second_scale = kept

    sums = {}

    def reduction(name, pair, which):
        sums[name] = Reduction(*pair, size, which)

    def given(pair, clock):
        return [swap(after(values, *clock), "col") for values in pair]

    def settle(clock, *names):
        for name in names:
            sums[name].got = after(sums[name].got, *clock)
            clock = (sums[name].combine(),)
        return clock

    def scattered(values):
        return lax.psum_scatter(values, "dp", scatter_dimension=0, tiled=True).astype(F32)

    natural = jnp.stack(
        [jnp.asarray(v, jnp.int32) for v in [col, row] + 2 * list(range(lane_blocks))]
    )
    both = [([second_normed], 0), ([second_normed], lane_blocks)]
    own_gate, other_gate = weight_grad(natural, both, d_gate, 1)
    grad_gate_own = scattered(own_gate)
    got_gate = swap(other_gate, "col")
    own_down, other_down = grads_of(
        [([grad_out, grads_far], 0), ([grads_other, grads_far_other], 0)],
        after(hidden, own_gate, got_gate),
        (order, turned_order),
    )
    reduction("down_own", own_down, order)
    down_given = given(other_down, ())

    def half_second(index, *clock):
        own, other = second_grad(
            index, place, after(d_gate, *clock), d_up, gate_weight, gate_got, up_weight, up_got
        )
        got = swap(other, "col")
        return (own.astype(F32) + got.astype(F32)).astype(BF16)

    chip_far = half_second(1, own_down[0])
    reduction("down_got", [after(v, chip_far) for v in down_given], turned_order)
    far_got_own = swap(chip_far, "row")
    chip_own = half_second(0, chip_far)
    far_got_far = swap(chip_own, "row")
    grad_gate_got = scattered(after(got_gate, chip_own))
    own_up, other_up = weight_grad(natural, both, after(d_up, chip_own), 1)
    got_up = swap(other_up, "col")
    y_own, y_other = down_product(place, after(hidden, own_up), down_weight, mlp_down_got)
    clock = settle((y_own,), "down_own", "down_got")

    y_got = swap(y_other, "col")
    totals = []
    for chip, got in ((chip_own, far_got_own), (chip_far, far_got_far)):
        total = (chip.astype(F32) + after(got, *clock).astype(F32)).astype(BF16)
        totals.append(total)
        clock = (total,)
    totals = [(total, swap(after(total, *clock), "col")) for total in totals]

    def back(index, grads, kept):
        return norm_back(
            index,
            place,
            totals[index],
            second_normed,
            second_scale,
            grads,
            second_gain_full,
            output_rows_own,
            output_got,
            output_up_full,
            output_down_padded,
            kept,
            index == 0,
        )

    outs = back(0, (grad_out, grads_other), ())
    kept, gain_sum, grad_state = outs[:3], outs[3], outs[4]
    grad_up_own = scattered(after(own_up, kept[0]))
    outs = back(1, (grads_far, grads_far_other), kept)
    kept = outs[:3]
    d_mixed, d_mine, d_out_padded = kept
    grad_second_gain = (gain_sum + outs[3])[0]
    d_out_adapter = d_out_padded[:, :rank]
    y_send = (y_own[half_rows:].astype(F32) + y_got[half_rows:].astype(F32)).astype(BF16)
    y_far = swap(y_send, "row")
    lefts = mixed_pair
    if not direct:
        lefts = relative_blocks(
            ordered(mixed_local, mixed_pair[query_part:], col, 0), 0, device, order
        )
    output_pair = weight_grad(
        places(order, rows_of_pair=True), [([lefts], 0)], after(d_mine, y_send), 2, True
    )
    reduction("output", output_pair, order)
    clock = (output_pair[0],)

    d_queries, d_keys, d_values, grad_query_map, grad_key_map = attention_backward(
        marks,
        starts,
        queries,
        keys_values,
        query_map_own,
        key_map_own,
        after(d_mixed, *clock),
        mixed,
        inverse,
    )
    clock = settle((d_queries,), "down_own", "down_got", "output")
    d_queries = after(d_queries, y_far, *clock)
    grad_up_got = scattered(after(got_up, d_queries))

    d_projected = sequence_order(
        jnp.concatenate(
            [
                d_queries,
                d_keys[:, WINDOW : WINDOW + seq_rows],
                d_values[:, WINDOW : WINDOW + seq_rows],
            ],
            axis=0,
        ),
        1,
    )
    d_pair = jnp.concatenate([d_projected, swap(d_projected, "col")], axis=0)
    adapter_sum = contract(up_native, d_pair, 1, 0)
    adapter_far = swap(other_half(adapter_sum, 1), "row")
    inverse_first = 1.0 / first_gain
    hat_near = normed_first[:half_rows, :feature_cols]
    hat_far = normed_first[half_rows:, :feature_cols]
    d_first_far = contract(d_pair[:, half_rows:], proj_native, 0, 1)
    gain_far = jnp.sum(d_first_far * hat_far.astype(F32), axis=0)
    d_first_far = swap(d_first_far.astype(BF16), "row")
    (proj_pair,) = grads_of([([normed_first], 0)], after(d_pair, gain_far), (order,), True)
    reduction("proj", proj_pair, order)
    d_adapter = (adapter_sum + after(adapter_far, proj_pair[0])).astype(BF16)
    d_first = contract(d_pair[:, :half_rows], proj_native, 0, 1) + contract(
        d_adapter[:, :half_rows], down_own, 0, 1
    )
    grad_first_gain = (
        gain_far + jnp.sum(d_first * hat_near.astype(F32), axis=0)
    ) * inverse_first
    grad_first_gain = grad_first_gain + swap(grad_first_gain, "row")
    clock = ()
    grad_down = contract(d_adapter, normed_first[:, :feature_cols], 1, 0)
    grad_up = contract(adapters[:, : 3 * rank], d_projected, 0, 1)
    grad_output_up = contract(out_adapter, d_mine, 0, 0)
    grad_output_down = contract(d_out_adapter, mixed_local, 0, 1)
    small = (
        grad_first_gain,
        grad_second_gain,
        grad_output_up,
        grad_down,
        grad_output_down,
        grad_up[:rank, :query_part],
        grad_up[rank : 2 * rank, query_part : query_part + key_part],
        grad_up[2 * rank :, query_part + key_part :],
        grad_query_map,
        grad_key_map,
    )
    flat = [values.reshape(-1, LANES) for values in small]
    packed = total_over(jnp.concatenate(flat, axis=0), size, bits)
    shared_rows = sum(values.shape[0] for values in flat[:4])
    packed_other = swap(packed[shared_rows:], "col")

    result = (
        state
        + (y_own[:half_rows].astype(F32) + y_got[:half_rows].astype(F32))
        + y_far.astype(F32)
    ).astype(BF16)
    d_first = d_first + after(d_first_far, d_first, result, *clock).astype(F32)
    first_scale = first_scale[:half_rows]
    hat_own = activations.astype(F32) * first_scale
    grad_hat = d_first * first_gain
    inner = jnp.sum(grad_hat * hat_own, axis=1)
    inner = ((inner + swap(inner, "col")) / width)[:, None]
    grad_activations = grad_state + first_scale * (
        grad_hat - hat_own * inner
    )
    clock = (grad_activations,)
    waiting = FINISH_ORDER
    while any(not sums[name].done for name in waiting):
        for name in waiting:
            if not sums[name].done:
                clock = settle(clock, name)

    def unpacked(index, source, base):
        first = sum(values.shape[0] for values in flat[:index]) - base
        return source[first : first + flat[index].shape[0]].reshape(small[index].shape)

    def joined(index, axis):
        return ordered(
            unpacked(index, packed, 0), unpacked(index, packed_other, shared_rows), col, axis
        )

    down_total = jnp.transpose(unpacked(3, packed, 0))
    grad_proj = sums["proj"].keep
    proj_grads = [
        ordered(
            grad_proj[:, first : first + count],
            grad_proj[:, part_cols + first : part_cols + first + count],
            col,
            1,
        )
        for first, count in (
            (0, query_part),
            (query_part, key_part),
            (query_part + key_part, key_part),
        )
    ]

    grad_gate = ordered(grad_gate_own, grad_gate_got, col, 1)
    grad_up_weight = ordered(grad_up_own, grad_up_got, col, 1)
    grad_down_weight = ordered(sums["down_own"].keep, sums["down_got"].keep, col, 1)
    return (
        result,
        grad_activations,
        unpacked(0, packed, 0),
        proj_grads[0],
        proj_grads[1],
        proj_grads[2],
        down_total[:, :rank],
        joined(5, 1),
        down_total[:, rank : 2 * rank],
        joined(6, 1),
        down_total[:, 2 * rank :],
        joined(7, 1),
        joined(8, 0),
        joined(9, 0),
        sums["output"].keep,
        jnp.transpose(joined(4, 1)),
        unpacked(2, packed, 0),
        unpacked(1, packed, 0),
        grad_gate,
        grad_up_weight,
        jnp.transpose(grad_down_weight),
    )


def solution(mesh):
    placed = (
        P(("dp", "row"), "col"),
        P(("dp", "row"), "col"),
        P("dp", None),
        P("col"),
        P("col", "row"),
        P("col", "row"),
        P("col", "row"),
        P("col", None),
        P(None, "row"),
        P("col", None),
        P(None, "row"),
        P("col", None),
        P(None, "row"),
        P("row", None, None),
        P("row", None, None),
        P("row", "col"),
        P("row", None),
        P(None, "col"),
        P("col"),
        P("col", "row"),
        P("col", "row"),
        P("row", "col"),
    )
    return jax.shard_map(
        on_device,
        mesh=mesh,
        in_specs=placed,
        out_specs=(
            P(("dp", "row"), "col"),
            P(("dp", "row"), "col"),
            P("col"),
            P(("col", "dp"), "row"),
            P(("col", "dp"), "row"),
            P(("col", "dp"), "row"),
            P("col", None),
            P(None, "row"),
            P("col", None),
            P(None, "row"),
            P("col", None),
            P(None, "row"),
            P("row", None, None),
            P("row", None, None),
            P(("row", "dp"), "col"),
            P("row", None),
            P(None, "col"),
            P("col"),
            P(("col", "dp"), "row"),
            P(("col", "dp"), "row"),
            P("row", ("col", "dp")),
        ),
        check_vma=False,
    )
```

time: 2790 us -> 837 us (0.30)
  waiting for transfers between devices: 1460 us -> 143 us
  matrix products: 592 us -> 36.6 us
  Pallas kernels: 0 us -> 447 us
  local copies, waits for them, and re-layouts: 456 us -> 47.5 us
  other arithmetic: 182 us -> 99.9 us
  blocking collectives: 50.8 us -> 0 us
  starting transfers between devices: 2.78 us -> 37.4 us
    reduce_scatter x18 -> x4, waiting for transfers between devices: 1030 us -> 0.03 us  [scattered(): lax.psum_scatter(values, 'dp', scatter_dimension=0, tiled=True).astype(F32)]
    dot_general x110 -> x13, matrix products: 592 us -> 36.6 us  [contract(): lax.dot_general(left, right, (((left_dim,), (right_dim,)), ((), ())), pre...]
    pallas_call x0 -> x20, Pallas kernels: none -> 447 us  [the longest x5 104 us: weight_grad(): grid_call(functools.partial(weight_grad_kernel, len(sets), chunks, pieces...]
    all_gather x8 -> x0, waiting for transfers between devices: 279 us -> none  [the longest x4 166 us: gather_rows(): return lax.all_gather(values, 'row', axis=0, tiled=True)]
    dynamic_update_slice x25 -> x0, local copies, waits for them, and re-layouts: 264 us -> none  [the longest x16 261 us: on_device(): lax.scan(backward_step, start_back, (block_indices, kept_states, kept_nor...]
    ppermute x0 -> x49, waiting for transfers between devices: none -> 143 us  [the longest x34 57.2 us: swap(): return lax.ppermute(values, axis, [(0, 1), (1, 0)])]
    psum x1 -> x0, waiting for transfers between devices: 139 us -> none  [on_device(): lax.psum((place_slot(grad_first_gain, 0, col_count, col_index), place_slo...]
    psum x5 -> x0, blocking collectives: 50.8 us -> none  [the longest x1 40.5 us: on_device(): lax.psum((place_slot(grad_first_gain, 0, col_count, col_index), place_slo...]
  transfers between devices with their start and end apart: 28 -> 53, of which waited for: 24 -> 21; matrix products, arithmetic and copies ran while one was open for 13% -> 20% of each run, Pallas kernels for 0% -> 42%
where the time goes in v1:
time: 837 us; the launch traced here: 827 us
  Pallas kernels  447 us (53%)
  waiting for transfers between devices  143 us (17%)
  other arithmetic  99.9 us (12%)
  local copies, waits for them, and re-layouts  47.5 us (6%)
  starting transfers between devices  37.4 us (4%)
  matrix products  36.6 us (4%)
  between operations  15.3 us (2%)
    pallas_call x5, Pallas kernels, weight_grad(): grid_call(functools.partial(weight_grad_kernel, len(sets), chunks, pieces...  104 us
    pallas_call x4, Pallas kernels, mlp_block(): grid_call(functools.partial(mlp_kernel, len(shapes)), 'mlp_block', (tiles...  80.4 us
    ppermute x34, waiting for transfers between devices, swap(): return lax.ppermute(values, axis, [(0, 1), (1, 0)])  57.2 us
    pallas_call x1, Pallas kernels, exchange(): pl.pallas_call(functools.partial(exchange_kernel, query_cols, key_cols),...  52 us
    pallas_call x2, Pallas kernels, second_grad(): grid_call(second_grad_kernel, 'second_grad', (half // tile,), (jax.ShapeD...  50.3 us
    pallas_call x1, Pallas kernels, attention_backward(): pl.pallas_call(backward_kernel, out_shape=(jax.ShapeDtypeStruct(qt.shape,...  44.2 us
    ppermute x3, waiting for transfers between devices, total_over(): lax.ppermute(values, 'dp', [(i, i ^ 1 << k) for i in range(size)])  42.8 us
    ppermute x12, waiting for transfers between devices, launch(): lax.ppermute(send, 'dp', [(i, i ^ bit) for i in range(self.size)])  42.8 us
  transfers between devices with their start and end apart: 53, of which 21 were waited for; matrix products, arithmetic and copies ran while one was open for 20% of the time, Pallas kernels for 42%

profile of v1, /device:TPU:0, one launch (start us, length us, event | category | flops | bytes accessed | tf_op | source)
XLA Modules:
  0.0 826.8 jit_solution(15212652619021557325)
XLA Ops:
  12.0 52.0 %exchange.1 = (bf16[1024,1024]{1,0:T(8,128)(2,1)}, bf16[1024,1024]{1,0:T(8,128)(2,1)}, bf16[1024,1024]{1,0:T(8,128)(2,1)}, bf16[1024,1024]{1,0:T(8,128)(2,1)}, b...) custom-call(bf16[1024,1024]{1,0:T(8,128)(2,1)} %in_mine.3, ...), custom_call_target="tpu_custom_call" | custom-call | flops 1000 | bytes 1000 | tf_op jit(solution)/shard_map/exchange/pallas_call | solution.py:520
  74.0 10.5 %project_block.2 = (bf16[2048,2048]{1,0:T(8,128)(2,1)}, bf16[512,2048]{1,0:T(8,128)(2,1)}, bf16[256,2048]{1,0:T(8,128)(2,1)}, bf16[2048,128]{1,0:T(8,128)(2,1)}, f32[2048,1]{1,0:T(8,128)}) custom-call(s32[10]{0:T(128)} %stack.54.place_ref, bf16[1024,1024]{1,0:T(8,128)(2,1)} %in_mine.3, bf16[1024,1024]{1,0:T(8,128)(2,1)} %get-tuple-element.157.other_ref.in_other, ...), custom_call_target="tpu_custom_call" | custom-call | flops 1000 | bytes 1000 | tf_op jit(solution)/shard_map/project_block/pallas_call | solution.py:612
  84.7 10.7 %project_block.3 = (bf16[2048,2048]{1,0:T(8,128)(2,1)}, bf16[512,2048]{1,0:T(8,128)(2,1)}, bf16[256,2048]{1,0:T(8,128)(2,1)}, bf16[2048,128]{1,0:T(8,128)(2,1)}, f32[2048,1]{1,0:T(8,128)}) custom-call(s32[10]{0:T(128)} %stack.54.place_ref, ...), custom_call_target="tpu_custom_call", output_to_operand_aliasing={{0}: (8, {}), {1}: (9, {}), {2}: (10, {}), {3}: (11, {}), {... | custom-call | flops 1000 | bytes 1000 | tf_op jit(solution)/shard_map/project_block/pallas_call | solution.py:612
  102.4 19.4 %attention_forward.1 = (bf16[512,2048]{1,0:T(8,128)(2,1)S(1)}, f32[2,4,2048]{2,1,0:T(4,128)S(1)}) custom-call(s32[5]{0:T(128)S(1)} %pad_add_fusion.mark_ref, s32[1,1,2048]{2,1,0:T(1,128)S(1)} %bitcast.52, bf16[512,2048]{1,0:T(8,128)(2,1)S(1)} %copy-done.1, bf16[256,2176]{1,0:T(8,128)(2,1)S(1)} %pad.28.kt_ref.vt_ref, ...), custom_call_target="tpu_custom_call" | custom-call | flops 1000 | bytes 1000 | tf_op jit(solution)/shard_map/attention_forward/pallas_call | solution.py:279
  124.3 5.4 collective-permute-done.1
  149.0 24.5 %hidden_grad.1.dh_ref = bf16[2048,2048]{1,0:T(8,128)(2,1)} custom-call(s32[10]{0:T(128)} %stack.54.place_ref, bf16[1024,1024]{1,0:T(8,128)(2,1)} %grad_mine.1, bf16[1024,1024]{1,0:T(8,128)(2,1)} %get-tuple-element.184.go_own.refs_16_.refs_18_.refs_20_.refs_22_.refs_24_.refs_26_.refs_28_.refs_30_.grad_other, ...), custom_call_target="tpu_custom_call" | custom-call | flops 1000 | bytes 1000 | tf_op jit(solution)/shard_map/hidden_grad/pallas_call | solution.py:555
  177.7 19.8 %mlp_block.4 = (bf16[2048,2048]{1,0:T(8,128)(2,1)}, bf16[2048,2048]{1,0:T(8,128)(2,1)}, bf16[2048,2048]{1,0:T(8,128)(2,1)}, bf16[2048,2048]{1,0:T(8,128)(2,1)}, f32[2048,1]{1,0:T(8,128)}, /*index=5*/f32[1024,1024]{1,0:T(8,128)}) custom-call(s32[10]{0:T(128)} %stack.54.place_ref, bf16[1024,1024]{1,0:T(8,128)(2,1)} %in_mine.3, ...), custom_call_target="tpu_custom_call" | custom-call | flops 1000 | bytes 1000 | tf_op jit(solution)/shard_map/mlp_block/pallas_call | solution.py:739
  203.0 21.2 %mlp_block.5 = (bf16[2048,2048]{1,0:T(8,128)(2,1)}, bf16[2048,2048]{1,0:T(8,128)(2,1)}, bf16[2048,2048]{1,0:T(8,128)(2,1)}, bf16[2048,2048]{1,0:T(8,128)(2,1)}, f32[2048,1]{1,0:T(8,128)}, /*index=5*/f32[1024,1024]{1,0:T(8,128)}) custom-call(s32[10]{0:T(128)} %stack.54.place_ref, ...), custom_call_target="tpu_custom_call", output_to_operand_aliasing={{0}: (15, {}), {1}: (16, {}), {2}: (17, {}), {3}: (18, {}),... | custom-call | flops 1000 | bytes 1000 | tf_op jit(solution)/shard_map/mlp_block/pallas_call | solution.py:739
  228.7 19.5 %mlp_block.6 = (bf16[2048,2048]{1,0:T(8,128)(2,1)}, bf16[2048,2048]{1,0:T(8,128)(2,1)}, bf16[2048,2048]{1,0:T(8,128)(2,1)}, bf16[2048,2048]{1,0:T(8,128)(2,1)}, f32[2048,1]{1,0:T(8,128)}) custom-call(s32[10]{0:T(128)} %stack.54.place_ref, ...), custom_call_target="tpu_custom_call", output_to_operand_aliasing={{0}: (15, {}), {1}: (16, {}), {2}: (17, {}), {3}: (18, {}),... | custom-call | flops 1000 | bytes 1000 | tf_op jit(solution)/shard_map/mlp_block/pallas_call | solution.py:739
  253.5 19.9 %mlp_block.7 = (bf16[2048,2048]{1,0:T(8,128)(2,1)}, bf16[2048,2048]{1,0:T(8,128)(2,1)}, bf16[2048,2048]{1,0:T(8,128)(2,1)}, bf16[2048,2048]{1,0:T(8,128)(2,1)}, f32[2048,1]{1,0:T(8,128)}) custom-call(s32[10]{0:T(128)} %stack.54.place_ref, ...), custom_call_target="tpu_custom_call", output_to_operand_aliasing={{0}: (15, {}), {1}: (16, {}), {2}: (17, {}), {3}: (18, {}),... | custom-call | flops 1000 | bytes 1000 | tf_op jit(solution)/shard_map/mlp_block/pallas_call | solution.py:739
  273.4 26.6 %weight_grad.5 = (bf16[1024,2048]{1,0:T(8,128)(2,1)}, bf16[1024,2048]{1,0:T(8,128)(2,1)}) custom-call(s32[18]{0:T(128)} %stack.110.place_ref, bf16[2048,2048]{1,0:T(8,128)(2,1)} %get-tuple-element.219.refs_0_.refs_1_.refs_2_.refs_3_.refs_4_.refs_5_.refs_6_.refs_7_.refs_8_.refs_9_.refs_10_.refs_11_.refs_12_.refs_13_.refs_14_.refs_15_.normed_ref, ...), custom_call_target="tpu_custom_call" | custom-call | flops 1000 | bytes 1000 | tf_op jit(solution)/shard_map/weight_grad/pallas_call | solution.py:964
  300.9 6.7 collective-permute-done.16
  307.5 27.4 %weight_grad.6 = (bf16[512,2048]{1,0:T(8,128)(2,1)}, bf16[512,2048]{1,0:T(8,128)(2,1)}, bf16[512,2048]{1,0:T(8,128)(2,1)}, bf16[512,2048]{1,0:T(8,128)(2,1)}) custom-call(s32[18]{0:T(128)} %stack.111.place_ref, bf16[1024,1024]{1,0:T(8,128)(2,1)} %grad_mine.1, ...), custom_call_target="tpu_custom_call" | custom-call | flops 1000 | bytes 1000 | tf_op jit(solution)/shard_map/weight_grad/pallas_call | solution.py:964
  335.0 25.1 %second_grad.2 = (bf16[1024,1024]{1,0:T(8,128)(2,1)}, bf16[1024,1024]{1,0:T(8,128)(2,1)}) custom-call(s32[10]{0:T(128)} %stack.54.place_ref, bf16[2048,2048]{1,0:T(8,128)(2,1)} %get-tuple-element.229.refs_16_.dg_ref, bf16[2048,2048]{1,0:T(8,128)(2,1)} %get-tuple-element.232.du_ref.refs_16_, bf16[1024,4096]{1,0:T(8,128)(2,1)} %gate_own.11, ...), custom_call_target="tpu_custom_call" | custom-call | flops 1000 | bytes 1000 | tf_op jit(solution)/shard_map/second_grad/pallas_call | solution.py:876
  360.1 4.2 collective-permute-done.17
  366.9 25.2 %second_grad.3 = (bf16[1024,1024]{1,0:T(8,128)(2,1)}, bf16[1024,1024]{1,0:T(8,128)(2,1)}) custom-call(s32[10]{0:T(128)} %stack.54.place_ref, bf16[2048,2048]{1,0:T(8,128)(2,1)} %get-tuple-element.229.refs_16_.dg_ref, bf16[2048,2048]{1,0:T(8,128)(2,1)} %get-tuple-element.232.du_ref.refs_16_, bf16[1024,4096]{1,0:T(8,128)(2,1)} %gate_own.11, ...), custom_call_target="tpu_custom_call" | custom-call | flops 1000 | bytes 1000 | tf_op jit(solution)/shard_map/second_grad/pallas_call | solution.py:876
  392.3 4.2 collective-permute-done.18
  396.6 3.9 add_convert_fusion.4
  408.7 27.0 %weight_grad.7 = (bf16[1024,2048]{1,0:T(8,128)(2,1)}, bf16[1024,2048]{1,0:T(8,128)(2,1)}) custom-call(s32[18]{0:T(128)} %stack.110.place_ref, bf16[2048,2048]{1,0:T(8,128)(2,1)} %get-tuple-element.219.refs_0_.refs_1_.refs_2_.refs_3_.refs_4_.refs_5_.refs_6_.refs_7_.refs_8_.refs_9_.refs_10_.refs_11_.refs_12_.refs_13_.refs_14_.refs_15_.normed_ref, ...), custom_call_target="tpu_custom_call" | custom-call | flops 1000 | bytes 1000 | tf_op jit(solution)/shard_map/weight_grad/pallas_call | solution.py:964
  435.7 24.8 %down_product.1 = (bf16[2048,1024]{1,0:T(8,128)(2,1)}, bf16[2048,1024]{1,0:T(8,128)(2,1)}) custom-call(s32[10]{0:T(128)} %stack.54.place_ref, bf16[2048,2048]{1,0:T(8,128)(2,1)} %get-tuple-element.234.refs_32_.hidden_ref, bf16[4096,1024]{1,0:T(8,128)(2,1)} %down_own.3, bf16[2048,1024]{1,0:T(8,128)(2,1)} %get-tuple-element.186.down_got), custom_call_target="tpu_custom_call" | custom-call | flops 1000 | bytes 1000 | tf_op jit(solution)/shard_map/down_product/pallas_call | solution.py:896
  460.5 3.8 add_convert_fusion.6
  464.3 22.4 %collective-permute-done.24 = bf16[512,2048]{1,0:T(8,128)(2,1)} collective-permute-done((bf16[512,2048]{1,0:T(8,128)(2,1)}, bf16[512,2048]{1,0:T(8,128)(2,1)}, u32[]{:S(2)}, u32[]{:S(2)}) %collective-permute-start.24) | collective-permute-done | bytes 2097184 | tf_op jit(solution)/shard_map/ppermute | solution.py:1018
  486.8 4.6 add_convert_fusion.7
  491.4 3.9 add_convert_fusion.1.total_mine
  495.3 3.8 collective-permute-done.26
  499.1 3.9 add_convert_fusion.total_mine
  511.7 13.8 %norm_back.2 = (bf16[512,2048]{1,0:T(8,128)(2,1)}, bf16[2048,1024]{1,0:T(8,128)(2,1)}, bf16[2048,128]{1,0:T(8,128)(2,1)}, f32[1,1024]{1,0:T(1,128)}, f32[1024,1024]{1,0:T(8,128)}) custom-call(s32[10]{0:T(128)} %stack.54.place_ref, bf16[1024,1024]{1,0:T(8,128)(2,1)} %add_convert_fusion.1.total_mine, bf16[1024,1024]{1,0:T(8,128)(2,1)} %copy-done.33, ...), custom_call_target="tpu_custom_call" | custom-call | flops 1000 | bytes 1000 | tf_op jit(solution)/shard_map/norm_back/pallas_call | solution.py:844
  527.7 4.5 add_convert_fusion.3
  536.9 12.8 %norm_back.3 = (bf16[512,2048]{1,0:T(8,128)(2,1)}, bf16[2048,1024]{1,0:T(8,128)(2,1)}, bf16[2048,128]{1,0:T(8,128)(2,1)}, f32[1,1024]{1,0:T(1,128)}) custom-call(s32[10]{0:T(128)} %stack.54.place_ref, bf16[1024,1024]{1,0:T(8,128)(2,1)} %add_convert_fusion.total_mine, ...), custom_call_target="tpu_custom_call", output_to_operand_aliasing={{0}: (12, {}), {1}: (13, {}), {2}: (14, {})} | custom-call | flops 1000 | bytes 1000 | tf_op jit(solution)/shard_map/norm_back/pallas_call | solution.py:844
  549.8 9.5 %weight_grad.8 = (bf16[512,1024]{1,0:T(8,128)(2,1)}, bf16[512,1024]{1,0:T(8,128)(2,1)}) custom-call(s32[10]{0:T(128)} %stack.120.place_ref, bf16[1024,2048]{1,0:T(8,128)(2,1)} %copy-done.10, bf16[1024,2048]{1,0:T(8,128)(2,1)} %copy-done.10, bf16[1024,2048]{1,0:T(8,128)(2,1)} %copy-done.10, bf16[1024,2048]{1,0:T(8,128)(2,1)} %copy-done.10, ...), custom_call_target="tpu_custom_call" | custom-call | flops 1000 | bytes 1000 | tf_op jit(solution)/shard_map/weight_grad/pallas_call | solution.py:964
  560.8 44.2 %attention_backward.1 = (bf16[512,2048]{1,0:T(8,128)(2,1)S(1)}, bf16[128,2176]{1,0:T(8,128)(2,1)S(1)}, bf16[128,2176]{1,0:T(8,128)(2,1)S(1)}, f32[8,64,64]{2,1,0:T(8,128)S(1)}, f32[2,64,64]{2,1,0:T(8,128)S(1)}) custom-call(s32[5]{0:T(128)S(1)} %copy-done.9, s32[1,1,2048]{2,1,0:T(1,128)S(1)} %bitcast.53, bf16[512,2048]{1,0:T(8,128)(2,1)} %get-tuple-element.171.qt_ref, ...), custom_call_target="tpu_custom_call" | custom-call | flops 1000 | bytes 1000 | tf_op jit(solution)/shard_map/attention_backward/pallas_call | solution.py:319
  612.8 5.6 maximum_select_fusion
  620.4 3.0 fusion.98
  633.7 7.1 add_convert_fusion.2
  643.0 3.7 fusion.42
  647.7 6.1 fusion.86
  655.0 6.6 pad_maximum_fusion.refs_8_
  661.6 13.0 %weight_grad.9 = (bf16[512,1536]{1,0:T(8,128)(2,1)}, bf16[512,1536]{1,0:T(8,128)(2,1)}) custom-call(s32[10]{0:T(128)} %stack.54.place_ref, bf16[2048,2048]{1,0:T(8,128)(2,1)} %get-tuple-element.270.refs_0_.refs_1_.refs_2_.refs_3_.refs_4_.refs_5_.refs_6_.refs_7_, ...), custom_call_target="tpu_custom_call" | custom-call | flops 1000 | bytes 1000 | tf_op jit(solution)/shard_map/weight_grad/pallas_call | solution.py:964
  677.0 5.3 fusion.9
  682.4 18.4 %collective-permute-done.34 = bf16[1024,1024]{1,0:T(8,128)(2,1)S(1)} collective-permute-done((bf16[1024,1024]{1,0:T(8,128)(2,1)S(1)}, bf16[1024,1024]{1,0:T(8,128)(2,1)S(1)}, u32[]{:S(2)}, u32[]{:S(2)}) %collective-permute-start.34) | collective-permute-done | bytes 2097184 | tf_op jit(solution)/shard_map/ppermute | solution.py:980
  700.8 4.3 multiply_reduce_fusion
  706.5 3.0 fusion
  714.8 6.3 multiply_add_fusion
  725.7 3.0 add_convert_fusion.10
  737.2 16.9 %collective-permute-done.45 = bf16[128,1024]{1,0:T(8,128)(2,1)} collective-permute-done((bf16[128,1024]{1,0:T(8,128)(2,1)}, bf16[128,1024]{1,0:T(8,128)(2,1)}, u32[]{:S(2)}, u32[]{:S(2)}) %collective-permute-start.45) | collective-permute-done | bytes 262176 | tf_op jit(solution)/shard_map/ppermute | solution.py:1018
  755.8 22.0 %collective-permute-done.38 = f32[672,128]{1,0:T(8,128)} collective-permute-done((f32[672,128]{1,0:T(8,128)S(1)}, f32[672,128]{1,0:T(8,128)}, u32[]{:S(2)}, u32[]{:S(2)}) %collective-permute-start.38) | collective-permute-done | bytes 344096 | tf_op jit(solution)/shard_map/ppermute | solution.py:1042
  783.3 20.5 %collective-permute-done.39 = f32[672,128]{1,0:T(8,128)S(1)} collective-permute-done((f32[672,128]{1,0:T(8,128)S(1)}, f32[672,128]{1,0:T(8,128)S(1)}, u32[]{:S(2)}, u32[]{:S(2)}) %collective-permute-start.39) | collective-permute-done | bytes 344096 | tf_op jit(solution)/shard_map/ppermute | solution.py:1042
  807.3 3.4 collective-permute-done.46
  (405 shorter events, 157.8 us)
Async XLA Ops:
  7.2 611.9 %reduce-scatter.5.cloned.1.call-start = ((), (), s32[]{:S(2)}) async-start(), calls=%async_computation.4 | async-start | bytes 4718592 | tf_op jit(solution)/shard_map/reduce_scatter | solution.py:1305
  64.0 58.5 %collective-permute-start = (bf16[1024,1024]{1,0:T(8,128)(2,1)}, bf16[1024,1024]{1,0:T(8,128)(2,1)}, u32[]{:S(2)}, u32[]{:S(2)}) collective-permute-start(bf16[1024,1024]{1,0:T(8,128)(2,1)} %grad_mine.1), channel_id=1, source_target_pairs={{0,2},{2,0},{1,3},{3,1},{4,6},{6,4},{5,7},{7,5},{8,10},{10,8},{9,1... | collective-permute-start | bytes 6291464 | tf_op jit(solution)/shard_map/ppermute | solution.py:980
  123.8 5.9 collective-permute-start.1
  123.9 23.7 %collective-permute-start.4 = (bf16[1024,1024]{1,0:T(8,128)(2,1)}, bf16[1024,1024]{1,0:T(8,128)(2,1)S(1)}, u32[]{:S(2)}, u32[]{:S(2)}) collective-permute-start(bf16[1024,1024]{1,0:T(8,128)(2,1)} %collective-permute-done.gm_far.refs_1_.refs_3_.refs_5_.refs_7_.refs_9_.refs_11_.refs_13_.refs_15_.grad_mine), channel_id=1, source_target_pairs={{0,1},{1,0},{2,3},{3,2},{4,5},{5,4},{6,7},{7,6},{8,9},{9,8},{10,11... | collective-permute-start | bytes 6291464 | tf_op jit(solution)/shard_map/ppermute | solution.py:980
  131.0 4.7 collective-permute-start.2
  135.7 37.8 %collective-permute-start.3 = (bf16[512,1024]{1,0:T(8,128)(2,1)}, bf16[512,1024]{1,0:T(8,128)(2,1)}, u32[]{:S(2)}, u32[]{:S(2)}) collective-permute-start(bf16[512,1024]{1,0:T(8,128)(2,1)} %convolution_convert_fusion.3.at_mine), channel_id=1, source_target_pairs={{0,2},{2,0},{1,3},{3,1},{4,6},{6,4},{5,7},{7,5},{8,10},{10,8},{9,1... | collective-permute-start | bytes 3145736 | tf_op jit(solution)/shard_map/ppermute | solution.py:980
  141.0 35.7 %collective-permute-start.7 = (bf16[512,1024]{1,0:T(8,128)(2,1)}, bf16[512,1024]{1,0:T(8,128)(2,1)}, u32[]{:S(2)}, u32[]{:S(2)}) collective-permute-start(bf16[512,1024]{1,0:T(8,128)(2,1)} %convolution_convert_fusion.1.at_mine), channel_id=1, source_target_pairs={{0,1},{1,0},{2,3},{3,2},{4,5},{5,4},{6,7},{7,6},{8,9},{9,8},{10,11... | collective-permute-start | bytes 3145736 | tf_op jit(solution)/shard_map/ppermute | solution.py:980
  174.0 25.3 %collective-permute-start.6 = (bf16[512,1024]{1,0:T(8,128)(2,1)}, bf16[512,1024]{1,0:T(8,128)(2,1)S(1)}, u32[]{:S(2)}, u32[]{:S(2)}) collective-permute-start(bf16[512,1024]{1,0:T(8,128)(2,1)} %convolution_convert_fusion.2.at_mine), channel_id=1, source_target_pairs={{0,2},{2,0},{1,3},{3,1},{4,6},{6,4},{5,7},{7,5},{8,10},{10,8},{9,1... | collective-permute-start | bytes 3145736 | tf_op jit(solution)/shard_map/ppermute | solution.py:980
  176.7 24.1 %collective-permute-start.5 = (bf16[512,1024]{1,0:T(8,128)(2,1)S(1)}, bf16[512,1024]{1,0:T(8,128)(2,1)S(1)}, u32[]{:S(2)}, u32[]{:S(2)}) collective-permute-start(bf16[512,1024]{1,0:T(8,128)(2,1)S(1)} %copy-done.20), channel_id=1, source_target_pairs={{0,1},{1,0},{2,3},{3,2},{4,5},{5,4},{6,7},{7,6},{8,9},{9,8},{10,11... | collective-permute-start | bytes 3145736 | tf_op jit(solution)/shard_map/ppermute | solution.py:980
  199.3 25.8 %collective-permute-start.10 = (bf16[512,1024]{1,0:T(8,128)(2,1)}, bf16[512,1024]{1,0:T(8,128)(2,1)S(1)}, u32[]{:S(2)}, u32[]{:S(2)}) collective-permute-start(bf16[512,1024]{1,0:T(8,128)(2,1)} %convolution_convert_fusion.1.at_mine), channel_id=1, source_target_pairs={{0,2},{2,0},{1,3},{3,1},{4,6},{6,4},{5,7},{7,5},{8,10},{10,8},{9,1... | collective-permute-start | bytes 3145736 | tf_op jit(solution)/shard_map/ppermute | solution.py:980
  200.6 26.0 %collective-permute-start.13 = (bf16[512,1024]{1,0:T(8,128)(2,1)}, bf16[512,1024]{1,0:T(8,128)(2,1)S(1)}, u32[]{:S(2)}, u32[]{:S(2)}) collective-permute-start(bf16[512,1024]{1,0:T(8,128)(2,1)} %convolution_convert_fusion.3.at_mine), channel_id=1, source_target_pairs={{0,1},{1,0},{2,3},{3,2},{4,5},{5,4},{6,7},{7,6},{8,9},{9,8},{10,11... | collective-permute-start | bytes 3145736 | tf_op jit(solution)/shard_map/ppermute | solution.py:980
  225.1 25.6 %collective-permute-start.12 = (bf16[512,1024]{1,0:T(8,128)(2,1)S(1)}, bf16[512,1024]{1,0:T(8,128)(2,1)S(1)}, u32[]{:S(2)}, u32[]{:S(2)}) collective-permute-start(bf16[512,1024]{1,0:T(8,128)(2,1)S(1)} %copy-done.21), channel_id=1, source_target_pairs={{0,2},{2,0},{1,3},{3,1},{4,6},{6,4},{5,7},{7,5},{8,10},{10,8},{9,1... | collective-permute-start | bytes 3145736 | tf_op jit(solution)/shard_map/ppermute | solution.py:980
  226.4 25.0 %collective-permute-start.11 = (bf16[512,1024]{1,0:T(8,128)(2,1)}, bf16[512,1024]{1,0:T(8,128)(2,1)S(1)}, u32[]{:S(2)}, u32[]{:S(2)}) collective-permute-start(bf16[512,1024]{1,0:T(8,128)(2,1)} %convolution_convert_fusion.2.at_mine), channel_id=1, source_target_pairs={{0,1},{1,0},{2,3},{3,2},{4,5},{5,4},{6,7},{7,6},{8,9},{9,8},{10,11... | collective-permute-start | bytes 3145736 | tf_op jit(solution)/shard_map/ppermute | solution.py:980
  300.0 7.5 collective-permute-start.16
  300.2 340.6 %reduce-scatter.7.cloned.1.call-start = ((), (), s32[]{:S(2)}) async-start(), calls=%async_computation.5 | async-start | bytes 4718592 | tf_op jit(solution)/shard_map/reduce_scatter | solution.py:1305
  360.0 4.4 collective-permute-start.17
  392.2 4.4 collective-permute-start.18
  400.5 405.6 %reduce-scatter.9.cloned.1.call-start = ((), (), s32[]{:S(2)}) async-start(), calls=%async_computation.6 | async-start | bytes 4718592 | tf_op jit(solution)/shard_map/reduce_scatter | solution.py:1305
  400.5 4.6 collective-permute-start.23
  400.7 7.9 collective-permute-start.22
  401.1 59.4 %collective-permute-start.25 = (bf16[512,2048]{1,0:T(8,128)(2,1)}, bf16[512,2048]{1,0:T(8,128)(2,1)}, u32[]{:S(2)}, u32[]{:S(2)}) collective-permute-start(bf16[512,2048]{1,0:T(8,128)(2,1)} %get-tuple-element.241), channel_id=1, source_target_pairs={{0,4},{4,0},{8,12},{12,8},{16,20},{20,16},{24,28},{28,24},{1,5},{5... | collective-permute-start | bytes 6291464 | tf_op jit(solution)/shard_map/ppermute | solution.py:1018
  405.1 81.7 %collective-permute-start.24 = (bf16[512,2048]{1,0:T(8,128)(2,1)}, bf16[512,2048]{1,0:T(8,128)(2,1)}, u32[]{:S(2)}, u32[]{:S(2)}) collective-permute-start(bf16[512,2048]{1,0:T(8,128)(2,1)} %collective-permute-done.23), channel_id=1, source_target_pairs={{0,8},{4,12},{8,0},{12,4},{16,24},{20,28},{24,16},{28,20},{1,9},{5... | collective-permute-start | bytes 6291464 | tf_op jit(solution)/shard_map/ppermute | solution.py:1018
  406.6 84.7 %collective-permute-start.21 = (bf16[1024,1024]{1,0:T(8,128)(2,1)S(1)}, bf16[1024,1024]{1,0:T(8,128)(2,1)}, u32[]{:S(2)}, u32[]{:S(2)}) collective-permute-start(bf16[1024,1024]{1,0:T(8,128)(2,1)S(1)} %add_convert_fusion.5), channel_id=1, source_target_pairs={{0,2},{2,0},{1,3},{3,1},{4,6},{6,4},{5,7},{7,5},{8,10},{10,8},{9,1... | collective-permute-start | bytes 6291464 | tf_op jit(solution)/shard_map/ppermute | solution.py:980
  408.1 91.0 %collective-permute-start.26 = (bf16[1024,1024]{1,0:T(8,128)(2,1)}, bf16[1024,1024]{1,0:T(8,128)(2,1)}, u32[]{:S(2)}, u32[]{:S(2)}) collective-permute-start(bf16[1024,1024]{1,0:T(8,128)(2,1)} %add_convert_fusion.4), channel_id=1, source_target_pairs={{0,2},{2,0},{1,3},{3,1},{4,6},{6,4},{5,7},{7,5},{8,10},{10,8},{9,1... | collective-permute-start | bytes 6291464 | tf_op jit(solution)/shard_map/ppermute | solution.py:980
  503.0 7.3 collective-permute-start.27
  503.0 24.7 %collective-permute-start.19 = (bf16[2048,1024]{1,0:T(8,128)(2,1)}, bf16[2048,1024]{1,0:T(8,128)(2,1)}, u32[]{:S(2)}, u32[]{:S(2)}) collective-permute-start(bf16[2048,1024]{1,0:T(8,128)(2,1)} %get-tuple-element.236), channel_id=1, source_target_pairs={{0,1},{1,0},{2,3},{3,2},{4,5},{5,4},{6,7},{7,6},{8,9},{9,8},{10,11... | collective-permute-start | bytes 12582920 | tf_op jit(solution)/shard_map/ppermute | solution.py:980
  525.5 291.7 %reduce-scatter.11.cloned.1.call-start = ((), (), s32[]{:S(2)}) async-start(), calls=%async_computation.7 | async-start | bytes 4718592 | tf_op jit(solution)/shard_map/reduce_scatter | solution.py:1305
  527.1 9.8 %collective-permute-start.28 = (bf16[1024,1024]{1,0:T(8,128)(2,1)S(1)}, bf16[1024,1024]{1,0:T(8,128)(2,1)}, u32[]{:S(2)}, u32[]{:S(2)}) collective-permute-start(bf16[1024,1024]{1,0:T(8,128)(2,1)S(1)} %copy-done.18), channel_id=1, source_target_pairs={{0,1},{1,0},{2,3},{3,2},{4,5},{5,4},{6,7},{7,6},{8,9},{9,8},{10,11... | collective-permute-start | bytes 6291464 | tf_op jit(solution)/shard_map/ppermute | solution.py:980
  527.2 78.2 %collective-permute-start.31 = (bf16[256,2048]{1,0:T(8,128)(2,1)}, bf16[256,2048]{1,0:T(8,128)(2,1)}, u32[]{:S(2)}, u32[]{:S(2)}) collective-permute-start(bf16[256,2048]{1,0:T(8,128)(2,1)} %get-tuple-element.406), channel_id=1, source_target_pairs={{0,8},{4,12},{8,0},{12,4},{16,24},{20,28},{24,16},{28,20},{1,9},{5... | collective-permute-start | bytes 3145736 | tf_op jit(solution)/shard_map/ppermute | solution.py:1018
  532.2 79.8 %collective-permute-start.20 = (bf16[1024,1024]{1,0:T(8,128)(2,1)}, bf16[1024,1024]{1,0:T(8,128)(2,1)}, u32[]{:S(2)}, u32[]{:S(2)}) collective-permute-start(bf16[1024,1024]{1,0:T(8,128)(2,1)} %add_convert_fusion.3), channel_id=1, source_target_pairs={{0,2},{2,0},{1,3},{3,1},{4,6},{6,4},{5,7},{7,5},{8,10},{10,8},{9,1... | collective-permute-start | bytes 6291464 | tf_op jit(solution)/shard_map/ppermute | solution.py:980
  533.7 74.4 %collective-permute-start.30 = (bf16[256,2048]{1,0:T(8,128)(2,1)}, bf16[256,2048]{1,0:T(8,128)(2,1)}, u32[]{:S(2)}, u32[]{:S(2)}) collective-permute-start(bf16[256,2048]{1,0:T(8,128)(2,1)} %get-tuple-element.408), channel_id=1, source_target_pairs={{0,16},{4,20},{8,24},{12,28},{16,0},{20,4},{24,8},{28,12},{1,17},{... | collective-permute-start | bytes 3145736 | tf_op jit(solution)/shard_map/ppermute | solution.py:1018
  559.2 51.3 %collective-permute-start.29 = (bf16[512,1024]{1,0:T(8,128)(2,1)}, bf16[512,1024]{1,0:T(8,128)(2,1)S(1)}, u32[]{:S(2)}, u32[]{:S(2)}) collective-permute-start(bf16[512,1024]{1,0:T(8,128)(2,1)} %get-tuple-element.262), channel_id=1, source_target_pairs={{0,4},{4,0},{8,12},{12,8},{16,20},{20,16},{24,28},{28,24},{1,5},{5... | collective-permute-start | bytes 3145736 | tf_op jit(solution)/shard_map/ppermute | solution.py:1018
  560.7 72.8 %collective-permute-start.48 = (bf16[1024,2048]{1,0:T(8,128)(2,1)}, bf16[1024,2048]{1,0:T(8,128)(2,1)}, u32[]{:S(2)}, u32[]{:S(2)}) collective-permute-start(bf16[1024,2048]{1,0:T(8,128)(2,1)} %get-tuple-element.291), channel_id=1, source_target_pairs={{0,1},{1,0},{2,3},{3,2},{4,5},{5,4},{6,7},{7,6},{8,9},{9,8},{10,11... | collective-permute-start | bytes 12582920 | tf_op jit(solution)/shard_map/ppermute | solution.py:980
  618.4 24.5 %collective-permute-start.32 = (bf16[768,2048]{1,0:T(8,128)(2,1)}, bf16[768,2048]{1,0:T(8,128)(2,1)}, u32[]{:S(2)}, u32[]{:S(2)}) collective-permute-start(bf16[768,2048]{1,0:T(8,128)(2,1)} %maximum_select_fusion), channel_id=1, source_target_pairs={{0,1},{1,0},{2,3},{3,2},{4,5},{5,4},{6,7},{7,6},{8,9},{9,8},{10,11... | collective-permute-start | bytes 9437192 | tf_op jit(solution)/shard_map/ppermute | solution.py:980
  627.7 94.8 %collective-permute-start.42 = (bf16[128,2048]{1,0:T(8,128)(2,1)}, bf16[128,2048]{1,0:T(8,128)(2,1)}, u32[]{:S(2)}, u32[]{:S(2)}) collective-permute-start(bf16[128,2048]{1,0:T(8,128)(2,1)} %get-tuple-element.416), channel_id=1, source_target_pairs={{0,4},{4,0},{8,12},{12,8},{16,20},{20,16},{24,28},{28,24},{1,5},{5... | collective-permute-start | bytes 1572872 | tf_op jit(solution)/shard_map/ppermute | solution.py:1018
  628.2 92.9 %collective-permute-start.43 = (bf16[128,2048]{1,0:T(8,128)(2,1)}, bf16[128,2048]{1,0:T(8,128)(2,1)}, u32[]{:S(2)}, u32[]{:S(2)}) collective-permute-start(bf16[128,2048]{1,0:T(8,128)(2,1)} %get-tuple-element.414), channel_id=1, source_target_pairs={{0,16},{4,20},{8,24},{12,28},{16,0},{20,4},{24,8},{28,12},{1,17},{... | collective-permute-start | bytes 1572872 | tf_op jit(solution)/shard_map/ppermute | solution.py:1018
  628.5 95.2 %collective-permute-start.41 = (bf16[256,1024]{1,0:T(8,128)(2,1)}, bf16[256,1024]{1,0:T(8,128)(2,1)}, u32[]{:S(2)}, u32[]{:S(2)}) collective-permute-start(bf16[256,1024]{1,0:T(8,128)(2,1)} %get-tuple-element.418), channel_id=1, source_target_pairs={{0,8},{4,12},{8,0},{12,4},{16,24},{20,28},{24,16},{28,20},{1,9},{5... | collective-permute-start | bytes 1572872 | tf_op jit(solution)/shard_map/ppermute | solution.py:1018
  646.7 27.9 %collective-permute-start.33 = (f32[24,2048]{1,0:T(8,128)S(1)}, f32[24,2048]{1,0:T(8,128)S(1)}, u32[]{:S(2)}, u32[]{:S(2)}) collective-permute-start(f32[24,2048]{1,0:T(8,128)S(1)} %pad_maximum_fusion.3), channel_id=1, source_target_pairs={{0,2},{2,0},{1,3},{3,1},{4,6},{6,4},{5,7},{7,5},{8,10},{10,8},{9,1... | collective-permute-start | bytes 589832 | tf_op jit(solution)/shard_map/ppermute | solution.py:980
  653.8 47.0 %collective-permute-start.34 = (bf16[1024,1024]{1,0:T(8,128)(2,1)S(1)}, bf16[1024,1024]{1,0:T(8,128)(2,1)S(1)}, u32[]{:S(2)}, u32[]{:S(2)}) collective-permute-start(bf16[1024,1024]{1,0:T(8,128)(2,1)S(1)} %get-tuple-element.404), channel_id=1, source_target_pairs={{0,2},{2,0},{1,3},{3,1},{4,6},{6,4},{5,7},{7,5},{8,10},{10,8},{9,1... | collective-permute-start | bytes 6291464 | tf_op jit(solution)/shard_map/ppermute | solution.py:980
  674.6 51.1 %collective-permute-start.40 = (bf16[512,1536]{1,0:T(8,128)(2,1)}, bf16[512,1536]{1,0:T(8,128)(2,1)}, u32[]{:S(2)}, u32[]{:S(2)}) collective-permute-start(bf16[512,1536]{1,0:T(8,128)(2,1)} %get-tuple-element.281), channel_id=1, source_target_pairs={{0,4},{4,0},{8,12},{12,8},{16,20},{20,16},{24,28},{28,24},{1,5},{5... | collective-permute-start | bytes 4718600 | tf_op jit(solution)/shard_map/ppermute | solution.py:1018
  705.8 3.9 collective-permute-start.36
  713.3 20.6 %collective-permute-start.37 = (f32[672,128]{1,0:T(8,128)S(1)}, f32[672,128]{1,0:T(8,128)S(1)}, u32[]{:S(2)}, u32[]{:S(2)}) collective-permute-start(f32[672,128]{1,0:T(8,128)S(1)} %constant_dynamic-update-slice_fusion.3), channel_id=1, source_target_pairs={{0,4},{4,0},{8,12},{12,8},{16,20},{20,16},{24,28},{28,24},{1,5},{5... | collective-permute-start | bytes 1032200 | tf_op jit(solution)/shard_map/ppermute | solution.py:1042
  728.7 51.5 %collective-permute-start.44 = (bf16[256,1536]{1,0:T(8,128)(2,1)}, bf16[256,1536]{1,0:T(8,128)(2,1)}, u32[]{:S(2)}, u32[]{:S(2)}) collective-permute-start(bf16[256,1536]{1,0:T(8,128)(2,1)} %get-tuple-element.410), channel_id=1, source_target_pairs={{0,8},{4,12},{8,0},{12,4},{16,24},{20,28},{24,16},{28,20},{1,9},{5... | collective-permute-start | bytes 2359304 | tf_op jit(solution)/shard_map/ppermute | solution.py:1018
  730.9 23.1 %collective-permute-start.45 = (bf16[128,1024]{1,0:T(8,128)(2,1)}, bf16[128,1024]{1,0:T(8,128)(2,1)}, u32[]{:S(2)}, u32[]{:S(2)}) collective-permute-start(bf16[128,1024]{1,0:T(8,128)(2,1)} %get-tuple-element.424), channel_id=1, source_target_pairs={{0,16},{4,20},{8,24},{12,28},{16,0},{20,4},{24,8},{28,12},{1,17},{... | collective-permute-start | bytes 786440 | tf_op jit(solution)/shard_map/ppermute | solution.py:1018
  733.9 44.0 %collective-permute-start.38 = (f32[672,128]{1,0:T(8,128)S(1)}, f32[672,128]{1,0:T(8,128)}, u32[]{:S(2)}, u32[]{:S(2)}) collective-permute-start(f32[672,128]{1,0:T(8,128)S(1)} %add.270), channel_id=1, source_target_pairs={{0,8},{4,12},{8,0},{12,4},{16,24},{20,28},{24,16},{28,20},{1,9},{5... | collective-permute-start | bytes 1032200 | tf_op jit(solution)/shard_map/ppermute | solution.py:1042
  778.9 24.9 %collective-permute-start.39 = (f32[672,128]{1,0:T(8,128)S(1)}, f32[672,128]{1,0:T(8,128)S(1)}, u32[]{:S(2)}, u32[]{:S(2)}) collective-permute-start(f32[672,128]{1,0:T(8,128)S(1)} %add.271), channel_id=1, source_target_pairs={{0,16},{4,20},{8,24},{12,28},{16,0},{20,4},{24,8},{28,12},{1,17},{... | collective-permute-start | bytes 1032200 | tf_op jit(solution)/shard_map/ppermute | solution.py:1042
  781.5 29.2 %collective-permute-start.46 = (bf16[128,1536]{1,0:T(8,128)(2,1)S(1)}, bf16[128,1536]{1,0:T(8,128)(2,1)S(1)}, u32[]{:S(2)}, u32[]{:S(2)}) collective-permute-start(bf16[128,1536]{1,0:T(8,128)(2,1)S(1)} %get-tuple-element.423), channel_id=1, source_target_pairs={{0,16},{4,20},{8,24},{12,28},{16,0},{20,4},{24,8},{28,12},{1,17},{... | collective-permute-start | bytes 1179656 | tf_op jit(solution)/shard_map/ppermute | solution.py:1018
  803.9 9.1 %collective-permute-start.47 = (f32[400,128]{1,0:T(8,128)S(1)}, f32[400,128]{1,0:T(8,128)S(1)}, u32[]{:S(2)}, u32[]{:S(2)}) collective-permute-start(f32[400,128]{1,0:T(8,128)S(1)} %slice.398), channel_id=1, source_target_pairs={{0,1},{1,0},{2,3},{3,2},{4,5},{5,4},{6,7},{7,6},{8,9},{9,8},{10,11... | collective-permute-start | bytes 614408 | tf_op jit(solution)/shard_map/ppermute | solution.py:980
  (90 other events, 1161.7 us)
Sparse Core Ops, SparseCore 0:
  300.3 89.0 reduce-scatter.4
  400.6 122.6 reduce-scatter.6
  527.0 144.6 reduce-scatter.8
  675.6 103.9 reduce-scatter.10

commit v2 on v1

--- a/solution.py
+++ b/solution.py
@@ -17,7 +17,7 @@
 SUM_TILE = 256
 GRAD_TILE = 512
 VMEM_LIMIT = 56 * 1024 * 1024
-FINISH_ORDER = ("down_own", "down_got", "output", "proj")
+FINISH_ORDER = ("up_got", "output", "down_own", "down_got")
 norm_eps = 1e-05
 F32 = jnp.float32
 BF16 = jnp.bfloat16
@@ -246,15 +246,25 @@
     def _():
         key_probs = softmax_halves(dot_nn(kmap_ref[0], kt_ref[...]))
         dpre = halves_backward(key_probs, dkf_acc[...]).astype(BF16)
-        dk = dk_acc[...] * SCALE + dot_nn(kback_ref[0], dpre)
-        dkt_ref[...] = dk.astype(BF16)
-        dvt_ref[...] = dv_acc[...].astype(BF16)
+        dk = (dk_acc[...] * SCALE + dot_nn(kback_ref[0], dpre)).astype(BF16)
+        dv = dv_acc[...].astype(BF16)
+        half = dkt_ref.shape[1] // 2
+        flip = mark_ref[count + 1]
+        for i in range(2):
+            lanes = pl.ds(pl.multiple_of((i ^ flip) * half, half), half)
+            dkt_ref[:, lanes] = dk[:, WINDOW + i * half : WINDOW + (i + 1) * half]
+            dvt_ref[:, lanes] = dv[:, WINDOW + i * half : WINDOW + (i + 1) * half]
         gkm_ref[0] = dot_nt(kt_ref[...], dpre)
 
 
 def signed_maps(maps):
     turned = jnp.swapaxes(maps, 1, 2)
     return jnp.concatenate([turned, -turned], axis=1)
+
+
+def local_block(block, marks, blocks):
+    half = blocks // 2
+    return ((block // half) ^ marks[blocks + 1]) * half + block % half
 
 
 def attention_specs(groups, ratio, padded, block_of):
@@ -287,7 +297,7 @@
             grid=(groups, blocks),
             in_specs=attention_specs(groups, ratio, padded, lambda i: i),
             out_specs=[
-                pl.BlockSpec((rows, BLOCK), lambda g, i, *_: (g, i)),
+                pl.BlockSpec((rows, BLOCK), lambda g, i, s: (g, local_block(i, s, blocks))),
                 pl.BlockSpec((1, ratio, BLOCK), lambda g, i, *_: (g, 0, i)),
             ],
             scratch_shapes=[
@@ -315,13 +325,14 @@
     blocks = length // BLOCK
     back = lambda i: blocks - 1 - i
     query_spec = pl.BlockSpec((rows, BLOCK), lambda g, i, *_: (g, back(i)))
-    key_spec = pl.BlockSpec((HEAD_DIM, padded), lambda g, i, *_: (g, 0))
+    local_spec = pl.BlockSpec((rows, BLOCK), lambda g, i, s: (g, local_block(back(i), s, blocks)))
+    key_spec = pl.BlockSpec((HEAD_DIM, length), lambda g, i, *_: (g, 0))
     return pl.pallas_call(
         backward_kernel,
         out_shape=(
             jax.ShapeDtypeStruct(qt.shape, BF16),
-            jax.ShapeDtypeStruct((groups * HEAD_DIM, padded), BF16),
-            jax.ShapeDtypeStruct((groups * HEAD_DIM, padded), BF16),
+            jax.ShapeDtypeStruct((groups * HEAD_DIM, length), BF16),
+            jax.ShapeDtypeStruct((groups * HEAD_DIM, length), BF16),
             jax.ShapeDtypeStruct(qmap.shape, F32),
             jax.ShapeDtypeStruct(kmap.shape, F32),
         ),
@@ -331,13 +342,13 @@
             in_specs=attention_specs(groups, ratio, padded, back)
             + [
                 query_spec,
-                query_spec,
+                local_spec,
                 pl.BlockSpec((1, ratio, BLOCK), lambda g, i, *_: (g, 0, back(i))),
                 pl.BlockSpec((ratio, HEAD_DIM, HEAD_DIM), lambda g, i, *_: (g, 0, 0)),
                 pl.BlockSpec((1, HEAD_DIM, HEAD_DIM), lambda g, i, *_: (g, 0, 0)),
             ],
             out_specs=[
-                query_spec,
+                local_spec,
                 key_spec,
                 key_spec,
                 pl.BlockSpec((ratio, HEAD_DIM, HEAD_DIM), lambda g, i, *_: (g, 0, 0)),
@@ -393,40 +404,35 @@
 
 
 MESH = pl.DeviceIdType.MESH
-FAR_CHUNKS = 4
 
 
 def exchange_kernel(query_cols, key_cols, *refs):
     inputs, grads, query, key, value, gate, up, down, output = refs[:9]
-    thin = refs[9:15]
-    far, near_other, far_other, grads_other, proj_got, gate_got, up_got, down_got, output_got = (
-        refs[15:24]
-    )
-    thin_got = refs[24:30]
-    proj_own, proj_both, output_both = refs[30:33]
-    send_sem, recv_sem, local_sem, proj_all, output_all = refs[33:]
-    row, col = lax.axis_index("row"), lax.axis_index("col")
+    thin = refs[9:11]
+    near_other, grads_other, proj_got, gate_got, up_got, down_got, output_got = refs[11:18]
+    thin_got = refs[18:20]
+    proj_own, proj_both, output_both = refs[20:23]
+    send_sem, recv_sem, local_sem, proj_all, output_all = refs[23:]
+    col = lax.axis_index("col")
 
     barrier = pltpu.get_barrier_semaphore()
-    pl.semaphore_signal(barrier, inc=1, device_id={"row": 1 - row}, device_id_type=MESH)
     pl.semaphore_signal(barrier, inc=1, device_id={"col": 1 - col}, device_id_type=MESH)
-    pl.semaphore_wait(barrier, 2)
+    pl.semaphore_wait(barrier, 1)
 
     copies = []
 
-    def remote(source, target, axis, place):
+    def remote(source, target):
         n = len(copies)
         copy = pltpu.make_async_remote_copy(
             src_ref=source,
             dst_ref=target,
             send_sem=send_sem.at[n],
             recv_sem=recv_sem.at[n],
-            device_id={axis: 1 - place},
+            device_id={"col": 1 - col},
             device_id_type=MESH,
         )
         copy.start()
         copies.append(copy)
-        return copy
 
     def columns(ref, index, width):
         return ref.at[:, pl.ds(pl.multiple_of(index * width, width), width)]
@@ -434,23 +440,18 @@
     def rows_of(ref, index, height):
         return ref.at[pl.ds(pl.multiple_of(index * height, height), height), :]
 
-    size = inputs.shape[0] // FAR_CHUNKS
-    chunks = [pl.ds(i * size, size) for i in range(FAR_CHUNKS)]
-    arriving = [remote(inputs.at[at, :], far.at[at, :], "row", row) for at in chunks]
-    remote(inputs, near_other, "col", col)
+    remote(inputs, near_other)
     first = 0
     for weight, width in ((query, query_cols), (key, key_cols), (value, key_cols)):
-        remote(
-            columns(weight, 1 - col, width), proj_got.at[:, pl.ds(first, width)], "col", col
-        )
+        remote(columns(weight, 1 - col, width), proj_got.at[:, pl.ds(first, width)])
         first += width
     for source, target in zip(thin, thin_got):
-        remote(source, target, "col", col)
-    remote(columns(gate, 1 - col, gate_got.shape[1]), gate_got, "col", col)
-    remote(columns(up, 1 - col, up_got.shape[1]), up_got, "col", col)
-    remote(rows_of(down, 1 - col, down_got.shape[0]), down_got, "col", col)
-    remote(rows_of(output, 1 - col, output_got.shape[0]), output_got, "col", col)
-    remote(grads, grads_other, "col", col)
+        remote(source, target)
+    remote(columns(gate, 1 - col, gate_got.shape[1]), gate_got)
+    remote(columns(up, 1 - col, up_got.shape[1]), up_got)
+    remote(rows_of(down, 1 - col, down_got.shape[0]), down_got)
+    remote(rows_of(output, 1 - col, output_got.shape[0]), output_got)
+    remote(grads, grads_other)
 
     def local(source, target, n):
         copy = pltpu.make_async_copy(source, target, local_sem.at[n])
@@ -486,15 +487,10 @@
         local(output_all, output_both, 10),
     ]
 
-    for copy, at in zip(arriving, chunks):
-        copy.wait_recv()
-        remote(far.at[at, :], far_other.at[at, :], "col", col)
     for copy in stores:
         copy.wait()
-    for n, copy in enumerate(copies):
-        copy.wait_send()
-        if n >= FAR_CHUNKS:
-            copy.wait_recv()
+    for copy in copies:
+        copy.wait()
 
 
 def exchange(inputs, grads, projections, gate, up, down, output, thin):
@@ -504,8 +500,6 @@
     columns = query_cols + 2 * key_cols
     like = lambda *shape: jax.ShapeDtypeStruct(shape, BF16)
     outs = [
-        like(rows, half),
-        like(rows, half),
         like(rows, half),
         like(rows, half),
         like(half, columns),
@@ -516,7 +510,7 @@
     ]
     outs += [jax.ShapeDtypeStruct(values.shape, values.dtype) for values in thin]
     outs += [like(half, columns), like(half, 2 * columns), like(output.shape[0], half)]
-    copies = 2 * FAR_CHUNKS + 1 + 3 + len(thin) + 5
+    copies = 1 + 3 + len(thin) + 5
     return pl.pallas_call(
         functools.partial(exchange_kernel, query_cols, key_cols),
         out_shape=tuple(outs),
@@ -567,7 +561,17 @@
 
 
 def project_kernel(
-    place_ref, mine_ref, other_ref, gain_ref, proj_own, proj_got, down_ref, up_ref, *refs
+    place_ref,
+    mine_ref,
+    other_ref,
+    gain_ref,
+    gain_got_ref,
+    proj_own,
+    proj_got,
+    thin_ref,
+    thin_got_ref,
+    up_ref,
+    *refs,
 ):
     normed_ref, queries_ref, keys_ref, adapters_ref, scale_ref = refs[-5:]
     half = mine_ref.shape[1]
@@ -576,12 +580,12 @@
         other * other, axis=1, keepdims=True
     )
     scale = lax.rsqrt(squares / (2 * half) + norm_eps)
-    left = (mine * scale * gain_ref[:, :half]).astype(BF16)
-    right = (other * scale * gain_ref[:, half:]).astype(BF16)
+    left = (mine * scale * gain_ref[:1, :]).astype(BF16)
+    right = (other * scale * gain_got_ref[:1, :]).astype(BF16)
     normed_ref[:, :half] = left
     normed_ref[:, half:] = right
     scale_ref[...] = scale
-    adapters = (dot_nn(left, down_ref[:half]) + dot_nn(right, down_ref[half:])).astype(BF16)
+    adapters = (dot_nt(left, thin_ref[...]) + dot_nt(right, thin_got_ref[...])).astype(BF16)
     adapters_ref[...] = adapters
     sums = dot_nn(left, proj_own[...]) + dot_nn(right, proj_got[...]) + dot_nn(adapters, up_ref[...])
     turned = jnp.transpose(sums.astype(BF16))
@@ -594,7 +598,8 @@
     return ((local // half_blocks) ^ flip) * half_blocks + local % half_blocks
 
 
-def project_block(index, place, mine, other, gain, proj_own, proj_got, down, up, query_part, kept):
+def project_block(index, place, mine, other, gains, projections, thin, up, query_part, kept):
+    proj_own, proj_got = projections
     rows, half = mine.shape
     length = 2 * half_rows_of(kept, rows)
     blocks, half_blocks = length // BLOCK, length // BLOCK // 2
@@ -606,9 +611,10 @@
         jax.ShapeDtypeStruct((length, 2 * half), BF16),
         jax.ShapeDtypeStruct((query_part, length), BF16),
         jax.ShapeDtypeStruct((columns - query_part, length), BF16),
-        jax.ShapeDtypeStruct((length, LANES), BF16),
+        jax.ShapeDtypeStruct((length, up.shape[0]), BF16),
         jax.ShapeDtypeStruct((length, 1), F32),
     )
+    operands = (mine, other, *gains, proj_own, proj_got, *thin, up)
     return grid_call(
         project_kernel,
         "project_block",
@@ -617,22 +623,18 @@
         [
             pl.BlockSpec((BLOCK, half), lambda i, s: (i, 0)),
             pl.BlockSpec((BLOCK, half), lambda i, s: (i, 0)),
-            whole(gain),
-            whole(proj_own),
-            whole(proj_got),
-            whole(down),
-            whole(up),
         ]
+        + [whole(values) for values in operands[2:]]
         + [pl.BlockSpec(memory_space=pl.ANY)] * len(kept),
         [
             pl.BlockSpec((BLOCK, 2 * half), local),
             pl.BlockSpec((query_part, BLOCK), lanes),
             pl.BlockSpec((columns - query_part, BLOCK), lanes),
-            pl.BlockSpec((BLOCK, LANES), local),
+            pl.BlockSpec((BLOCK, up.shape[0]), local),
             pl.BlockSpec((BLOCK, 1), local),
         ],
-        aliases={8 + i: i for i in range(len(kept))},
-    )(place, mine, other, gain, proj_own, proj_got, down, up, *kept)
+        aliases={1 + len(operands) + i: i for i in range(len(kept))},
+    )(place, *operands, *kept)
 
 
 def half_rows_of(kept, rows):
@@ -854,57 +856,230 @@
     )(place, *totals, normed, scale, *grads, gain, out_own, out_got, up, down, *kept)
 
 
-def second_grad_kernel(
-    place_ref, dg_ref, du_ref, gate_own, gate_got, up_own, up_got, own_ref, other_ref
-):
-    own_ref[...] = (dot_nt(dg_ref[...], gate_own[...]) + dot_nt(du_ref[...], up_own[...])).astype(
-        BF16
-    )
-    other_ref[...] = (
-        dot_nt(dg_ref[...], gate_got[...]) + dot_nt(du_ref[...], up_got[...])
-    ).astype(BF16)
-
-
-def second_grad(index, place, d_gate, d_up, gate_weight, gate_got, up_weight, up_got):
+def pair_sum_kernel(products, *refs):
+    operands = refs[:-5]
+    out_ref, send_buf, recv_buf, send_sem, recv_sem = refs[-5:]
+    step = pl.program_id(0)
+    tiles = send_buf.shape[0]
+    col = lax.axis_index("col")
+
+    def copy(tile):
+        return pltpu.make_async_remote_copy(
+            src_ref=send_buf.at[tile],
+            dst_ref=recv_buf.at[tile],
+            send_sem=send_sem.at[tile],
+            recv_sem=recv_sem.at[tile],
+            device_id={"col": 1 - col},
+            device_id_type=MESH,
+        )
+
+    @pl.when(step == 0)
+    def _():
+        barrier = pltpu.get_barrier_semaphore()
+        pl.semaphore_signal(barrier, inc=1, device_id={"col": 1 - col}, device_id_type=MESH)
+        pl.semaphore_wait(barrier, 1)
+
+    @pl.when(step < tiles)
+    def _():
+        send_buf[step] = products(operands, False).astype(BF16)
+        copy(step).start()
+
+    @pl.when(step >= tiles)
+    def _():
+        tile = step - tiles
+        sums = products(operands, True)
+        copy(tile).wait_recv()
+        out_ref[...] = (sums + recv_buf[tile].astype(F32)).astype(BF16)
+
+    @pl.when(step == 2 * tiles - 1)
+    def _():
+        for tile in range(tiles):
+            copy(tile).wait_send()
+
+
+def pair_sum(products, name, collective, rows, half, in_specs, operands):
+    tile = min(SUM_TILE, half)
+    tiles = half // tile
+    return pl.pallas_call(
+        functools.partial(pair_sum_kernel, products),
+        grid=(2 * tiles,),
+        out_shape=jax.ShapeDtypeStruct((rows, half), BF16),
+        in_specs=in_specs,
+        out_specs=pl.BlockSpec((rows, tile), lambda i: (0, jnp.maximum(i - tiles, 0))),
+        scratch_shapes=[
+            pltpu.VMEM((tiles, rows, tile), BF16),
+            pltpu.VMEM((tiles, rows, tile), BF16),
+            pltpu.SemaphoreType.DMA((tiles,)),
+            pltpu.SemaphoreType.DMA((tiles,)),
+        ],
+        compiler_params=pltpu.CompilerParams(
+            dimension_semantics=("arbitrary",),
+            collective_id=collective,
+            has_side_effects=True,
+            vmem_limit_bytes=VMEM_LIMIT,
+        ),
+        cost_estimate=FREE,
+        name=name,
+    )(*operands)
+
+
+def second_products(refs, own):
+    d_gate, d_up, gate_own, gate_got, up_own, up_got = refs
+    if own:
+        return dot_nt(d_gate[...], gate_own[...]) + dot_nt(d_up[...], up_own[...])
+    return dot_nt(d_gate[...], gate_got[...]) + dot_nt(d_up[...], up_got[...])
+
+
+def second_grad(index, d_gate, d_up, gate_weight, gate_got, up_weight, up_got):
     half, hidden_cols = gate_got.shape
+    rows = d_gate.shape[0] // 2
     tile = min(SUM_TILE, half)
-    rows = d_gate.shape[0] // 2
-    left = pl.BlockSpec((rows, hidden_cols), lambda i, s: (index, 0))
-    own_spec = pl.BlockSpec((tile, hidden_cols), lambda i, s: (i, s[0]))
-    got_spec = pl.BlockSpec((tile, hidden_cols), lambda i, s: (i, 0))
-    out_spec = pl.BlockSpec((rows, tile), lambda i, s: (0, i))
-    return grid_call(
-        second_grad_kernel,
+    tiles = half // tile
+    left = pl.BlockSpec((rows, hidden_cols), lambda i: (index, 0))
+    own = pl.BlockSpec(
+        (tile, hidden_cols), lambda i: (jnp.maximum(i - tiles, 0), lax.axis_index("col"))
+    )
+    got = pl.BlockSpec((tile, hidden_cols), lambda i: (jnp.minimum(i, tiles - 1), 0))
+    return pair_sum(
+        second_products,
         "second_grad",
-        (half // tile,),
-        (jax.ShapeDtypeStruct((rows, half), BF16),) * 2,
-        [left, left, own_spec, got_spec, own_spec, got_spec],
-        [out_spec, out_spec],
-    )(place, d_gate, d_up, gate_weight, gate_got, up_weight, up_got)
-
-
-def down_kernel(place_ref, hidden_ref, down_own, down_got, own_ref, other_ref):
-    own_ref[...] = dot_nn(hidden_ref[...], down_own[...]).astype(BF16)
-    other_ref[...] = dot_nn(hidden_ref[...], down_got[...]).astype(BF16)
-
-
-def down_product(place, hidden, down_weight, down_got):
-    length, hidden_cols = hidden.shape
+        1 + index,
+        rows,
+        half,
+        [left, left, own, got, own, got],
+        (d_gate, d_up, gate_weight, gate_got, up_weight, up_got),
+    )
+
+
+def down_products(refs, own):
+    hidden, down_own, down_got = refs
+    return dot_nn(hidden[...], (down_own if own else down_got)[...])
+
+
+def down_product(hidden, down_weight, down_got):
+    rows, hidden_cols = hidden.shape
     half = down_got.shape[1]
     tile = min(SUM_TILE, half)
-    out_spec = pl.BlockSpec((length, tile), lambda i, s: (0, i))
-    return grid_call(
-        down_kernel,
+    tiles = half // tile
+    return pair_sum(
+        down_products,
         "down_product",
-        (half // tile,),
-        (jax.ShapeDtypeStruct((length, half), BF16),) * 2,
+        3,
+        rows,
+        half,
         [
-            pl.BlockSpec((length, hidden_cols), lambda i, s: (0, 0)),
-            pl.BlockSpec((hidden_cols, tile), lambda i, s: (s[0], i)),
-            pl.BlockSpec((hidden_cols, tile), lambda i, s: (0, i)),
+            pl.BlockSpec((rows, hidden_cols), lambda i: (0, 0)),
+            pl.BlockSpec(
+                (hidden_cols, tile), lambda i: (lax.axis_index("col"), jnp.maximum(i - tiles, 0))
+            ),
+            pl.BlockSpec((hidden_cols, tile), lambda i: (0, jnp.minimum(i, tiles - 1))),
         ],
-        [out_spec, out_spec],
-    )(place, hidden, down_weight, down_got)
+        (hidden, down_weight, down_got),
+    )
+
+
+def finish_kernel(orders, size, *refs):
+    count = len(orders)
+    far_ref, small_ref = refs[:2]
+    grads = refs[2 : 2 + count]
+    far_out, small_out = refs[2 + count : 4 + count]
+    outs = refs[4 + count : 4 + 2 * count]
+    small_got, small_sum, send_sem, recv_sem = refs[4 + 2 * count : 8 + 2 * count]
+    buffers = refs[8 + 2 * count :]
+    bits = len(orders[0])
+    row, place = lax.axis_index("row"), lax.axis_index("dp")
+
+    barrier = pltpu.get_barrier_semaphore()
+    partners = [{"row": 1 - row}] + [{"dp": place ^ (1 << k)} for k in range(bits)]
+    for partner in partners:
+        pl.semaphore_signal(barrier, inc=1, device_id=partner, device_id_type=MESH)
+    pl.semaphore_wait(barrier, len(partners))
+
+    def send(source, target, n, partner):
+        copy = pltpu.make_async_remote_copy(
+            src_ref=source,
+            dst_ref=target,
+            send_sem=send_sem.at[n],
+            recv_sem=recv_sem.at[n],
+            device_id=partner,
+            device_id_type=MESH,
+        )
+        copy.start()
+        return copy
+
+    waiting = [send(far_ref, far_out, 0, partners[0])]
+    current = list(grads)
+    small_sum[0] = small_ref[...]
+    for step in range(bits):
+        first = 1 + step * (count + 1)
+        bit = (step + bits - 1) % bits
+        small = send(small_sum.at[step], small_got.at[step], first, partners[1 + bit])
+        moving = []
+        for n in range(count):
+            rows = current[n].shape[0] // 2
+            got = buffers[n * (2 * bits - 1) + step]
+            moving.append(
+                send(
+                    current[n].at[pl.ds(rows, rows), :],
+                    got,
+                    first + 1 + n,
+                    partners[1 + orders[n][step]],
+                )
+            )
+        small.wait_recv()
+        if step + 1 < bits:
+            small_sum[step + 1] = small_sum[step] + small_got[step]
+        else:
+            small_out[...] = small_sum[step] + small_got[step]
+        for n in range(count):
+            rows = current[n].shape[0] // 2
+            got = buffers[n * (2 * bits - 1) + step]
+            moving[n].wait_recv()
+            sums = current[n][:rows].astype(F32) + got[...].astype(F32)
+            if step + 1 < bits:
+                target = buffers[n * (2 * bits - 1) + bits + step]
+                target[...] = sums.astype(BF16)
+                current[n] = target
+            else:
+                outs[n][...] = sums
+        waiting += [small] + moving
+    waiting[0].wait_recv()
+    for copy in waiting:
+        copy.wait_send()
+
+
+def finish(far, small, grads, orders, size):
+    bits = len(orders[0])
+    count = len(grads)
+    vmem = pl.BlockSpec(memory_space=pltpu.VMEM)
+    anywhere = pl.BlockSpec(memory_space=pl.ANY)
+    copies = 1 + bits * (count + 1)
+    scratch = [
+        pltpu.VMEM((bits,) + small.shape, F32),
+        pltpu.VMEM((bits,) + small.shape, F32),
+        pltpu.SemaphoreType.DMA((copies,)),
+        pltpu.SemaphoreType.DMA((copies,)),
+    ]
+    for grad in grads:
+        rows, columns = grad.shape
+        scratch += [pltpu.VMEM((rows >> (k + 1), columns), BF16) for k in range(bits)]
+        scratch += [pltpu.VMEM((rows >> (k + 1), columns), BF16) for k in range(bits - 1)]
+    return pl.pallas_call(
+        functools.partial(finish_kernel, orders, size),
+        out_shape=(
+            jax.ShapeDtypeStruct(far.shape, far.dtype),
+            jax.ShapeDtypeStruct(small.shape, F32),
+        )
+        + tuple(jax.ShapeDtypeStruct((g.shape[0] // size, g.shape[1]), F32) for g in grads),
+        in_specs=[anywhere, vmem] + [vmem] * count,
+        out_specs=(anywhere, vmem) + (vmem,) * count,
+        scratch_shapes=scratch,
+        compiler_params=pltpu.CompilerParams(
+            collective_id=4, has_side_effects=True, vmem_limit_bytes=VMEM_LIMIT
+        ),
+        cost_estimate=FREE,
+        name="finish",
+    )(far, small, *grads)
 
 
 def weight_grad_kernel(sets, chunks, pieces, turned, right_turned, place_ref, *refs):
@@ -936,12 +1111,13 @@
             outs[pieces * which + i][...] = sums[i * size : (i + 1) * size].astype(BF16)
 
 
-def weight_grad(places, sets, right, pieces=2, turned=False, right_turned=False):
+def weight_grad(places, sets, right, pieces=2, turned=False, right_turned=False, cut=(0, 1)):
     chunks = len(sets[0][0])
     length = sets[0][0][0].shape[1] if turned else sum(c.shape[0] for c in sets[0][0])
     count = (places.shape[0] - 2) // len(sets)
-    columns = right.shape[0] if right_turned else right.shape[1]
-    tile = min(GRAD_TILE, columns)
+    columns = (right.shape[0] if right_turned else right.shape[1]) // cut[1]
+    tile = next(size for size in (GRAD_TILE, 384, 256, 128) if columns % size == 0)
+    skip = cut[0] * (columns // tile)
     in_specs, operands = [], []
     for n, (lefts, base) in enumerate(sets):
         for p in range(count):
@@ -956,9 +1132,9 @@
                 in_specs.append(spec)
                 operands.append(left)
     if right_turned:
-        in_specs.append(pl.BlockSpec((tile, length), lambda j, s: (j, 0)))
+        in_specs.append(pl.BlockSpec((tile, length), lambda j, s: (skip + j, 0)))
     else:
-        in_specs.append(pl.BlockSpec((length, tile), lambda j, s: (0, j)))
+        in_specs.append(pl.BlockSpec((length, tile), lambda j, s: (0, skip + j)))
     size = count * LANES // pieces
     out_spec = pl.BlockSpec((size, tile), lambda j, s: (0, j))
     return grid_call(
@@ -970,6 +1146,67 @@
         [out_spec] * (pieces * len(sets)),
         [pltpu.VMEM((len(sets) * count * LANES, length), BF16)],
     )(places, *operands, right)
+
+
+def first_back_kernel(place_ref, *refs):
+    parts, (proj_ref, up_ref, normed_ref) = refs[:6], refs[6:9]
+    far_ref, own_ref, turned_ref, adapter_ref, gain_ref = refs[9:]
+    step = pl.program_id(0)
+    first = 0
+    for source in parts:
+        turned_ref[:, first : first + source.shape[0]] = jnp.transpose(source[...])
+        first += source.shape[0]
+    turned = turned_ref[...]
+    adapter_ref[...] = dot_nt(turned, up_ref[...])
+    sums = dot_nt(turned, proj_ref[...])
+    term = jnp.sum(sums * normed_ref[...].astype(F32), axis=0, keepdims=True)
+
+    @pl.when(step < pl.num_programs(0) // 2)
+    def _():
+        far_ref[...] = sums.astype(BF16)
+
+    @pl.when(step >= pl.num_programs(0) // 2)
+    def _():
+        own_ref[...] = sums
+
+    @pl.when(step == 0)
+    def _():
+        gain_ref[...] = term
+
+    @pl.when(step > 0)
+    def _():
+        gain_ref[...] += term
+
+
+def first_back(place, parts, proj_native, up_native, normed):
+    length = parts[0].shape[1]
+    half, columns = proj_native.shape
+    blocks = length // BLOCK
+    middle = blocks // 2
+    at = lambda i: (i + middle) % blocks
+    whole = lambda values: pl.BlockSpec(values.shape, lambda i, s: (0, 0))
+    return grid_call(
+        first_back_kernel,
+        "first_back",
+        (blocks,),
+        (
+            jax.ShapeDtypeStruct((length // 2, half), BF16),
+            jax.ShapeDtypeStruct((length // 2, half), F32),
+            jax.ShapeDtypeStruct((length, columns), BF16),
+            jax.ShapeDtypeStruct((length, up_native.shape[0]), F32),
+            jax.ShapeDtypeStruct((1, half), F32),
+        ),
+        [pl.BlockSpec((values.shape[0], BLOCK), lambda i, s: (0, at(i))) for values in parts]
+        + [whole(proj_native), whole(up_native)]
+        + [pl.BlockSpec((BLOCK, half), lambda i, s: (at(i), 0))],
+        [
+            pl.BlockSpec((BLOCK, half), lambda i, s: (jnp.minimum(i, middle - 1), 0)),
+            pl.BlockSpec((BLOCK, half), lambda i, s: (jnp.maximum(i - middle, 0), 0)),
+            pl.BlockSpec((BLOCK, columns), lambda i, s: (at(i), 0)),
+            pl.BlockSpec((BLOCK, up_native.shape[0]), lambda i, s: (at(i), 0)),
+            whole(jnp.zeros((1, half))),
+        ],
+    )(place, *parts, proj_native, up_native, normed)
 
 
 def after(value, *others):
@@ -1120,7 +1357,7 @@
 
     place = places(order)
 
-    def grads_of(sets, right, orders, right_turned=False):
+    def grads_of(sets, right, orders, right_turned=False, cut=(0, 1), pieces=2):
         if not direct:
             sets = [
                 (
@@ -1134,8 +1371,8 @@
                 )
                 for (lefts, base), which in zip(sets, orders)
             ]
-        outs = weight_grad(places(*orders), sets, right, 2, False, right_turned)
-        return [outs[2 * n : 2 * n + 2] for n in range(len(sets))]
+        outs = weight_grad(places(*orders), sets, right, pieces, False, right_turned, cut)
+        return [outs[pieces * n : pieces * (n + 1)] for n in range(len(sets))]
 
     def ups(index):
         zeros_key = jnp.zeros((rank, key_part), BF16)
@@ -1145,26 +1382,26 @@
                 jnp.concatenate([part(query_up, index, 2, 1), zeros_key, zeros_key], axis=1),
                 jnp.concatenate([zeros_query, part(key_up, index, 2, 1), zeros_key], axis=1),
                 jnp.concatenate([zeros_query, zeros_key, part(value_up, index, 2, 1)], axis=1),
+                jnp.zeros((rank, part_cols), BF16),
             ],
             axis=0,
         )
 
+    thin = jnp.concatenate(
+        [jnp.transpose(v) for v in (query_down, key_down, value_down)] + [output_up], axis=0
+    )
+    gains = jnp.stack([first_gain, second_gain])
+    inputs_far = swap(activations, "row")
     (
-        inputs_far,
         inputs_other,
-        inputs_far_other,
         grads_other,
         proj_got,
         gate_got,
         up_got,
         mlp_down_got,
         output_got,
-        first_gain_got,
-        second_gain_got,
-        query_down_got,
-        key_down_got,
-        value_down_got,
-        output_up_got,
+        thin_got,
+        gains_got,
         proj_own,
         proj_native,
         output_native,
@@ -1176,19 +1413,13 @@
         up_weight,
         down_weight,
         output_weight,
-        (first_gain, second_gain, query_down, key_down, value_down, output_up),
+        (thin, gains),
     )
     grads_far = swap(after(grad_out, inputs_far), "row")
     up_own = ups(col)
     up_native = jnp.concatenate([up_own, ups(1 - col)], axis=1)
-    down_own = jnp.concatenate([query_down, key_down, value_down], axis=1)
-    down_got = jnp.concatenate([query_down_got, key_down_got, value_down_got], axis=1)
-    down_full = jnp.concatenate([down_own, down_got], axis=0)
-    down_full = jnp.pad(down_full, ((0, 0), (0, LANES - 3 * rank)))
-    up_padded = jnp.pad(up_own, ((0, LANES - 3 * rank), (0, 0)))
-    gain_full = jnp.concatenate([first_gain, first_gain_got])[None]
-    second_gain_full = jnp.concatenate([second_gain, second_gain_got])[None]
-    output_up_full = jnp.concatenate([output_up, output_up_got], axis=1)
+    second_gain_full = jnp.concatenate([gains[1:], gains_got[1:]], axis=1)
+    output_up_full = jnp.concatenate([output_up, thin_got[3 * rank :]], axis=1)
     output_up_full = jnp.pad(output_up_full, ((0, LANES - rank), (0, 0)))
     output_rows_own = part(output_weight, col, 2, 0)
     output_down_own = part(output_down, col, 2, 0)
@@ -1202,7 +1433,11 @@
     documents = segments[0]
     starts = jnp.sum((documents[None, :] < documents[:, None]).astype(jnp.int32), axis=1)
     marks = jnp.concatenate(
-        [jnp.full((1,), seq_rows, jnp.int32), starts[BLOCK - WINDOW - 1 :: BLOCK]]
+        [
+            jnp.full((1,), seq_rows, jnp.int32),
+            starts[BLOCK - WINDOW - 1 :: BLOCK],
+            jnp.asarray(row, jnp.int32)[None],
+        ]
     )
     starts = starts.reshape(1, 1, seq_rows)
 
@@ -1212,16 +1447,17 @@
             place,
             mine,
             other,
-            gain_full,
-            proj_own,
-            proj_got,
-            down_full,
-            up_padded,
+            (gains, gains_got),
+            (proj_own, proj_got),
+            (thin, thin_got),
+            up_own,
             query_part,
             kept,
         )
 
     kept = project(0, activations, inputs_other, ())
+    inputs_far = after(inputs_far, kept[0])
+    inputs_far_other = swap(inputs_far, "col")
     kept = project(half_blocks, inputs_far, inputs_far_other, kept)
     normed_first, queries, keys_values, adapters, first_scale = kept
     keys_values = jnp.pad(keys_values, ((0, 0), (WINDOW, WINDOW)))
@@ -1230,8 +1466,7 @@
     )
 
     mixed, grads_far = lax.optimization_barrier((mixed, grads_far))
-    mixed_local = sequence_order(mixed, 1)
-    mixed_pair = jnp.concatenate([mixed_local, swap(mixed_local, "col")], axis=0)
+    mixed_pair = jnp.concatenate([mixed, swap(mixed, "col")], axis=0)
     adapter_sum = contract(mixed_pair, output_down_native, 0, 0)
     adapter_far = swap(other_half(adapter_sum, 0), "row")
     grads_far_other = swap(after(grads_far, mixed), "col")
@@ -1308,36 +1543,47 @@
         [jnp.asarray(v, jnp.int32) for v in [col, row] + 2 * list(range(lane_blocks))]
     )
     both = [([second_normed], 0), ([second_normed], lane_blocks)]
+
+    def up_grads(right):
+        own, other = both
+        if not direct:
+            columns = second_normed[:, feature_cols:]
+            other = ([jnp.concatenate(
+                [second_normed[:, :feature_cols], relative_blocks(columns, 1, device, order)], axis=1
+            )], lane_blocks)
+        entries = [col, row] + list(range(lane_blocks)) + block_order(order)
+        table = jnp.stack([jnp.asarray(v, jnp.int32) for v in entries])
+        outs = weight_grad(table, [own, other], right, 1)
+        half = feature_cols // 2
+        return outs[0], (outs[1][:half], outs[1][half:])
+
     own_gate, other_gate = weight_grad(natural, both, d_gate, 1)
     grad_gate_own = scattered(own_gate)
     got_gate = swap(other_gate, "col")
     own_down, other_down = grads_of(
         [([grad_out, grads_far], 0), ([grads_other, grads_far_other], 0)],
-        after(hidden, own_gate, got_gate),
+        after(hidden, own_gate),
         (order, turned_order),
     )
     reduction("down_own", own_down, order)
     down_given = given(other_down, ())
 
-    def half_second(index, *clock):
-        own, other = second_grad(
-            index, place, after(d_gate, *clock), d_up, gate_weight, gate_got, up_weight, up_got
-        )
-        got = swap(other, "col")
-        return (own.astype(F32) + got.astype(F32)).astype(BF16)
-
-    chip_far = half_second(1, own_down[0])
-    reduction("down_got", [after(v, chip_far) for v in down_given], turned_order)
+    reduction("down_got", down_given, turned_order)
+    chip_far = second_grad(
+        1, after(d_gate, own_down[0]), d_up, gate_weight, gate_got, up_weight, up_got
+    )
     far_got_own = swap(chip_far, "row")
-    chip_own = half_second(0, chip_far)
+    chip_own = second_grad(
+        0, after(d_gate, chip_far), d_up, gate_weight, gate_got, up_weight, up_got
+    )
     far_got_far = swap(chip_own, "row")
     grad_gate_got = scattered(after(got_gate, chip_own))
-    own_up, other_up = weight_grad(natural, both, after(d_up, chip_own), 1)
-    got_up = swap(other_up, "col")
-    y_own, y_other = down_product(place, after(hidden, own_up), down_weight, mlp_down_got)
-    clock = settle((y_own,), "down_own", "down_got")
-
-    y_got = swap(y_other, "col")
+    own_up, other_up = up_grads(after(d_up, chip_own))
+    got_up = given(other_up, ())
+    y_chip = down_product(after(hidden, own_up), down_weight, mlp_down_got)
+    reduction("up_got", [after(v, y_chip) for v in got_up], order)
+    clock = settle((y_chip,), "down_own", "down_got")
+
     totals = []
     for chip, got in ((chip_own, far_got_own), (chip_far, far_got_far)):
         total = (chip.astype(F32) + after(got, *clock).astype(F32)).astype(BF16)
@@ -1370,18 +1616,21 @@
     d_mixed, d_mine, d_out_padded = kept
     grad_second_gain = (gain_sum + outs[3])[0]
     d_out_adapter = d_out_padded[:, :rank]
-    y_send = (y_own[half_rows:].astype(F32) + y_got[half_rows:].astype(F32)).astype(BF16)
-    y_far = swap(y_send, "row")
+    y_far = swap(after(y_chip, kept[0])[half_rows:], "row")
+    grad_output_up = contract(out_adapter, d_mine, 0, 0)
+    grad_output_down = contract(d_out_adapter, mixed, 0, 1)
     lefts = mixed_pair
     if not direct:
-        lefts = relative_blocks(
-            ordered(mixed_local, mixed_pair[query_part:], col, 0), 0, device, order
-        )
+        lefts = relative_blocks(ordered(mixed, mixed_pair[query_part:], col, 0), 0, device, order)
     output_pair = weight_grad(
-        places(order, rows_of_pair=True), [([lefts], 0)], after(d_mine, y_send), 2, True
+        places(order, rows_of_pair=True),
+        [([lefts], 0)],
+        after(d_mine, grad_output_up, grad_output_down),
+        2,
+        True,
     )
     reduction("output", output_pair, order)
-    clock = (output_pair[0],)
+    clock = settle((output_pair[0],), "down_own", "down_got", "up_got")
 
     d_queries, d_keys, d_values, grad_query_map, grad_key_map = attention_backward(
         marks,
@@ -1394,45 +1643,27 @@
         mixed,
         inverse,
     )
-    clock = settle((d_queries,), "down_own", "down_got", "output")
-    d_queries = after(d_queries, y_far, *clock)
-    grad_up_got = scattered(after(got_up, d_queries))
-
-    d_projected = sequence_order(
-        jnp.concatenate(
-            [
-                d_queries,
-                d_keys[:, WINDOW : WINDOW + seq_rows],
-                d_values[:, WINDOW : WINDOW + seq_rows],
-            ],
-            axis=0,
-        ),
-        1,
-    )
-    d_pair = jnp.concatenate([d_projected, swap(d_projected, "col")], axis=0)
-    adapter_sum = contract(up_native, d_pair, 1, 0)
-    adapter_far = swap(other_half(adapter_sum, 1), "row")
-    inverse_first = 1.0 / first_gain
-    hat_near = normed_first[:half_rows, :feature_cols]
-    hat_far = normed_first[half_rows:, :feature_cols]
-    d_first_far = contract(d_pair[:, half_rows:], proj_native, 0, 1)
-    gain_far = jnp.sum(d_first_far * hat_far.astype(F32), axis=0)
-    d_first_far = swap(d_first_far.astype(BF16), "row")
-    (proj_pair,) = grads_of([([normed_first], 0)], after(d_pair, gain_far), (order,), True)
-    reduction("proj", proj_pair, order)
-    d_adapter = (adapter_sum + after(adapter_far, proj_pair[0])).astype(BF16)
-    d_first = contract(d_pair[:, :half_rows], proj_native, 0, 1) + contract(
-        d_adapter[:, :half_rows], down_own, 0, 1
-    )
-    grad_first_gain = (
-        gain_far + jnp.sum(d_first * hat_near.astype(F32), axis=0)
-    ) * inverse_first
-    grad_first_gain = grad_first_gain + swap(grad_first_gain, "row")
-    clock = ()
-    grad_down = contract(d_adapter, normed_first[:, :feature_cols], 1, 0)
-    grad_up = contract(adapters[:, : 3 * rank], d_projected, 0, 1)
-    grad_output_up = contract(out_adapter, d_mine, 0, 0)
-    grad_output_down = contract(d_out_adapter, mixed_local, 0, 1)
+
+    d_parts = (d_queries, d_keys, d_values)
+    d_parts += tuple(swap(values, "col") for values in d_parts)
+    clock = settle((d_queries,), "down_own", "down_got", "up_got", "output")
+    d_first_far, d_first, d_turned, adapter_sum, gain_term = first_back(
+        place, (after(d_queries, y_far, *clock),) + d_parts[1:], proj_native, up_native, normed_first
+    )
+    adapter_far = swap(other_half(adapter_sum, 0), "row")
+    gain_far = swap(gain_term, "row")
+    (proj_a,) = grads_of([([normed_first], 0)], d_turned, (order,), False, (0, 2), 1)
+    (proj_b,) = grads_of(
+        [([normed_first], 0)], after(d_turned, proj_a[0]), (turned_order,), False, (1, 2), 1
+    )
+    adapter_far, gain_far, _ = lax.optimization_barrier((adapter_far, gain_far, proj_b[0]))
+    gain_term = (gain_term + gain_far)[0]
+    d_adapter = (adapter_sum + adapter_far).astype(BF16)
+    grad_down = contract(d_adapter, normed_first[:, :feature_cols], 0, 0)
+    grad_up = contract(adapters, d_turned[:, :part_cols], 0, 0)
+    down_term = jnp.sum(thin[: 3 * rank].astype(F32) * grad_down[: 3 * rank], axis=0)
+    grad_first_gain = (gain_term + down_term) / first_gain
+    grad_down = grad_down[: 3 * rank]
     small = (
         grad_first_gain,
         grad_second_gain,
@@ -1441,35 +1672,32 @@
         grad_output_down,
         grad_up[:rank, :query_part],
         grad_up[rank : 2 * rank, query_part : query_part + key_part],
-        grad_up[2 * rank :, query_part + key_part :],
+        grad_up[2 * rank : 3 * rank, query_part + key_part :],
         grad_query_map,
         grad_key_map,
     )
     flat = [values.reshape(-1, LANES) for values in small]
-    packed = total_over(jnp.concatenate(flat, axis=0), size, bits)
+    result = (
+        state + y_chip[:half_rows].astype(F32) + y_far.astype(F32)
+    ).astype(BF16)
+    d_first = d_first + contract(d_adapter[:half_rows], thin, 1, 0)
+    packed = after(jnp.concatenate(flat, axis=0), result, d_first)
+    clock = settle((packed,), "up_got", "output")
+    d_first_far, packed, grad_proj_a, grad_proj_b = finish(
+        after(d_first_far, *clock), packed, (proj_a[0], proj_b[0]), (order, turned_order), size
+    )
     shared_rows = sum(values.shape[0] for values in flat[:4])
     packed_other = swap(packed[shared_rows:], "col")
-
-    result = (
-        state
-        + (y_own[:half_rows].astype(F32) + y_got[:half_rows].astype(F32))
-        + y_far.astype(F32)
-    ).astype(BF16)
-    d_first = d_first + after(d_first_far, d_first, result, *clock).astype(F32)
+    d_first = d_first + d_first_far.astype(F32)
     first_scale = first_scale[:half_rows]
     hat_own = activations.astype(F32) * first_scale
     grad_hat = d_first * first_gain
     inner = jnp.sum(grad_hat * hat_own, axis=1)
     inner = ((inner + swap(inner, "col")) / width)[:, None]
-    grad_activations = grad_state + first_scale * (
-        grad_hat - hat_own * inner
-    )
-    clock = (grad_activations,)
-    waiting = FINISH_ORDER
-    while any(not sums[name].done for name in waiting):
-        for name in waiting:
-            if not sums[name].done:
-                clock = settle(clock, name)
+    grad_activations = grad_state + first_scale * (grad_hat - hat_own * inner)
+    clock = (packed,)
+    while any(not sums[name].done for name in FINISH_ORDER):
+        clock = settle(clock, *(name for name in FINISH_ORDER if not sums[name].done))
 
     def unpacked(index, source, base):
         first = sum(values.shape[0] for values in flat[:index]) - base
@@ -1481,11 +1709,10 @@
         )
 
     down_total = jnp.transpose(unpacked(3, packed, 0))
-    grad_proj = sums["proj"].keep
     proj_grads = [
         ordered(
-            grad_proj[:, first : first + count],
-            grad_proj[:, part_cols + first : part_cols + first + count],
+            grad_proj_a[:, first : first + count],
+            grad_proj_b[:, first : first + count],
             col,
             1,
         )
@@ -1497,7 +1724,7 @@
     ]
 
     grad_gate = ordered(grad_gate_own, grad_gate_got, col, 1)
-    grad_up_weight = ordered(grad_up_own, grad_up_got, col, 1)
+    grad_up_weight = ordered(grad_up_own, sums["up_got"].keep, col, 1)
     grad_down_weight = ordered(sums["down_own"].keep, sums["down_got"].keep, col, 1)
     return (
         result,

time: 837 us -> 812 us (0.970)
  Pallas kernels: 447 us -> 531 us
  waiting for transfers between devices: 143 us -> 63.2 us
  other arithmetic: 99.9 us -> 80.5 us
  matrix products: 36.6 us -> 20 us
  local copies, waits for them, and re-layouts: 47.5 us -> 56.5 us
    pallas_call x3 -> x5, Pallas kernels: 75.1 us -> 174 us  [the longest x3 80.4 us: pair_sum(): pl.pallas_call(functools.partial(pair_sum_kernel, products), grid=(2 * ti...]
    ppermute x3 -> x0, waiting for transfers between devices: 42.8 us -> none  [total_over(): lax.ppermute(values, 'dp', [(i, i ^ 1 << k) for i in range(size)])]
    ppermute x34 -> x35, waiting for transfers between devices: 57.2 us -> 31.1 us  [swap(): return lax.ppermute(values, axis, [(0, 1), (1, 0)])]
    pallas_call x1, Pallas kernels: 52 us -> 29.7 us  [exchange(): pl.pallas_call(functools.partial(exchange_kernel, query_cols, key_cols),...]
    dot_general x13 -> x10, matrix products: 36.6 us -> 20 us  [contract(): lax.dot_general(left, right, (((left_dim,), (right_dim,)), ((), ())), pre...]
    convert_element_type x5 -> x2, other arithmetic: 18 us -> 6.28 us  [the longest x1 6.17 us: on_device(): result = (state + y_chip[:half_rows].astype(F32) + y_far.astype(F32)).ast...]
    ppermute x12, waiting for transfers between devices: 42.8 us -> 32 us  [launch(): lax.ppermute(send, 'dp', [(i, i ^ bit) for i in range(self.size)])]
    unnamed x185 -> x235, local copies, waits for them, and re-layouts: 23.4 us -> 13.7 us
  transfers between devices with their start and end apart: 53 -> 50, of which waited for: 21 -> 13; matrix products, arithmetic and copies ran while one was open for 20% -> 18% of each run, Pallas kernels for 42% -> 60%
where the time goes in v2:
time: 812 us; the launch traced here: 802 us
  Pallas kernels  531 us (65%)
  other arithmetic  80.5 us (10%)
  waiting for transfers between devices  63.2 us (8%)
  local copies, waits for them, and re-layouts  56.5 us (7%)
  starting transfers between devices  35.5 us (4%)
  matrix products  20 us (2%)
  between operations  15.7 us (2%)
    pallas_call x6, Pallas kernels, weight_grad(): grid_call(functools.partial(weight_grad_kernel, len(sets), chunks, pieces...  111 us
    pallas_call x3, Pallas kernels, pair_sum(): pl.pallas_call(functools.partial(pair_sum_kernel, products), grid=(2 * ti...  80.4 us
    pallas_call x4, Pallas kernels, mlp_block(): grid_call(functools.partial(mlp_kernel, len(shapes)), 'mlp_block', (tiles...  80.2 us
    pallas_call x1, Pallas kernels, finish(): pl.pallas_call(functools.partial(finish_kernel, orders, size), out_shape=...  77.1 us
    pallas_call x1, Pallas kernels, attention_backward(): pl.pallas_call(backward_kernel, out_shape=(jax.ShapeDtypeStruct(qt.shape,...  44 us
    ppermute x12, waiting for transfers between devices, launch(): lax.ppermute(send, 'dp', [(i, i ^ bit) for i in range(self.size)])  32 us
    ppermute x35, waiting for transfers between devices, swap(): return lax.ppermute(values, axis, [(0, 1), (1, 0)])  31.1 us
    pallas_call x1, Pallas kernels, exchange(): pl.pallas_call(functools.partial(exchange_kernel, query_cols, key_cols),...  29.7 us
  transfers between devices with their start and end apart: 50, of which 13 were waited for; matrix products, arithmetic and copies ran while one was open for 18% of the time, Pallas kernels for 60%

profile of v2, /device:TPU:0, one launch (start us, length us, event | category | flops | bytes accessed | tf_op | source)
XLA Modules:
  0.0 802.3 jit_solution(7388998558507497083)
XLA Ops:
  7.2 3.0 collective-permute-start
  13.0 29.7 %exchange.1 = (bf16[1024,1024]{1,0:T(8,128)(2,1)}, bf16[1024,1024]{1,0:T(8,128)(2,1)}, bf16[1024,768]{1,0:T(8,128)(2,1)}, bf16[1024,2048]{1,0:T(8,128)(2,1)}, bf...) custom-call(bf16[1024,1024]{1,0:T(8,128)(2,1)} %in_mine.3, ...), custom_call_target="tpu_custom_call" | custom-call | flops 1000 | bytes 1000 | tf_op jit(solution)/shard_map/exchange/pallas_call | solution.py:514
  45.3 10.5 %project_block.2 = (bf16[2048,2048]{1,0:T(8,128)(2,1)}, bf16[512,2048]{1,0:T(8,128)(2,1)}, bf16[256,2048]{1,0:T(8,128)(2,1)}, bf16[2048,32]{1,0:T(8,128)(2,1)}, f32[2048,1]{1,0:T(8,128)}) custom-call(s32[10]{0:T(128)} %stack.64.place_ref, bf16[1024,1024]{1,0:T(8,128)(2,1)} %in_mine.3, bf16[1024,1024]{1,0:T(8,128)(2,1)} %get-tuple-element.155.other_ref.in_other, ...), custom_call_target="tpu_custom_call" | custom-call | flops 1000 | bytes 1000 | tf_op jit(solution)/shard_map/project_block/pallas_call | solution.py:618
  61.8 10.4 %project_block.3 = (bf16[2048,2048]{1,0:T(8,128)(2,1)}, bf16[512,2048]{1,0:T(8,128)(2,1)}, bf16[256,2048]{1,0:T(8,128)(2,1)}, bf16[2048,32]{1,0:T(8,128)(2,1)}, f32[2048,1]{1,0:T(8,128)}) custom-call(s32[10]{0:T(128)} %stack.64.place_ref, ...), custom_call_target="tpu_custom_call", output_to_operand_aliasing={{0}: (10, {}), {1}: (11, {}), {2}: (12, {}), {3}: (13, {}),... | custom-call | flops 1000 | bytes 1000 | tf_op jit(solution)/shard_map/project_block/pallas_call | solution.py:618
  74.1 19.7 %attention_forward.1 = (bf16[512,2048]{1,0:T(8,128)(2,1)S(1)}, f32[2,4,2048]{2,1,0:T(4,128)S(1)}) custom-call(s32[6]{0:T(128)S(1)} %pad_add_fusion.mark_ref, s32[1,1,2048]{2,1,0:T(1,128)S(1)} %bitcast.53, bf16[512,2048]{1,0:T(8,128)(2,1)S(1)} %copy-done.2, bf16[256,2176]{1,0:T(8,128)(2,1)S(1)} %pad.18.kt_ref.vt_ref, ...), custom_call_target="tpu_custom_call" | custom-call | flops 1000 | bytes 1000 | tf_op jit(solution)/shard_map/attention_forward/pallas_call | solution.py:289
  93.8 10.5 %collective-permute-done.2.gm_far.refs_1_.refs_3_.refs_5_.refs_7_.refs_9_.refs_11_.refs_13_.refs_15_.grad_mine = bf16[1024,1024]{1,0:T(8,128)(2,1)} collective-permute-done((bf16[1024,1024]{1,0:T(8,128)(2,1)S(1)}, bf16[1024,1024]{1,0:T(8,128)(2,1)}, u32[]{:S(2)}, u32[]{:S(2)}) %collective-permute-start.2) | collective-permute-done | bytes 2097184 | tf_op jit(solution)/shard_map/ppermute | solution.py:1217
  105.1 5.5 collective-permute-done.3
  127.5 24.5 %hidden_grad.1.dh_ref = bf16[2048,2048]{1,0:T(8,128)(2,1)} custom-call(s32[10]{0:T(128)} %stack.64.place_ref, bf16[1024,1024]{1,0:T(8,128)(2,1)} %grad_mine.1, bf16[1024,1024]{1,0:T(8,128)(2,1)} %get-tuple-element.179.go_own.refs_16_.refs_18_.refs_20_.refs_22_.refs_24_.refs_26_.refs_28_.refs_30_.grad_other, ...), custom_call_target="tpu_custom_call" | custom-call | flops 1000 | bytes 1000 | tf_op jit(solution)/shard_map/hidden_grad/pallas_call | solution.py:549
  156.1 20.0 %mlp_block.4 = (bf16[2048,2048]{1,0:T(8,128)(2,1)}, bf16[2048,2048]{1,0:T(8,128)(2,1)}, bf16[2048,2048]{1,0:T(8,128)(2,1)}, bf16[2048,2048]{1,0:T(8,128)(2,1)}, f32[2048,1]{1,0:T(8,128)}, /*index=5*/f32[1024,1024]{1,0:T(8,128)}) custom-call(s32[10]{0:T(128)} %stack.64.place_ref, bf16[1024,1024]{1,0:T(8,128)(2,1)} %in_mine.3, ...), custom_call_target="tpu_custom_call" | custom-call | flops 1000 | bytes 1000 | tf_op jit(solution)/shard_map/mlp_block/pallas_call | solution.py:741
  181.6 21.1 %mlp_block.5 = (bf16[2048,2048]{1,0:T(8,128)(2,1)}, bf16[2048,2048]{1,0:T(8,128)(2,1)}, bf16[2048,2048]{1,0:T(8,128)(2,1)}, bf16[2048,2048]{1,0:T(8,128)(2,1)}, f32[2048,1]{1,0:T(8,128)}, /*index=5*/f32[1024,1024]{1,0:T(8,128)}) custom-call(s32[10]{0:T(128)} %stack.64.place_ref, ...), custom_call_target="tpu_custom_call", output_to_operand_aliasing={{0}: (15, {}), {1}: (16, {}), {2}: (17, {}), {3}: (18, {}),... | custom-call | flops 1000 | bytes 1000 | tf_op jit(solution)/shard_map/mlp_block/pallas_call | solution.py:741
  207.4 19.4 %mlp_block.6 = (bf16[2048,2048]{1,0:T(8,128)(2,1)}, bf16[2048,2048]{1,0:T(8,128)(2,1)}, bf16[2048,2048]{1,0:T(8,128)(2,1)}, bf16[2048,2048]{1,0:T(8,128)(2,1)}, f32[2048,1]{1,0:T(8,128)}) custom-call(s32[10]{0:T(128)} %stack.64.place_ref, ...), custom_call_target="tpu_custom_call", output_to_operand_aliasing={{0}: (15, {}), {1}: (16, {}), {2}: (17, {}), {3}: (18, {}),... | custom-call | flops 1000 | bytes 1000 | tf_op jit(solution)/shard_map/mlp_block/pallas_call | solution.py:741
  233.0 19.6 %mlp_block.7 = (bf16[2048,2048]{1,0:T(8,128)(2,1)}, bf16[2048,2048]{1,0:T(8,128)(2,1)}, bf16[2048,2048]{1,0:T(8,128)(2,1)}, bf16[2048,2048]{1,0:T(8,128)(2,1)}, f32[2048,1]{1,0:T(8,128)}) custom-call(s32[10]{0:T(128)} %stack.64.place_ref, ...), custom_call_target="tpu_custom_call", output_to_operand_aliasing={{0}: (15, {}), {1}: (16, {}), {2}: (17, {}), {3}: (18, {}),... | custom-call | flops 1000 | bytes 1000 | tf_op jit(solution)/shard_map/mlp_block/pallas_call | solution.py:741
  252.6 26.6 %weight_grad.6 = (bf16[1024,2048]{1,0:T(8,128)(2,1)}, bf16[1024,2048]{1,0:T(8,128)(2,1)}) custom-call(s32[18]{0:T(128)} %stack.70.place_ref, bf16[2048,2048]{1,0:T(8,128)(2,1)} %get-tuple-element.212.refs_0_.refs_1_.refs_2_.refs_3_.refs_4_.refs_5_.refs_6_.refs_7_.refs_8_.refs_9_.refs_10_.refs_11_.refs_12_.refs_13_.refs_14_.refs_15_.normed_ref, ...), custom_call_target="tpu_custom_call" | custom-call | flops 1000 | bytes 1000 | tf_op jit(solution)/shard_map/weight_grad/pallas_call | solution.py:1140
  280.2 27.3 %weight_grad.7 = (bf16[512,2048]{1,0:T(8,128)(2,1)}, bf16[512,2048]{1,0:T(8,128)(2,1)}, bf16[512,2048]{1,0:T(8,128)(2,1)}, bf16[512,2048]{1,0:T(8,128)(2,1)}) custom-call(s32[18]{0:T(128)} %stack.69.place_ref, bf16[1024,1024]{1,0:T(8,128)(2,1)} %grad_mine.1, ...), custom_call_target="tpu_custom_call" | custom-call | flops 1000 | bytes 1000 | tf_op jit(solution)/shard_map/weight_grad/pallas_call | solution.py:1140
  307.9 26.2 %second_grad.2 = bf16[1024,1024]{1,0:T(8,128)(2,1)} custom-call(bf16[2048,2048]{1,0:T(8,128)(2,1)} %get-tuple-element.219.refs_16_.refs_0_, bf16[2048,2048]{1,0:T(8,128)(2,1)} %get-tuple-element.220.refs_1_.refs_16_, bf16[1024,4096]{1,0:T(8,128)(2,1)} %refs_2_.7, bf16[1024,2048]{1,0:T(8,128)(2,1)} %get-tuple-element.185.gate_got.refs_3_, ...), custom_call_target="tpu_custom_call" | custom-call | flops 1000 | bytes 1000 | tf_op jit(solution)/shard_map/second_grad/pallas_call | solution.py:903
  334.1 26.4 %second_grad.3 = bf16[1024,1024]{1,0:T(8,128)(2,1)} custom-call(bf16[2048,2048]{1,0:T(8,128)(2,1)} %get-tuple-element.219.refs_16_.refs_0_, bf16[2048,2048]{1,0:T(8,128)(2,1)} %get-tuple-element.220.refs_1_.refs_16_, bf16[1024,4096]{1,0:T(8,128)(2,1)} %refs_2_.7, bf16[1024,2048]{1,0:T(8,128)(2,1)} %get-tuple-element.185.gate_got.refs_3_, ...), custom_call_target="tpu_custom_call" | custom-call | flops 1000 | bytes 1000 | tf_op jit(solution)/shard_map/second_grad/pallas_call | solution.py:903
  366.4 27.0 %weight_grad.8 = (bf16[1024,2048]{1,0:T(8,128)(2,1)}, bf16[1024,2048]{1,0:T(8,128)(2,1)}) custom-call(s32[18]{0:T(128)} %stack.68.place_ref, bf16[2048,2048]{1,0:T(8,128)(2,1)} %get-tuple-element.212.refs_0_.refs_1_.refs_2_.refs_3_.refs_4_.refs_5_.refs_6_.refs_7_.refs_8_.refs_9_.refs_10_.refs_11_.refs_12_.refs_13_.refs_14_.refs_15_.normed_ref, ...), custom_call_target="tpu_custom_call" | custom-call | flops 1000 | bytes 1000 | tf_op jit(solution)/shard_map/weight_grad/pallas_call | solution.py:1140
  393.4 27.8 %down_product.1 = bf16[2048,1024]{1,0:T(8,128)(2,1)} custom-call(bf16[2048,2048]{1,0:T(8,128)(2,1)} %get-tuple-element.222.refs_32_.refs_0_, bf16[4096,1024]{1,0:T(8,128)(2,1)} %refs_1_.3, bf16[2048,1024]{1,0:T(8,128)(2,1)} %get-tuple-element.181.down_got.refs_2_), custom_call_target="tpu_custom_call" | custom-call | flops 1000 | bytes 1000 | tf_op jit(solution)/shard_map/down_product/pallas_call | solution.py:903
  423.6 3.4 add_convert_fusion.5
  427.0 18.2 %collective-permute-done.22 = bf16[512,2048]{1,0:T(8,128)(2,1)} collective-permute-done((bf16[512,2048]{1,0:T(8,128)(2,1)}, bf16[512,2048]{1,0:T(8,128)(2,1)}, u32[]{:S(2)}, u32[]{:S(2)}) %collective-permute-start.22) | collective-permute-done | bytes 2097184 | tf_op jit(solution)/shard_map/ppermute | solution.py:1255
  445.2 4.6 add_convert_fusion.6
  449.7 4.1 add_convert_fusion.2.total_mine
  453.8 3.1 collective-permute-done.18
  467.1 2.6 collective-permute-start.30
  469.7 13.5 %norm_back.2 = (bf16[512,2048]{1,0:T(8,128)(2,1)}, bf16[2048,1024]{1,0:T(8,128)(2,1)}, bf16[2048,128]{1,0:T(8,128)(2,1)}, f32[1,1024]{1,0:T(1,128)}, f32[1024,1024]{1,0:T(8,128)}) custom-call(s32[10]{0:T(128)} %stack.64.place_ref, bf16[1024,1024]{1,0:T(8,128)(2,1)} %add_convert_fusion.2.total_mine, bf16[1024,1024]{1,0:T(8,128)(2,1)} %collective-permute-done.25.total_other, ...), custom_call_target="tpu_custom_call" | custom-call | flops 1000 | bytes 1000 | tf_op jit(solution)/shard_map/norm_back/pallas_call | solution.py:846
  483.2 13.3 %norm_back.3 = (bf16[512,2048]{1,0:T(8,128)(2,1)}, bf16[2048,1024]{1,0:T(8,128)(2,1)}, bf16[2048,128]{1,0:T(8,128)(2,1)}, f32[1,1024]{1,0:T(1,128)}) custom-call(s32[10]{0:T(128)} %stack.64.place_ref, bf16[1024,1024]{1,0:T(8,128)(2,1)} %copy-done.26, ...), custom_call_target="tpu_custom_call", output_to_operand_aliasing={{0}: (12, {}), {1}: (13, {}), {2}: (14, {})} | custom-call | flops 1000 | bytes 1000 | tf_op jit(solution)/shard_map/norm_back/pallas_call | solution.py:846
  496.6 3.0 fusion.40
  502.6 3.1 slice.267
  506.4 9.4 %weight_grad.9 = (bf16[512,1024]{1,0:T(8,128)(2,1)}, bf16[512,1024]{1,0:T(8,128)(2,1)}) custom-call(s32[10]{0:T(128)} %stack.79.place_ref, bf16[1024,2048]{1,0:T(8,128)(2,1)} %copy-done.20, bf16[1024,2048]{1,0:T(8,128)(2,1)} %copy-done.20, bf16[1024,2048]{1,0:T(8,128)(2,1)} %copy-done.20, bf16[1024,2048]{1,0:T(8,128)(2,1)} %copy-done.20, ...), custom_call_target="tpu_custom_call" | custom-call | flops 1000 | bytes 1000 | tf_op jit(solution)/shard_map/weight_grad/pallas_call | solution.py:1140
  515.8 4.4 collective-permute-done.31
  522.8 9.5 %collective-permute-done.30 = bf16[256,2048]{1,0:T(8,128)(2,1)} collective-permute-done((bf16[256,2048]{1,0:T(8,128)(2,1)}, bf16[256,2048]{1,0:T(8,128)(2,1)}, u32[]{:S(2)}, u32[]{:S(2)}) %collective-permute-start.30) | collective-permute-done | bytes 1048608 | tf_op jit(solution)/shard_map/ppermute | solution.py:1255
  532.3 2.6 add_convert_fusion.15
  536.5 4.5 add_convert_fusion.3
  541.5 4.0 collective-permute-start.33
  545.6 44.0 %attention_backward.1 = (bf16[512,2048]{1,0:T(8,128)(2,1)S(1)}, bf16[128,2048]{1,0:T(8,128)(2,1)S(1)}, bf16[128,2048]{1,0:T(8,128)(2,1)S(1)}, f32[8,64,64]{2,1,0:T(8,128)S(1)}, f32[2,64,64]{2,1,0:T(8,128)S(1)}) custom-call(s32[6]{0:T(128)S(1)} %copy-done.19, s32[1,1,2048]{2,1,0:T(1,128)S(1)} %bitcast.54, bf16[512,2048]{1,0:T(8,128)(2,1)} %get-tuple-element.166.qt_ref, ...), custom_call_target="tpu_custom_call" | custom-call | flops 1000 | bytes 1000 | tf_op jit(solution)/shard_map/attention_backward/pallas_call | solution.py:330
  596.6 2.9 copy.126
  599.7 3.0 add_convert_fusion.9
  602.6 2.6 add_convert_fusion.10
  606.9 16.6 %first_back.1 = (bf16[1024,1024]{1,0:T(8,128)(2,1)}, f32[1024,1024]{1,0:T(8,128)}, bf16[2048,1536]{1,0:T(8,128)(2,1)}, f32[2048,32]{1,0:T(8,128)}, f32[1,1024]{1,0:T(1,128)}) custom-call(s32[10]{0:T(128)} %stack.64.place_ref, bf16[512,2048]{1,0:T(8,128)(2,1)} %copy-done.7, bf16[128,2048]{1,0:T(8,128)(2,1)} %copy-done.12, bf16[128,2048]{1,0:T(8,128)(2,1)} %copy-done.13, ...), custom_call_target="tpu_custom_call" | custom-call | flops 1000 | bytes 1000 | tf_op jit(solution)/shard_map/first_back/pallas_call | solution.py:1188
  627.9 6.2 add_convert_fusion
  634.7 10.2 %weight_grad.10.refs_2_ = bf16[1024,768]{1,0:T(8,128)(2,1)} custom-call(s32[10]{0:T(128)} %stack.64.place_ref, bf16[2048,2048]{1,0:T(8,128)(2,1)} %get-tuple-element.263.refs_8_.refs_0_.refs_1_.refs_2_.refs_3_.refs_4_.refs_5_.refs_6_.refs_7_, bf16[2048,2048]{1,0:T(8,128)(2,1)} %get-tuple-element.263.refs_8_.refs_0_.refs_1_.refs_2_.refs_3_.refs_4_.refs_5_.refs_6_.refs_7_, ...), custom_call_target="tpu_custom_call" | custom-call | flops 1000 | bytes 1000 | tf_op jit(solution)/shard_map/weight_grad/pallas_call | solution.py:1140
  644.9 10.5 %weight_grad.11.refs_3_ = bf16[1024,768]{1,0:T(8,128)(2,1)} custom-call(s32[10]{0:T(128)} %stack.160.place_ref, bf16[2048,2048]{1,0:T(8,128)(2,1)} %get-tuple-element.263.refs_8_.refs_0_.refs_1_.refs_2_.refs_3_.refs_4_.refs_5_.refs_6_.refs_7_, bf16[2048,2048]{1,0:T(8,128)(2,1)} %get-tuple-element.263.refs_8_.refs_0_.refs_1_.refs_2_.refs_3_.refs_4_.refs_5_.refs_6_.refs_7_, ...), custom_call_target="tpu_custom_call" | custom-call | flops 1000 | bytes 1000 | tf_op jit(solution)/shard_map/weight_grad/pallas_call | solution.py:1140
  658.4 3.1 multiply_reduce_fusion.1
  666.6 3.0 convert_add_fusion
  671.6 77.1 %finish.1 = (bf16[1024,1024]{1,0:T(8,128)(2,1)}, f32[672,128]{1,0:T(8,128)}, f32[128,768]{1,0:T(8,128)}, f32[128,768]{1,0:T(8,128)}) custom-call(bf16[1024,1024]{1,0:T(8,128)(2,1)} %get-tuple-element.280.refs_0_, f32[672,128]{1,0:T(8,128)} %copy-done.63, bf16[1024,768]{1,0:T(8,128)(2,1)} %weight_grad.10.refs_2_, bf16[1024,768]{1,0:T(8,128)(2,1)} %weight_grad.11.refs_3_), custom_call_target="tpu_custom_call" | custom-call | flops 1000 | bytes 1000 | tf_op jit(solution)/shard_map/finish/pallas_call | solution.py:1067
  751.9 2.8 multiply_reduce_fusion
  769.9 3.1 collective-permute-start.45
  775.0 6.1 multiply_add_fusion
  (442 shorter events, 137.2 us)
Async XLA Ops:
  7.2 648.8 %reduce-scatter.4.cloned.1.call-start = ((), (), s32[]{:S(2)}) async-start(), calls=%async_computation.3 | async-start | bytes 4718592 | tf_op jit(solution)/shard_map/reduce_scatter | solution.py:1540
  7.2 49.0 %collective-permute-start = (bf16[1024,1024]{1,0:T(8,128)(2,1)}, bf16[1024,1024]{1,0:T(8,128)(2,1)}, u32[]{:S(2)}, u32[]{:S(2)}) collective-permute-start(bf16[1024,1024]{1,0:T(8,128)(2,1)} %in_mine.3), channel_id=1, source_target_pairs={{0,2},{2,0},{1,3},{3,1},{4,6},{6,4},{5,7},{7,5},{8,10},{10,8},{9,1... | collective-permute-start | bytes 6291464 | tf_op jit(solution)/shard_map/ppermute | solution.py:1217
  56.2 5.6 collective-permute-start.1
  56.2 48.1 %collective-permute-start.2 = (bf16[1024,1024]{1,0:T(8,128)(2,1)S(1)}, bf16[1024,1024]{1,0:T(8,128)(2,1)}, u32[]{:S(2)}, u32[]{:S(2)}) collective-permute-start(bf16[1024,1024]{1,0:T(8,128)(2,1)S(1)} %copy-done.21), channel_id=1, source_target_pairs={{0,2},{2,0},{1,3},{3,1},{4,6},{6,4},{5,7},{7,5},{8,10},{10,8},{9,1... | collective-permute-start | bytes 6291464 | tf_op jit(solution)/shard_map/ppermute | solution.py:1217
  104.3 6.3 collective-permute-start.3
  104.4 21.8 %collective-permute-start.6 = (bf16[1024,1024]{1,0:T(8,128)(2,1)}, bf16[1024,1024]{1,0:T(8,128)(2,1)S(1)}, u32[]{:S(2)}, u32[]{:S(2)}) collective-permute-start(bf16[1024,1024]{1,0:T(8,128)(2,1)} %collective-permute-done.2.gm_far.refs_1_.refs_3_.refs_5_.refs_7_.refs_9_.refs_11_.refs_13_.refs_15_.grad_mine), channel_id=1, source_target_pairs={{0,1},{1,0},{2,3},{3,2},{4,5},{5,4},{6,7},{7,6},{8,9},{9,8},{10,11... | collective-permute-start | bytes 6291464 | tf_op jit(solution)/shard_map/ppermute | solution.py:1217
  111.6 4.7 collective-permute-start.4
  116.3 35.7 %collective-permute-start.5 = (bf16[512,1024]{1,0:T(8,128)(2,1)}, bf16[512,1024]{1,0:T(8,128)(2,1)}, u32[]{:S(2)}, u32[]{:S(2)}) collective-permute-start(bf16[512,1024]{1,0:T(8,128)(2,1)} %convolution_convert_fusion.3.at_mine), channel_id=1, source_target_pairs={{0,2},{2,0},{1,3},{3,1},{4,6},{6,4},{5,7},{7,5},{8,10},{10,8},{9,1... | collective-permute-start | bytes 3145736 | tf_op jit(solution)/shard_map/ppermute | solution.py:1217
  122.6 32.5 %collective-permute-start.9 = (bf16[512,1024]{1,0:T(8,128)(2,1)}, bf16[512,1024]{1,0:T(8,128)(2,1)}, u32[]{:S(2)}, u32[]{:S(2)}) collective-permute-start(bf16[512,1024]{1,0:T(8,128)(2,1)} %convolution_convert_fusion.1.at_mine), channel_id=1, source_target_pairs={{0,1},{1,0},{2,3},{3,2},{4,5},{5,4},{6,7},{7,6},{8,9},{9,8},{10,11... | collective-permute-start | bytes 3145736 | tf_op jit(solution)/shard_map/ppermute | solution.py:1217
  152.0 3.1 collective-permute-start.10
  152.6 25.4 %collective-permute-start.8 = (bf16[512,1024]{1,0:T(8,128)(2,1)}, bf16[512,1024]{1,0:T(8,128)(2,1)S(1)}, u32[]{:S(2)}, u32[]{:S(2)}) collective-permute-start(bf16[512,1024]{1,0:T(8,128)(2,1)} %convolution_convert_fusion.2.at_mine), channel_id=1, source_target_pairs={{0,2},{2,0},{1,3},{3,1},{4,6},{6,4},{5,7},{7,5},{8,10},{10,8},{9,1... | collective-permute-start | bytes 3145736 | tf_op jit(solution)/shard_map/ppermute | solution.py:1217
  155.1 23.4 %collective-permute-start.7 = (bf16[512,1024]{1,0:T(8,128)(2,1)S(1)}, bf16[512,1024]{1,0:T(8,128)(2,1)S(1)}, u32[]{:S(2)}, u32[]{:S(2)}) collective-permute-start(bf16[512,1024]{1,0:T(8,128)(2,1)S(1)} %copy-done.33), channel_id=1, source_target_pairs={{0,1},{1,0},{2,3},{3,2},{4,5},{5,4},{6,7},{7,6},{8,9},{9,8},{10,11... | collective-permute-start | bytes 3145736 | tf_op jit(solution)/shard_map/ppermute | solution.py:1217
  178.0 2.7 collective-permute-start.11
  178.0 25.8 %collective-permute-start.12 = (bf16[512,1024]{1,0:T(8,128)(2,1)}, bf16[512,1024]{1,0:T(8,128)(2,1)S(1)}, u32[]{:S(2)}, u32[]{:S(2)}) collective-permute-start(bf16[512,1024]{1,0:T(8,128)(2,1)} %convolution_convert_fusion.1.at_mine), channel_id=1, source_target_pairs={{0,2},{2,0},{1,3},{3,1},{4,6},{6,4},{5,7},{7,5},{8,10},{10,8},{9,1... | collective-permute-start | bytes 3145736 | tf_op jit(solution)/shard_map/ppermute | solution.py:1217
  178.5 25.8 %collective-permute-start.15 = (bf16[512,1024]{1,0:T(8,128)(2,1)}, bf16[512,1024]{1,0:T(8,128)(2,1)S(1)}, u32[]{:S(2)}, u32[]{:S(2)}) collective-permute-start(bf16[512,1024]{1,0:T(8,128)(2,1)} %convolution_convert_fusion.3.at_mine), channel_id=1, source_target_pairs={{0,1},{1,0},{2,3},{3,2},{4,5},{5,4},{6,7},{7,6},{8,9},{9,8},{10,11... | collective-permute-start | bytes 3145736 | tf_op jit(solution)/shard_map/ppermute | solution.py:1217
  203.8 25.6 %collective-permute-start.14 = (bf16[512,1024]{1,0:T(8,128)(2,1)S(1)}, bf16[512,1024]{1,0:T(8,128)(2,1)S(1)}, u32[]{:S(2)}, u32[]{:S(2)}) collective-permute-start(bf16[512,1024]{1,0:T(8,128)(2,1)S(1)} %copy-done.34), channel_id=1, source_target_pairs={{0,2},{2,0},{1,3},{3,1},{4,6},{6,4},{5,7},{7,5},{8,10},{10,8},{9,1... | collective-permute-start | bytes 3145736 | tf_op jit(solution)/shard_map/ppermute | solution.py:1217
  204.1 25.9 %collective-permute-start.13 = (bf16[512,1024]{1,0:T(8,128)(2,1)}, bf16[512,1024]{1,0:T(8,128)(2,1)S(1)}, u32[]{:S(2)}, u32[]{:S(2)}) collective-permute-start(bf16[512,1024]{1,0:T(8,128)(2,1)} %convolution_convert_fusion.2.at_mine), channel_id=1, source_target_pairs={{0,1},{1,0},{2,3},{3,2},{4,5},{5,4},{6,7},{7,6},{8,9},{9,8},{10,11... | collective-permute-start | bytes 3145736 | tf_op jit(solution)/shard_map/ppermute | solution.py:1217
  279.3 510.9 %reduce-scatter.6.cloned.1.call-start = ((), (), s32[]{:S(2)}) async-start(), calls=%async_computation.4 | async-start | bytes 4718592 | tf_op jit(solution)/shard_map/reduce_scatter | solution.py:1540
  279.3 81.2 %collective-permute-start.46 = (bf16[1024,2048]{1,0:T(8,128)(2,1)}, bf16[1024,2048]{1,0:T(8,128)(2,1)}, u32[]{:S(2)}, u32[]{:S(2)}) collective-permute-start(bf16[1024,2048]{1,0:T(8,128)(2,1)} %get-tuple-element.286), channel_id=1, source_target_pairs={{0,1},{1,0},{2,3},{3,2},{4,5},{5,4},{6,7},{7,6},{8,9},{9,8},{10,11... | collective-permute-start | bytes 12582920 | tf_op jit(solution)/shard_map/ppermute | solution.py:1217
  307.5 54.7 %collective-permute-start.21 = (bf16[512,2048]{1,0:T(8,128)(2,1)}, bf16[512,2048]{1,0:T(8,128)(2,1)}, u32[]{:S(2)}, u32[]{:S(2)}) collective-permute-start(bf16[512,2048]{1,0:T(8,128)(2,1)} %get-tuple-element.224), channel_id=1, source_target_pairs={{0,1},{1,0},{2,3},{3,2},{4,5},{5,4},{6,7},{7,6},{8,9},{9,8},{10,11... | collective-permute-start | bytes 6291464 | tf_op jit(solution)/shard_map/ppermute | solution.py:1217
  360.5 432.3 %reduce-scatter.8.cloned.1.call-start = ((), (), s32[]{:S(2)}) async-start(), calls=%async_computation.5 | async-start | bytes 4718592 | tf_op jit(solution)/shard_map/reduce_scatter | solution.py:1540
  360.6 62.5 %collective-permute-start.23 = (bf16[512,2048]{1,0:T(8,128)(2,1)}, bf16[512,2048]{1,0:T(8,128)(2,1)}, u32[]{:S(2)}, u32[]{:S(2)}) collective-permute-start(bf16[512,2048]{1,0:T(8,128)(2,1)} %get-tuple-element.225), channel_id=1, source_target_pairs={{0,4},{4,0},{8,12},{12,8},{16,20},{20,16},{24,28},{28,24},{1,5},{5... | collective-permute-start | bytes 6291464 | tf_op jit(solution)/shard_map/ppermute | solution.py:1255
  362.2 82.9 %collective-permute-start.22 = (bf16[512,2048]{1,0:T(8,128)(2,1)}, bf16[512,2048]{1,0:T(8,128)(2,1)}, u32[]{:S(2)}, u32[]{:S(2)}) collective-permute-start(bf16[512,2048]{1,0:T(8,128)(2,1)} %collective-permute-done.21), channel_id=1, source_target_pairs={{0,8},{4,12},{8,0},{12,4},{16,24},{20,28},{24,16},{28,20},{1,9},{5... | collective-permute-start | bytes 6291464 | tf_op jit(solution)/shard_map/ppermute | solution.py:1255
  363.8 81.4 %collective-permute-start.20 = (bf16[512,2048]{1,0:T(8,128)(2,1)}, bf16[512,2048]{1,0:T(8,128)(2,1)}, u32[]{:S(2)}, u32[]{:S(2)}) collective-permute-start(bf16[512,2048]{1,0:T(8,128)(2,1)} %get-tuple-element.223), channel_id=1, source_target_pairs={{0,1},{1,0},{2,3},{3,2},{4,5},{5,4},{6,7},{7,6},{8,9},{9,8},{10,11... | collective-permute-start | bytes 6291464 | tf_op jit(solution)/shard_map/ppermute | solution.py:1217
  363.8 86.0 %collective-permute-start.19 = (bf16[1024,1024]{1,0:T(8,128)(2,1)S(1)}, bf16[1024,1024]{1,0:T(8,128)(2,1)}, u32[]{:S(2)}, u32[]{:S(2)}) collective-permute-start(bf16[1024,1024]{1,0:T(8,128)(2,1)S(1)} %copy-done.27), channel_id=1, source_target_pairs={{0,2},{2,0},{1,3},{3,1},{4,6},{6,4},{5,7},{7,5},{8,10},{10,8},{9,1... | collective-permute-start | bytes 6291464 | tf_op jit(solution)/shard_map/ppermute | solution.py:1217
  364.9 91.9 %collective-permute-start.18 = (bf16[1024,1024]{1,0:T(8,128)(2,1)}, bf16[1024,1024]{1,0:T(8,128)(2,1)}, u32[]{:S(2)}, u32[]{:S(2)}) collective-permute-start(bf16[1024,1024]{1,0:T(8,128)(2,1)} %second_grad.3), channel_id=1, source_target_pairs={{0,2},{2,0},{1,3},{3,1},{4,6},{6,4},{5,7},{7,5},{8,10},{10,8},{9,1... | collective-permute-start | bytes 6291464 | tf_op jit(solution)/shard_map/ppermute | solution.py:1217
  423.1 37.0 %collective-permute-start.28 = (bf16[512,2048]{1,0:T(8,128)(2,1)S(1)}, bf16[512,2048]{1,0:T(8,128)(2,1)}, u32[]{:S(2)}, u32[]{:S(2)}) collective-permute-start(bf16[512,2048]{1,0:T(8,128)(2,1)S(1)} %get-tuple-element.401), channel_id=1, source_target_pairs={{0,1},{1,0},{2,3},{3,2},{4,5},{5,4},{6,7},{7,6},{8,9},{9,8},{10,11... | collective-permute-start | bytes 6291464 | tf_op jit(solution)/shard_map/ppermute | solution.py:1217
  445.1 21.9 %collective-permute-start.27 = (bf16[512,2048]{1,0:T(8,128)(2,1)}, bf16[512,2048]{1,0:T(8,128)(2,1)}, u32[]{:S(2)}, u32[]{:S(2)}) collective-permute-start(bf16[512,2048]{1,0:T(8,128)(2,1)} %get-tuple-element.400), channel_id=1, source_target_pairs={{0,1},{1,0},{2,3},{3,2},{4,5},{5,4},{6,7},{7,6},{8,9},{9,8},{10,11... | collective-permute-start | bytes 6291464 | tf_op jit(solution)/shard_map/ppermute | solution.py:1217
  459.5 10.2 %collective-permute-start.25 = (bf16[1024,1024]{1,0:T(8,128)(2,1)}, bf16[1024,1024]{1,0:T(8,128)(2,1)}, u32[]{:S(2)}, u32[]{:S(2)}) collective-permute-start(bf16[1024,1024]{1,0:T(8,128)(2,1)} %add_convert_fusion.2.total_mine), channel_id=1, source_target_pairs={{0,1},{1,0},{2,3},{3,2},{4,5},{5,4},{6,7},{7,6},{8,9},{9,8},{10,11... | collective-permute-start | bytes 6291464 | tf_op jit(solution)/shard_map/ppermute | solution.py:1217
  459.6 23.6 %collective-permute-start.24 = (bf16[1024,1024]{1,0:T(8,128)(2,1)S(1)}, bf16[1024,1024]{1,0:T(8,128)(2,1)}, u32[]{:S(2)}, u32[]{:S(2)}) collective-permute-start(bf16[1024,1024]{1,0:T(8,128)(2,1)S(1)} %add_convert_fusion.1.total_mine), channel_id=1, source_target_pairs={{0,1},{1,0},{2,3},{3,2},{4,5},{5,4},{6,7},{7,6},{8,9},{9,8},{10,11... | collective-permute-start | bytes 6291464 | tf_op jit(solution)/shard_map/ppermute | solution.py:1217
  460.1 74.7 %collective-permute-start.29 = (bf16[512,2048]{1,0:T(8,128)(2,1)}, bf16[512,2048]{1,0:T(8,128)(2,1)}, u32[]{:S(2)}, u32[]{:S(2)}) collective-permute-start(bf16[512,2048]{1,0:T(8,128)(2,1)} %collective-permute-done.28), channel_id=1, source_target_pairs={{0,4},{4,0},{8,12},{12,8},{16,20},{20,16},{24,28},{28,24},{1,5},{5... | collective-permute-start | bytes 6291464 | tf_op jit(solution)/shard_map/ppermute | solution.py:1255
  460.7 59.5 %collective-permute-start.31 = (bf16[256,2048]{1,0:T(8,128)(2,1)}, bf16[256,2048]{1,0:T(8,128)(2,1)}, u32[]{:S(2)}, u32[]{:S(2)}) collective-permute-start(bf16[256,2048]{1,0:T(8,128)(2,1)} %get-tuple-element.402), channel_id=1, source_target_pairs={{0,8},{4,12},{8,0},{12,4},{16,24},{20,28},{24,16},{28,20},{1,9},{5... | collective-permute-start | bytes 3145736 | tf_op jit(solution)/shard_map/ppermute | solution.py:1255
  467.1 65.2 %collective-permute-start.30 = (bf16[256,2048]{1,0:T(8,128)(2,1)}, bf16[256,2048]{1,0:T(8,128)(2,1)}, u32[]{:S(2)}, u32[]{:S(2)}) collective-permute-start(bf16[256,2048]{1,0:T(8,128)(2,1)} %get-tuple-element.404), channel_id=1, source_target_pairs={{0,16},{4,20},{8,24},{12,28},{16,0},{20,4},{24,8},{28,12},{1,17},{... | collective-permute-start | bytes 3145736 | tf_op jit(solution)/shard_map/ppermute | solution.py:1255
  505.7 99.6 %collective-permute-start.26 = (bf16[1024,1024]{1,0:T(8,128)(2,1)}, bf16[1024,1024]{1,0:T(8,128)(2,1)}, u32[]{:S(2)}, u32[]{:S(2)}) collective-permute-start(bf16[1024,1024]{1,0:T(8,128)(2,1)} %slice.267), channel_id=1, source_target_pairs={{0,2},{2,0},{1,3},{3,1},{4,6},{6,4},{5,7},{7,5},{8,10},{10,8},{9,1... | collective-permute-start | bytes 6291464 | tf_op jit(solution)/shard_map/ppermute | solution.py:1217
  534.9 58.5 %collective-permute-start.34 = (bf16[128,2048]{1,0:T(8,128)(2,1)}, bf16[128,2048]{1,0:T(8,128)(2,1)}, u32[]{:S(2)}, u32[]{:S(2)}) collective-permute-start(bf16[128,2048]{1,0:T(8,128)(2,1)} %get-tuple-element.412), channel_id=1, source_target_pairs={{0,4},{4,0},{8,12},{12,8},{16,20},{20,16},{24,28},{28,24},{1,5},{5... | collective-permute-start | bytes 1572872 | tf_op jit(solution)/shard_map/ppermute | solution.py:1255
  536.4 55.5 %collective-permute-start.35 = (bf16[128,2048]{1,0:T(8,128)(2,1)}, bf16[128,2048]{1,0:T(8,128)(2,1)}, u32[]{:S(2)}, u32[]{:S(2)}) collective-permute-start(bf16[128,2048]{1,0:T(8,128)(2,1)} %get-tuple-element.410), channel_id=1, source_target_pairs={{0,16},{4,20},{8,24},{12,28},{16,0},{20,4},{24,8},{28,12},{1,17},{... | collective-permute-start | bytes 1572872 | tf_op jit(solution)/shard_map/ppermute | solution.py:1255
  541.0 61.7 %collective-permute-start.32 = (bf16[512,1024]{1,0:T(8,128)(2,1)}, bf16[512,1024]{1,0:T(8,128)(2,1)}, u32[]{:S(2)}, u32[]{:S(2)}) collective-permute-start(bf16[512,1024]{1,0:T(8,128)(2,1)} %get-tuple-element.254), channel_id=1, source_target_pairs={{0,4},{4,0},{8,12},{12,8},{16,20},{20,16},{24,28},{28,24},{1,5},{5... | collective-permute-start | bytes 3145736 | tf_op jit(solution)/shard_map/ppermute | solution.py:1255
  541.5 58.0 %collective-permute-start.33 = (bf16[256,2048]{1,0:T(8,128)(2,1)}, bf16[256,2048]{1,0:T(8,128)(2,1)}, u32[]{:S(2)}, u32[]{:S(2)}) collective-permute-start(bf16[256,2048]{1,0:T(8,128)(2,1)} %get-tuple-element.398), channel_id=1, source_target_pairs={{0,8},{4,12},{8,0},{12,4},{16,24},{20,28},{24,16},{28,20},{1,9},{5... | collective-permute-start | bytes 3145736 | tf_op jit(solution)/shard_map/ppermute | solution.py:1255
  591.9 14.2 %collective-permute-start.36 = (bf16[512,2048]{1,0:T(8,128)(2,1)S(1)}, bf16[512,2048]{1,0:T(8,128)(2,1)}, u32[]{:S(2)}, u32[]{:S(2)}) collective-permute-start(bf16[512,2048]{1,0:T(8,128)(2,1)S(1)} %get-tuple-element.259.refs_0_), channel_id=1, source_target_pairs={{0,1},{1,0},{2,3},{3,2},{4,5},{5,4},{6,7},{7,6},{8,9},{9,8},{10,11... | collective-permute-start | bytes 6291464 | tf_op jit(solution)/shard_map/ppermute | solution.py:1217
  593.4 12.7 %collective-permute-start.37 = (bf16[128,2048]{1,0:T(8,128)(2,1)S(1)}, bf16[128,2048]{1,0:T(8,128)(2,1)}, u32[]{:S(2)}, u32[]{:S(2)}) collective-permute-start(bf16[128,2048]{1,0:T(8,128)(2,1)S(1)} %get-tuple-element.260.refs_1_), channel_id=1, source_target_pairs={{0,1},{1,0},{2,3},{3,2},{4,5},{5,4},{6,7},{7,6},{8,9},{9,8},{10,11... | collective-permute-start | bytes 1572872 | tf_op jit(solution)/shard_map/ppermute | solution.py:1217
  599.5 6.6 collective-permute-start.38
  605.2 64.3 %collective-permute-start.41 = (bf16[256,1024]{1,0:T(8,128)(2,1)}, bf16[256,1024]{1,0:T(8,128)(2,1)}, u32[]{:S(2)}, u32[]{:S(2)}) collective-permute-start(bf16[256,1024]{1,0:T(8,128)(2,1)} %get-tuple-element.408), channel_id=1, source_target_pairs={{0,8},{4,12},{8,0},{12,4},{16,24},{20,28},{24,16},{28,20},{1,9},{5... | collective-permute-start | bytes 1572872 | tf_op jit(solution)/shard_map/ppermute | solution.py:1255
  605.2 61.3 %collective-permute-start.42 = (bf16[128,2048]{1,0:T(8,128)(2,1)}, bf16[128,2048]{1,0:T(8,128)(2,1)}, u32[]{:S(2)}, u32[]{:S(2)}) collective-permute-start(bf16[128,2048]{1,0:T(8,128)(2,1)} %get-tuple-element.406), channel_id=1, source_target_pairs={{0,16},{4,20},{8,24},{12,28},{16,0},{20,4},{24,8},{28,12},{1,17},{... | collective-permute-start | bytes 1572872 | tf_op jit(solution)/shard_map/ppermute | solution.py:1255
  625.9 31.3 %collective-permute-start.39 = (f32[2048,32]{0,1:T(8,128)}, f32[2048,32]{0,1:T(8,128)S(1)}, u32[]{:S(2)}, u32[]{:S(2)}) collective-permute-start(f32[2048,32]{0,1:T(8,128)} %pad_maximum_fusion), channel_id=1, source_target_pairs={{0,2},{2,0},{1,3},{3,1},{4,6},{6,4},{5,7},{7,5},{8,10},{10,8},{9,1... | collective-permute-start | bytes 786440 | tf_op jit(solution)/shard_map/ppermute | solution.py:1217
  626.8 30.5 %collective-permute-start.40 = (f32[1,1024]{1,0:T(1,128)S(1)}, f32[1,1024]{1,0:T(1,128)S(1)}, u32[]{:S(2)}, u32[]{:S(2)}) collective-permute-start(f32[1,1024]{1,0:T(1,128)S(1)} %copy-done.108), channel_id=1, source_target_pairs={{0,2},{2,0},{1,3},{3,1},{4,6},{6,4},{5,7},{7,5},{8,10},{10,8},{9,1... | collective-permute-start | bytes 12296 | tf_op jit(solution)/shard_map/ppermute | solution.py:1217
  754.6 19.6 %collective-permute-start.43 = (f32[1024]{0:T(1024)S(1)}, f32[1024]{0:T(1024)}, u32[]{:S(2)}, u32[]{:S(2)}) collective-permute-start(f32[1024]{0:T(1024)S(1)} %multiply_reduce_fusion), channel_id=1, source_target_pairs={{0,1},{1,0},{2,3},{3,2},{4,5},{5,4},{6,7},{7,6},{8,9},{9,8},{10,11... | collective-permute-start | bytes 12296 | tf_op jit(solution)/shard_map/ppermute | solution.py:1217
  757.1 24.0 %collective-permute-start.44 = (f32[400,128]{1,0:T(8,128)}, f32[400,128]{1,0:T(8,128)}, u32[]{:S(2)}, u32[]{:S(2)}) collective-permute-start(f32[400,128]{1,0:T(8,128)} %slice.317), channel_id=1, source_target_pairs={{0,1},{1,0},{2,3},{3,2},{4,5},{5,4},{6,7},{7,6},{8,9},{9,8},{10,11... | collective-permute-start | bytes 614408 | tf_op jit(solution)/shard_map/ppermute | solution.py:1217
  769.9 18.5 %collective-permute-start.45 = (bf16[128,1024]{1,0:T(8,128)(2,1)}, bf16[128,1024]{1,0:T(8,128)(2,1)}, u32[]{:S(2)}, u32[]{:S(2)}) collective-permute-start(bf16[128,1024]{1,0:T(8,128)(2,1)} %get-tuple-element.414), channel_id=1, source_target_pairs={{0,16},{4,20},{8,24},{12,28},{16,0},{20,4},{24,8},{28,12},{1,17},{... | collective-permute-start | bytes 786440 | tf_op jit(solution)/shard_map/ppermute | solution.py:1255
  (114 other events, 1328.2 us)
Sparse Core Ops, SparseCore 0:
  279.4 88.4 reduce-scatter.3
  372.0 157.8 reduce-scatter.5
  592.0 122.5 reduce-scatter.7

commit v3 on v2

--- a/solution.py
+++ b/solution.py
@@ -17,7 +17,6 @@
 SUM_TILE = 256
 GRAD_TILE = 512
 VMEM_LIMIT = 56 * 1024 * 1024
-FINISH_ORDER = ("up_got", "output", "down_own", "down_got")
 norm_eps = 1e-05
 F32 = jnp.float32
 BF16 = jnp.bfloat16
@@ -133,6 +132,11 @@
     member = jnp.where(member_lanes(base, mark), tile, jnp.zeros_like(tile))
     state_ref[...] = keep * state_ref[...] + dot_nt(vt_ref[:, pl.ds(base, BLOCK)], member)
     norm_ref[...] = keep * norm + jnp.sum(member.astype(F32), axis=1, keepdims=True)
+
+
+def packed_map(grad):
+    half = grad.shape[0] // 2
+    return jnp.concatenate([grad[:half], grad[half:]], axis=1)
 
 
 def backward_kernel(
@@ -240,7 +244,7 @@
         dq = jnp.concatenate([part[:, lanes] for part in dq_parts], axis=1)
         dq = dq + dot_nn(qback_ref[h], dpre)
         dqt_ref[h * HEAD_DIM : (h + 1) * HEAD_DIM, :] = dq.astype(BF16)
-        gqm_ref[h] += dot_nt(queries[h], dpre)
+        gqm_ref[h] += packed_map(dot_nt(queries[h], dpre))
 
     @pl.when(step == blocks - 1)
     def _():
@@ -254,7 +258,7 @@
             lanes = pl.ds(pl.multiple_of((i ^ flip) * half, half), half)
             dkt_ref[:, lanes] = dk[:, WINDOW + i * half : WINDOW + (i + 1) * half]
             dvt_ref[:, lanes] = dv[:, WINDOW + i * half : WINDOW + (i + 1) * half]
-        gkm_ref[0] = dot_nt(kt_ref[...], dpre)
+        gkm_ref[0] = packed_map(dot_nt(kt_ref[...], dpre))
 
 
 def signed_maps(maps):
@@ -333,8 +337,8 @@
             jax.ShapeDtypeStruct(qt.shape, BF16),
             jax.ShapeDtypeStruct((groups * HEAD_DIM, length), BF16),
             jax.ShapeDtypeStruct((groups * HEAD_DIM, length), BF16),
-            jax.ShapeDtypeStruct(qmap.shape, F32),
-            jax.ShapeDtypeStruct(kmap.shape, F32),
+            jax.ShapeDtypeStruct((qmap.shape[0], HEAD_DIM // 2, 2 * HEAD_DIM), F32),
+            jax.ShapeDtypeStruct((kmap.shape[0], HEAD_DIM // 2, 2 * HEAD_DIM), F32),
         ),
         grid_spec=pltpu.PrefetchScalarGridSpec(
             num_scalar_prefetch=1,
@@ -351,8 +355,8 @@
                 local_spec,
                 key_spec,
                 key_spec,
-                pl.BlockSpec((ratio, HEAD_DIM, HEAD_DIM), lambda g, i, *_: (g, 0, 0)),
-                pl.BlockSpec((1, HEAD_DIM, HEAD_DIM), lambda g, i, *_: (g, 0, 0)),
+                pl.BlockSpec((ratio, HEAD_DIM // 2, 2 * HEAD_DIM), lambda g, i, *_: (g, 0, 0)),
+                pl.BlockSpec((1, HEAD_DIM // 2, 2 * HEAD_DIM), lambda g, i, *_: (g, 0, 0)),
             ],
             scratch_shapes=[
                 pltpu.VMEM((2 * HEAD_DIM, padded), BF16),
@@ -531,17 +535,13 @@
     )(inputs, grads, query, key, value, gate, up, down, output, *thin)
 
 
-def hidden_grad_kernel(place_ref, gm_own, go_own, gm_far, go_far, down_own, down_got, out_ref):
-    half = gm_own.shape[0]
-    out_ref[:half] = (
-        dot_nt(gm_own[...], down_own[...]) + dot_nt(go_own[...], down_got[...])
+def hidden_grad_kernel(place_ref, mine, other, down_own, down_got, *refs):
+    refs[-1][...] = (
+        dot_nt(mine[...], down_own[...]) + dot_nt(other[...], down_got[...])
     ).astype(BF16)
-    out_ref[half:] = (
-        dot_nt(gm_far[...], down_own[...]) + dot_nt(go_far[...], down_got[...])
-    ).astype(BF16)
-
-
-def hidden_grad(place, grads, down_weight, down_got):
+
+
+def hidden_grad(index, place, grads, down_weight, down_got, kept):
     half, width = grads[0].shape
     hidden_cols = down_got.shape[0]
     tiles = hidden_cols // MLP_TILE
@@ -551,13 +551,15 @@
         "hidden_grad",
         (tiles,),
         jax.ShapeDtypeStruct((2 * half, hidden_cols), BF16),
-        [whole] * 4
+        [whole] * 2
         + [
             pl.BlockSpec((MLP_TILE, width), lambda i, s: (s[0] * tiles + i, 0)),
             pl.BlockSpec((MLP_TILE, width), lambda i, s: (i, 0)),
-        ],
-        pl.BlockSpec((2 * half, MLP_TILE), lambda i, s: (0, i)),
-    )(place, *grads, down_weight, down_got)
+        ]
+        + [pl.BlockSpec(memory_space=pl.ANY)] * len(kept),
+        pl.BlockSpec((half, MLP_TILE), lambda i, s: (index, i)),
+        aliases={5 + i: i for i in range(len(kept))},
+    )(place, *grads, down_weight, down_got, *kept)
 
 
 def project_kernel(
@@ -978,108 +980,139 @@
     )
 
 
-def finish_kernel(orders, size, *refs):
+def finish_kernel(orders, small_count, joins, *refs):
     count = len(orders)
-    far_ref, small_ref = refs[:2]
-    grads = refs[2 : 2 + count]
-    far_out, small_out = refs[2 + count : 4 + count]
-    outs = refs[4 + count : 4 + 2 * count]
-    small_got, small_sum, send_sem, recv_sem = refs[4 + 2 * count : 8 + 2 * count]
-    buffers = refs[8 + 2 * count :]
-    bits = len(orders[0])
-    row, place = lax.axis_index("row"), lax.axis_index("dp")
+    far_ref, refs = refs[0], refs[1:]
+    smalls, refs = refs[:small_count], refs[small_count:]
+    grads, refs = refs[:count], refs[count:]
+    far_out, refs = refs[0], refs[1:]
+    totals, refs = refs[:small_count], refs[small_count:]
+    joined, refs = refs[: len(joins)], refs[len(joins) :]
+    outs, refs = refs[:count], refs[count:]
+    send_sem, recv_sem = refs[:2]
+    refs = refs[2:]
+    place, col = lax.axis_index("dp"), lax.axis_index("col")
+    bits = max(len(order) for order in orders)
+    small_sums, refs = refs[: small_count * (bits - 1)], refs[small_count * (bits - 1) :]
+    small_gots, buffers = refs[: small_count * bits], refs[small_count * bits :]
 
     barrier = pltpu.get_barrier_semaphore()
-    partners = [{"row": 1 - row}] + [{"dp": place ^ (1 << k)} for k in range(bits)]
+    partners = [{"col": 1 - col}]
+    partners += [{"dp": place ^ (1 << k)} for k in range(bits)]
+    partners.append({"row": 1 - lax.axis_index("row")})
     for partner in partners:
         pl.semaphore_signal(barrier, inc=1, device_id=partner, device_id_type=MESH)
     pl.semaphore_wait(barrier, len(partners))
 
-    def send(source, target, n, partner):
+    started = []
+
+    def send(source, target, partner):
         copy = pltpu.make_async_remote_copy(
             src_ref=source,
             dst_ref=target,
-            send_sem=send_sem.at[n],
-            recv_sem=recv_sem.at[n],
+            send_sem=send_sem.at[len(started)],
+            recv_sem=recv_sem.at[len(started)],
             device_id=partner,
             device_id_type=MESH,
         )
         copy.start()
+        started.append(copy)
         return copy
 
-    waiting = [send(far_ref, far_out, 0, partners[0])]
+    far_copy = send(far_ref, far_out, partners[-1])
     current = list(grads)
-    small_sum[0] = small_ref[...]
+    small_now = list(smalls)
+    used = 0
     for step in range(bits):
-        first = 1 + step * (count + 1)
-        bit = (step + bits - 1) % bits
-        small = send(small_sum.at[step], small_got.at[step], first, partners[1 + bit])
         moving = []
-        for n in range(count):
-            rows = current[n].shape[0] // 2
-            got = buffers[n * (2 * bits - 1) + step]
-            moving.append(
-                send(
-                    current[n].at[pl.ds(rows, rows), :],
-                    got,
-                    first + 1 + n,
-                    partners[1 + orders[n][step]],
+        for n in range(small_count):
+            got = small_gots[n * bits + step]
+            bit = (step + n) % bits
+            moving.append((send(small_now[n], got, partners[1 + bit]), got))
+        halves = {}
+        for n, order in enumerate(orders):
+            if step < len(order):
+                rows = current[n].shape[0] // 2
+                got = buffers[used]
+                used += 1
+                copy = send(
+                    current[n].at[pl.ds(rows, rows), :], got, partners[1 + order[step]]
                 )
-            )
-        small.wait_recv()
-        if step + 1 < bits:
-            small_sum[step + 1] = small_sum[step] + small_got[step]
-        else:
-            small_out[...] = small_sum[step] + small_got[step]
-        for n in range(count):
-            rows = current[n].shape[0] // 2
-            got = buffers[n * (2 * bits - 1) + step]
-            moving[n].wait_recv()
+                halves[n] = (copy, got, rows)
+        for n, (copy, got) in enumerate(moving):
+            copy.wait_recv()
+            target = totals[n] if step + 1 == bits else small_sums[n * (bits - 1) + step]
+            target[...] = small_now[n][...] + got[...]
+            small_now[n] = target
+        if step + 1 == bits:
+            joining = []
+            for out, (source, first, size, columns, axis) in zip(joined, joins):
+                total = totals[source]
+                if axis == 0:
+                    size = total.shape[0]
+                    part, slot = total, out.at[pl.ds(col * size, size)]
+                else:
+                    part = total.at[pl.ds(first, size), pl.ds(*columns)]
+                    slot = out.at[:, pl.ds(pl.multiple_of(col * columns[1], LANES), columns[1])]
+                joining.append(send(part, slot, partners[0]))
+                slot[...] = part[...]
+        for n, (copy, got, rows) in halves.items():
+            copy.wait_recv()
             sums = current[n][:rows].astype(F32) + got[...].astype(F32)
-            if step + 1 < bits:
-                target = buffers[n * (2 * bits - 1) + bits + step]
+            if step + 1 == len(orders[n]):
+                outs[n][...] = sums
+            else:
+                target = buffers[used]
+                used += 1
                 target[...] = sums.astype(BF16)
                 current[n] = target
-            else:
-                outs[n][...] = sums
-        waiting += [small] + moving
-    waiting[0].wait_recv()
-    for copy in waiting:
+    for copy in joining + [far_copy]:
+        copy.wait_recv()
+    for copy in started:
         copy.wait_send()
 
 
-def finish(far, small, grads, orders, size):
-    bits = len(orders[0])
+def finish(far, smalls, joins, grads, orders):
     count = len(grads)
+    bits = max(len(order) for order in orders)
     vmem = pl.BlockSpec(memory_space=pltpu.VMEM)
-    anywhere = pl.BlockSpec(memory_space=pl.ANY)
-    copies = 1 + bits * (count + 1)
-    scratch = [
-        pltpu.VMEM((bits,) + small.shape, F32),
-        pltpu.VMEM((bits,) + small.shape, F32),
-        pltpu.SemaphoreType.DMA((copies,)),
-        pltpu.SemaphoreType.DMA((copies,)),
+    copies = 1 + bits * len(smalls) + len(joins) + sum(len(order) for order in orders)
+    scratch = [pltpu.SemaphoreType.DMA((copies,)), pltpu.SemaphoreType.DMA((copies,))]
+    scratch += [pltpu.VMEM(s.shape, F32) for s in smalls for _ in range(bits - 1)]
+    scratch += [pltpu.VMEM(s.shape, F32) for s in smalls for _ in range(bits)]
+    for step in range(bits):
+        for target in range(2):
+            for grad, order in zip(grads, orders):
+                if step + target < len(order):
+                    rows = grad.shape[0] >> (step + 1)
+                    scratch.append(pltpu.VMEM((rows, grad.shape[1]), BF16))
+    joined = []
+    for source, first, size, columns, axis in joins:
+        shape = smalls[source].shape
+        if axis == 0:
+            joined.append(jax.ShapeDtypeStruct((2 * shape[0],) + shape[1:], F32))
+        else:
+            joined.append(jax.ShapeDtypeStruct((size, 2 * columns[1]), F32))
+    outs = [
+        jax.ShapeDtypeStruct((g.shape[0] >> len(order), g.shape[1]), F32)
+        for g, order in zip(grads, orders)
     ]
-    for grad in grads:
-        rows, columns = grad.shape
-        scratch += [pltpu.VMEM((rows >> (k + 1), columns), BF16) for k in range(bits)]
-        scratch += [pltpu.VMEM((rows >> (k + 1), columns), BF16) for k in range(bits - 1)]
-    return pl.pallas_call(
-        functools.partial(finish_kernel, orders, size),
-        out_shape=(
-            jax.ShapeDtypeStruct(far.shape, far.dtype),
-            jax.ShapeDtypeStruct(small.shape, F32),
-        )
-        + tuple(jax.ShapeDtypeStruct((g.shape[0] // size, g.shape[1]), F32) for g in grads),
-        in_specs=[anywhere, vmem] + [vmem] * count,
-        out_specs=(anywhere, vmem) + (vmem,) * count,
+    totals = [jax.ShapeDtypeStruct(s.shape, F32) for s in smalls]
+    results = pl.pallas_call(
+        functools.partial(finish_kernel, orders, len(smalls), joins),
+        out_shape=(jax.ShapeDtypeStruct(far.shape, far.dtype), *totals, *joined, *outs),
+        in_specs=[pl.BlockSpec(memory_space=pl.ANY)] + [vmem] * (len(smalls) + count),
+        out_specs=(pl.BlockSpec(memory_space=pl.ANY),)
+        + (vmem,) * (len(totals) + len(joined) + count),
         scratch_shapes=scratch,
         compiler_params=pltpu.CompilerParams(
             collective_id=4, has_side_effects=True, vmem_limit_bytes=VMEM_LIMIT
         ),
         cost_estimate=FREE,
         name="finish",
-    )(far, small, *grads)
+    )(far, *smalls, *grads)
+    first, second = 1 + len(smalls), 1 + len(smalls) + len(joins)
+    return results[0], results[1:first], results[first:second], results[second:]
 
 
 def weight_grad_kernel(sets, chunks, pieces, turned, right_turned, place_ref, *refs):
@@ -1148,6 +1181,142 @@
     )(places, *operands, right)
 
 
+def pair_grad_kernel(chunks, merged, *refs):
+    send_buf, own_buf, left_ref, send_sem, recv_sem, local_sem = refs[-6:]
+    outs = refs[-7:-6] if merged else refs[-10:-6]
+    inputs = refs[: -7 if merged else -10]
+    lefts, right_ref = inputs[:-1], inputs[-1]
+    step = pl.program_id(0)
+    tiles, rows, tile = send_buf.shape
+    count = rows // LANES
+    half = rows // 2
+    col = lax.axis_index("col")
+
+    def sent(source, target, n):
+        return pltpu.make_async_remote_copy(
+            src_ref=source,
+            dst_ref=target,
+            send_sem=send_sem.at[n],
+            recv_sem=recv_sem.at[n],
+            device_id={"col": 1 - col},
+            device_id_type=MESH,
+        )
+
+    def columns(index, base):
+        start = index * tile
+        if not isinstance(start, int):
+            start = pl.multiple_of(start, tile)
+        return pl.ds(base + start, tile)
+
+    def copies(index):
+        if merged:
+            (out,) = outs
+            whole = tiles * tile
+            return (
+                [sent(send_buf.at[index], out.at[:, columns(index, whole)], index)],
+                [
+                    pltpu.make_async_copy(
+                        own_buf.at[index], out.at[:, columns(index, 0)], local_sem.at[index]
+                    )
+                ],
+            )
+        got = outs[2:]
+        return [
+            sent(
+                send_buf.at[index, pl.ds(n * half, half), :],
+                got[n].at[:, columns(index, 0)],
+                2 * index + n,
+            )
+            for n in range(2)
+        ], []
+
+    @pl.when(step == 0)
+    def _():
+        barrier = pltpu.get_barrier_semaphore()
+        pl.semaphore_signal(barrier, inc=1, device_id={"col": 1 - col}, device_id_type=MESH)
+        pl.semaphore_wait(barrier, 1)
+        size = left_ref.shape[1] // chunks
+        for p in range(2 * count):
+            for i in range(chunks):
+                left_ref[p * LANES : (p + 1) * LANES, i * size : (i + 1) * size] = jnp.transpose(
+                    lefts[p * chunks + i][...]
+                )
+
+    send_buf[step] = dot_nn(left_ref[rows:, :], right_ref[...]).astype(BF16)
+    away, near = copies(step)
+    for copy in away:
+        copy.start()
+    own = dot_nn(left_ref[:rows, :], right_ref[...]).astype(BF16)
+    if merged:
+        own_buf[step] = own
+        near[0].start()
+    else:
+        outs[0][...] = own[:half]
+        outs[1][...] = own[half:]
+
+    @pl.when(step == tiles - 1)
+    def _():
+        for index in range(tiles):
+            away, near = copies(index)
+            for copy in away + near:
+                copy.wait()
+
+
+def pair_grad(name, collective, lefts, others, right, order, other_order, merged):
+    chunks = len(lefts[0])
+    length = sum(values.shape[0] for values in lefts[0])
+    columns = right.shape[1]
+    tile = min(GRAD_TILE, columns)
+    tiles = columns // tile
+    count = len(order)
+    rows = count * LANES
+    in_specs, operands = [], []
+    for (parts, base), which in ((lefts, order), (others, other_order)):
+        for p in range(count):
+            for values in parts:
+
+                def at(j, base=base, entry=which[p]):
+                    if isinstance(entry, tuple):
+                        return (0, base + (lax.axis_index("dp") ^ entry[0]))
+                    return (0, base + entry)
+
+                in_specs.append(pl.BlockSpec((values.shape[0], LANES), at))
+                operands.append(values)
+    in_specs.append(pl.BlockSpec((length, tile), lambda j: (0, j)))
+    anywhere = pl.BlockSpec(memory_space=pl.ANY)
+    like = lambda *shape: jax.ShapeDtypeStruct(shape, BF16)
+    if merged:
+        out_shape, out_specs = (like(rows, 2 * columns),), (anywhere,)
+    else:
+        out_shape = (like(rows // 2, columns),) * 4
+        near = pl.BlockSpec((rows // 2, tile), lambda j: (0, j))
+        out_specs = (near, near, anywhere, anywhere)
+    transfers = tiles if merged else 2 * tiles
+    return pl.pallas_call(
+        functools.partial(pair_grad_kernel, chunks, merged),
+        grid=(tiles,),
+        out_shape=out_shape,
+        in_specs=in_specs,
+        out_specs=out_specs,
+        scratch_shapes=[
+            pltpu.VMEM((tiles, rows, tile), BF16),
+            pltpu.VMEM((tiles if merged else 1, rows, tile), BF16),
+            pltpu.VMEM((2 * rows, length), BF16),
+            pltpu.SemaphoreType.DMA((transfers,)),
+            pltpu.SemaphoreType.DMA((transfers,)),
+            pltpu.SemaphoreType.DMA((tiles,)),
+        ],
+        compiler_params=pltpu.CompilerParams(
+            dimension_semantics=("arbitrary",),
+            collective_id=collective,
+            has_side_effects=True,
+            vmem_limit_bytes=VMEM_LIMIT,
+        ),
+        cost_estimate=FREE,
+        name=name,
+    )(*operands, right)
+
+
 def first_back_kernel(place_ref, *refs):
     parts, (proj_ref, up_ref, normed_ref) = refs[:6], refs[6:9]
     far_ref, own_ref, turned_ref, adapter_ref, gain_ref = refs[9:]
@@ -1157,7 +1326,7 @@
         turned_ref[:, first : first + source.shape[0]] = jnp.transpose(source[...])
         first += source.shape[0]
     turned = turned_ref[...]
-    adapter_ref[...] = dot_nt(turned, up_ref[...])
+    adapter_ref[...] = dot_nt(up_ref[...], turned)
     sums = dot_nt(turned, proj_ref[...])
     term = jnp.sum(sums * normed_ref[...].astype(F32), axis=0, keepdims=True)
 
@@ -1193,7 +1362,7 @@
             jax.ShapeDtypeStruct((length // 2, half), BF16),
             jax.ShapeDtypeStruct((length // 2, half), F32),
             jax.ShapeDtypeStruct((length, columns), BF16),
-            jax.ShapeDtypeStruct((length, up_native.shape[0]), F32),
+            jax.ShapeDtypeStruct((up_native.shape[0], length), F32),
             jax.ShapeDtypeStruct((1, half), F32),
         ),
         [pl.BlockSpec((values.shape[0], BLOCK), lambda i, s: (0, at(i))) for values in parts]
@@ -1203,7 +1372,7 @@
             pl.BlockSpec((BLOCK, half), lambda i, s: (jnp.minimum(i, middle - 1), 0)),
             pl.BlockSpec((BLOCK, half), lambda i, s: (jnp.maximum(i - middle, 0), 0)),
             pl.BlockSpec((BLOCK, columns), lambda i, s: (at(i), 0)),
-            pl.BlockSpec((BLOCK, up_native.shape[0]), lambda i, s: (at(i), 0)),
+            pl.BlockSpec((up_native.shape[0], BLOCK), lambda i, s: (0, at(i))),
             whole(jnp.zeros((1, half))),
         ],
     )(place, *parts, proj_native, up_native, normed)
@@ -1328,6 +1497,7 @@
     part_cols = query_part + 2 * key_part
     order = exchange_order(bits, 0)
     turned_order = exchange_order(bits, 1)
+    mixed_order = [1, 0] + order[2:]
 
     def other_half(values, axis):
         return jnp.roll(values, values.shape[axis] // 2, axis)
@@ -1465,7 +1635,10 @@
         marks, starts, queries, keys_values, query_map_own, key_map_own
     )
 
-    mixed, grads_far = lax.optimization_barrier((mixed, grads_far))
+    d_hidden = hidden_grad(
+        0, place, (after(grad_out, mixed), grads_other), down_weight, mlp_down_got, ()
+    )
+    mixed, grads_far, _ = lax.optimization_barrier((mixed, grads_far, d_hidden))
     mixed_pair = jnp.concatenate([mixed, swap(mixed, "col")], axis=0)
     adapter_sum = contract(mixed_pair, output_down_native, 0, 0)
     adapter_far = swap(other_half(adapter_sum, 0), "row")
@@ -1481,10 +1654,12 @@
     adapter_padded = jnp.pad(out_adapter, ((0, 0), (0, LANES - rank)))
     attended_other = [swap(attended[0], "col")] + [None] * (blocks - 1)
     d_hidden = hidden_grad(
+        1,
         place,
-        [after(grad_out, *attended, adapter_padded), grads_other, grads_far, grads_far_other],
+        (after(grads_far, *attended, adapter_padded), grads_far_other),
         down_weight,
         mlp_down_got,
+        (d_hidden,),
     )
 
     clock = (d_hidden,)
@@ -1527,48 +1702,55 @@
     def reduction(name, pair, which):
         sums[name] = Reduction(*pair, size, which)
 
-    def given(pair, clock):
-        return [swap(after(values, *clock), "col") for values in pair]
-
     def settle(clock, *names):
         for name in names:
             sums[name].got = after(sums[name].got, *clock)
             clock = (sums[name].combine(),)
         return clock
 
+    def arrived(values, *names):
+        tied = lax.optimization_barrier((values,) + tuple(sums[name].got for name in names))
+        for name, got in zip(names, tied[1:]):
+            sums[name].got = got
+        return tied[0]
+
     def scattered(values):
         return lax.psum_scatter(values, "dp", scatter_dimension=0, tiled=True).astype(F32)
 
-    natural = jnp.stack(
-        [jnp.asarray(v, jnp.int32) for v in [col, row] + 2 * list(range(lane_blocks))]
-    )
-    both = [([second_normed], 0), ([second_normed], lane_blocks)]
-
-    def up_grads(right):
-        own, other = both
-        if not direct:
-            columns = second_normed[:, feature_cols:]
-            other = ([jnp.concatenate(
-                [second_normed[:, :feature_cols], relative_blocks(columns, 1, device, order)], axis=1
-            )], lane_blocks)
-        entries = [col, row] + list(range(lane_blocks)) + block_order(order)
-        table = jnp.stack([jnp.asarray(v, jnp.int32) for v in entries])
-        outs = weight_grad(table, [own, other], right, 1)
-        half = feature_cols // 2
-        return outs[0], (outs[1][:half], outs[1][half:])
-
-    own_gate, other_gate = weight_grad(natural, both, d_gate, 1)
-    grad_gate_own = scattered(own_gate)
-    got_gate = swap(other_gate, "col")
-    own_down, other_down = grads_of(
-        [([grad_out, grads_far], 0), ([grads_other, grads_far_other], 0)],
-        after(hidden, own_gate),
-        (order, turned_order),
-    )
+    in_order = list(range(lane_blocks))
+
+    def relative(which):
+        return [(relative_index(p, which),) for p in range(size)] if direct else in_order
+
+    def arranged(parts, which):
+        if direct:
+            return parts
+        return [relative_blocks(values, 1, device, which) for values in parts]
+
+    (gate_pair,) = pair_grad(
+        "gate_grad",
+        5,
+        ([second_normed], 0),
+        ([second_normed], lane_blocks),
+        d_gate,
+        in_order,
+        in_order,
+        True,
+    )
+    grad_gate_pair = scattered(gate_pair)
+    down_outs = pair_grad(
+        "down_grad",
+        6,
+        (arranged([grad_out, grads_far], order), 0),
+        (arranged([grads_other, grads_far_other], turned_order), 0),
+        after(hidden, gate_pair),
+        relative(order),
+        relative(turned_order),
+        False,
+    )
+    own_down = down_outs[:2]
     reduction("down_own", own_down, order)
-    down_given = given(other_down, ())
-
-    reduction("down_got", down_given, turned_order)
+    reduction("down_got", down_outs[2:], turned_order)
     chip_far = second_grad(
         1, after(d_gate, own_down[0]), d_up, gate_weight, gate_got, up_weight, up_got
     )
@@ -1577,11 +1759,17 @@
         0, after(d_gate, chip_far), d_up, gate_weight, gate_got, up_weight, up_got
     )
     far_got_far = swap(chip_own, "row")
-    grad_gate_got = scattered(after(got_gate, chip_own))
-    own_up, other_up = up_grads(after(d_up, chip_own))
-    got_up = given(other_up, ())
-    y_chip = down_product(after(hidden, own_up), down_weight, mlp_down_got)
-    reduction("up_got", [after(v, y_chip) for v in got_up], order)
+    (up_pair,) = pair_grad(
+        "up_grad",
+        7,
+        ([second_normed], 0),
+        ([second_normed], lane_blocks),
+        after(d_up, chip_own),
+        in_order,
+        in_order,
+        True,
+    )
+    y_chip = down_product(after(hidden, up_pair), down_weight, mlp_down_got)
     clock = settle((y_chip,), "down_own", "down_got")
 
     totals = []
@@ -1610,11 +1798,11 @@
 
     outs = back(0, (grad_out, grads_other), ())
     kept, gain_sum, grad_state = outs[:3], outs[3], outs[4]
-    grad_up_own = scattered(after(own_up, kept[0]))
+    grad_up_pair = scattered(after(up_pair, kept[0]))
     outs = back(1, (grads_far, grads_far_other), kept)
     kept = outs[:3]
     d_mixed, d_mine, d_out_padded = kept
-    grad_second_gain = (gain_sum + outs[3])[0]
+    grad_second_gain = gain_sum + outs[3]
     d_out_adapter = d_out_padded[:, :rank]
     y_far = swap(after(y_chip, kept[0])[half_rows:], "row")
     grad_output_up = contract(out_adapter, d_mine, 0, 0)
@@ -1630,7 +1818,7 @@
         True,
     )
     reduction("output", output_pair, order)
-    clock = settle((output_pair[0],), "down_own", "down_got", "up_got")
+    clock = (output_pair[0],)
 
     d_queries, d_keys, d_values, grad_query_map, grad_key_map = attention_backward(
         marks,
@@ -1644,50 +1832,67 @@
         inverse,
     )
 
+    d_queries = arrived(d_queries, "output", "down_own", "down_got")
+    d_keys, d_values, _ = lax.optimization_barrier((d_keys, d_values, d_queries))
     d_parts = (d_queries, d_keys, d_values)
     d_parts += tuple(swap(values, "col") for values in d_parts)
-    clock = settle((d_queries,), "down_own", "down_got", "up_got", "output")
+    clock = tuple(sums[name].combine() for name in ("output", "down_own", "down_got"))
     d_first_far, d_first, d_turned, adapter_sum, gain_term = first_back(
         place, (after(d_queries, y_far, *clock),) + d_parts[1:], proj_native, up_native, normed_first
     )
-    adapter_far = swap(other_half(adapter_sum, 0), "row")
+    adapter_far = swap(other_half(adapter_sum, 1), "row")
     gain_far = swap(gain_term, "row")
     (proj_a,) = grads_of([([normed_first], 0)], d_turned, (order,), False, (0, 2), 1)
     (proj_b,) = grads_of(
-        [([normed_first], 0)], after(d_turned, proj_a[0]), (turned_order,), False, (1, 2), 1
+        [([normed_first], 0)], after(d_turned, proj_a[0]), (mixed_order,), False, (1, 2), 1
     )
     adapter_far, gain_far, _ = lax.optimization_barrier((adapter_far, gain_far, proj_b[0]))
-    gain_term = (gain_term + gain_far)[0]
     d_adapter = (adapter_sum + adapter_far).astype(BF16)
-    grad_down = contract(d_adapter, normed_first[:, :feature_cols], 0, 0)
+    grad_down = contract(d_adapter, normed_first[:, :feature_cols], 1, 0)[: 3 * rank]
     grad_up = contract(adapters, d_turned[:, :part_cols], 0, 0)
-    down_term = jnp.sum(thin[: 3 * rank].astype(F32) * grad_down[: 3 * rank], axis=0)
-    grad_first_gain = (gain_term + down_term) / first_gain
-    grad_down = grad_down[: 3 * rank]
-    small = (
-        grad_first_gain,
-        grad_second_gain,
-        grad_output_up,
-        grad_down,
-        grad_output_down,
-        grad_up[:rank, :query_part],
-        grad_up[rank : 2 * rank, query_part : query_part + key_part],
-        grad_up[2 * rank : 3 * rank, query_part + key_part :],
-        grad_query_map,
-        grad_key_map,
-    )
-    flat = [values.reshape(-1, LANES) for values in small]
-    result = (
-        state + y_chip[:half_rows].astype(F32) + y_far.astype(F32)
-    ).astype(BF16)
-    d_first = d_first + contract(d_adapter[:half_rows], thin, 1, 0)
-    packed = after(jnp.concatenate(flat, axis=0), result, d_first)
-    clock = settle((packed,), "up_got", "output")
-    d_first_far, packed, grad_proj_a, grad_proj_b = finish(
-        after(d_first_far, *clock), packed, (proj_a[0], proj_b[0]), (order, turned_order), size
-    )
-    shared_rows = sum(values.shape[0] for values in flat[:4])
-    packed_other = swap(packed[shared_rows:], "col")
+    grad_up = jnp.concatenate(
+        [
+            grad_up[n * rank : (n + 1) * rank, first : first + count]
+            for n, (first, count) in enumerate(
+                ((0, query_part), (query_part, key_part), (query_part + key_part, key_part))
+            )
+        ],
+        axis=1,
+    )
+    down_term = jnp.sum(thin[: 3 * rank].astype(F32) * grad_down, axis=0, keepdims=True)
+    grad_first_gain = (gain_term + gain_far + down_term) / first_gain[None]
+    result = (state + y_chip[:half_rows].astype(F32) + y_far.astype(F32)).astype(BF16)
+
+    def sides(pair):
+        half = pair.shape[1] // 2
+        return ordered(pair[:, :half], pair[:, half:], col, 1)
+
+    grad_gate = sides(grad_gate_pair)
+    clock = settle((grad_up, result, grad_gate), "output", "down_own", "down_got")
+    d_first = d_first + contract(d_adapter[:, :half_rows], thin, 0, 0)
+    d_first_far, totals, joined, reduced = finish(
+        after(d_first_far, *clock),
+        (
+            after(grad_first_gain, d_first),
+            grad_second_gain,
+            grad_output_up,
+            grad_down,
+            grad_output_down,
+            grad_up,
+            grad_query_map,
+            grad_key_map,
+        ),
+        (
+            (5, 0, rank, (0, query_part), 1),
+            (5, 0, rank, (query_part, key_part), 1),
+            (5, 0, rank, (query_part + key_part, key_part), 1),
+            (6, 0, 0, (), 0),
+            (7, 0, 0, (), 0),
+            (4, 0, rank, (0, query_part), 1),
+        ),
+        (proj_a[0], proj_b[0]),
+        (order, mixed_order),
+    )
     d_first = d_first + d_first_far.astype(F32)
     first_scale = first_scale[:half_rows]
     hat_own = activations.astype(F32) * first_scale
@@ -1695,20 +1900,16 @@
     inner = jnp.sum(grad_hat * hat_own, axis=1)
     inner = ((inner + swap(inner, "col")) / width)[:, None]
     grad_activations = grad_state + first_scale * (grad_hat - hat_own * inner)
-    clock = (packed,)
-    while any(not sums[name].done for name in FINISH_ORDER):
-        clock = settle(clock, *(name for name in FINISH_ORDER if not sums[name].done))
-
-    def unpacked(index, source, base):
-        first = sum(values.shape[0] for values in flat[:index]) - base
-        return source[first : first + flat[index].shape[0]].reshape(small[index].shape)
-
-    def joined(index, axis):
-        return ordered(
-            unpacked(index, packed, 0), unpacked(index, packed_other, shared_rows), col, axis
-        )
-
-    down_total = jnp.transpose(unpacked(3, packed, 0))
+    grad_proj_a, grad_proj_b = reduced
+    clock = (totals[0],)
+    while any(not item.done for item in sums.values()):
+        clock = settle(clock, *(name for name, item in sums.items() if not item.done))
+    down_total = jnp.transpose(totals[3])
+
+    def unpacked_maps(maps):
+        half = maps.shape[2] // 2
+        return jnp.concatenate([maps[:, :, :half], maps[:, :, half:]], axis=1)
+
     proj_grads = [
         ordered(
             grad_proj_a[:, first : first + count],
@@ -1723,28 +1924,27 @@
         )
     ]
 
-    grad_gate = ordered(grad_gate_own, grad_gate_got, col, 1)
-    grad_up_weight = ordered(grad_up_own, sums["up_got"].keep, col, 1)
+    grad_up_weight = sides(grad_up_pair)
     grad_down_weight = ordered(sums["down_own"].keep, sums["down_got"].keep, col, 1)
     return (
         result,
         grad_activations,
-        unpacked(0, packed, 0),
+        totals[0][0],
         proj_grads[0],
         proj_grads[1],
         proj_grads[2],
         down_total[:, :rank],
-        joined(5, 1),
+        joined[0],
         down_total[:, rank : 2 * rank],
-        joined(6, 1),
-        down_total[:, 2 * rank :],
-        joined(7, 1),
-        joined(8, 0),
-        joined(9, 0),
+        joined[1],
+        down_total[:, 2 * rank : 3 * rank],
+        joined[2],
+        unpacked_maps(joined[3]),
+        unpacked_maps(joined[4]),
         sums["output"].keep,
-        jnp.transpose(joined(4, 1)),
-        unpacked(2, packed, 0),
-        unpacked(1, packed, 0),
+        jnp.transpose(joined[5]),
+        totals[2],
+        totals[1][0],
         grad_gate,
         grad_up_weight,
         jnp.transpose(grad_down_weight),

time: 812 us -> 758 us (0.933)
  waiting for transfers between devices: 63.2 us -> 14.4 us
  Pallas kernels: 531 us -> 570 us
  other arithmetic: 80.5 us -> 58.8 us
  local copies, waits for them, and re-layouts: 56.5 us -> 36.8 us
    pallas_call x1 -> x4, Pallas kernels: 77.1 us -> 191 us  [the longest x1 108 us: finish(): pl.pallas_call(functools.partial(finish_kernel, orders, len(smalls), join...]
    pallas_call x6 -> x3, Pallas kernels: 111 us -> 30.7 us  [weight_grad(): grid_call(functools.partial(weight_grad_kernel, len(sets), chunks, pieces...]
    ppermute x12 -> x9, waiting for transfers between devices: 32 us -> 0.03 us  [launch(): lax.ppermute(send, 'dp', [(i, i ^ bit) for i in range(self.size)])]
    ppermute x35 -> x29, waiting for transfers between devices: 31.1 us -> 14.4 us  [swap(): return lax.ppermute(values, axis, [(0, 1), (1, 0)])]
    convert_element_type x8 -> x6, other arithmetic: 25.2 us -> 13.3 us  [combine(): (self.keep[rows].astype(F32) + got[rows].astype(F32)).astype(BF16)]
    reshape x17 -> x0, local copies, waits for them, and re-layouts: 9.63 us -> none  [the longest x11 6.07 us: unpacked(): source[first:first + flat[index].shape[0]].reshape(small[index].shape)]
    slice x12 -> x7, local copies, waits for them, and re-layouts: 12.5 us -> 3.89 us  [the longest x2 3.03 us: sides(): return ordered(pair[:, :half], pair[:, half:], col, 1)]
    unnamed x235 -> x232, local copies, waits for them, and re-layouts: 13.7 us -> 19.4 us
  transfers between devices with their start and end apart: 50 -> 40, of which waited for: 13 -> 11; matrix products, arithmetic and copies ran while one was open for 18% -> 13% of each run, Pallas kernels for 60% -> 70%
where the time goes in v3:
time: 758 us; the launch traced here: 749 us
  Pallas kernels  570 us (75%)
  other arithmetic  58.8 us (8%)
  local copies, waits for them, and re-layouts  36.8 us (5%)
  starting transfers between devices  30.9 us (4%)
  matrix products  22.4 us (3%)
  between operations  16.1 us (2%)
  waiting for transfers between devices  14.4 us (2%)
    pallas_call x1, Pallas kernels, finish(): pl.pallas_call(functools.partial(finish_kernel, orders, len(smalls), join...  108 us
    pallas_call x3, Pallas kernels, pair_grad(): pl.pallas_call(functools.partial(pair_grad_kernel, chunks, merged), grid=...  82.2 us
    pallas_call x3, Pallas kernels, pair_sum(): pl.pallas_call(functools.partial(pair_sum_kernel, products), grid=(2 * ti...  81.1 us
    pallas_call x4, Pallas kernels, mlp_block(): grid_call(functools.partial(mlp_kernel, len(shapes)), 'mlp_block', (tiles...  81 us
    pallas_call x1, Pallas kernels, attention_backward(): pl.pallas_call(backward_kernel, out_shape=(jax.ShapeDtypeStruct(qt.shape,...  44.1 us
    pallas_call x3, Pallas kernels, weight_grad(): grid_call(functools.partial(weight_grad_kernel, len(sets), chunks, pieces...  30.7 us
    pallas_call x1, Pallas kernels, exchange(): pl.pallas_call(functools.partial(exchange_kernel, query_cols, key_cols),...  29.7 us
    pallas_call x2, Pallas kernels, hidden_grad(): grid_call(hidden_grad_kernel, 'hidden_grad', (tiles,), jax.ShapeDtypeStru...  28.7 us
  transfers between devices with their start and end apart: 40, of which 11 were waited for; matrix products, arithmetic and copies ran while one was open for 13% of the time, Pallas kernels for 70%

profile of v3, /device:TPU:0, one launch (start us, length us, event | category | flops | bytes accessed | tf_op | source)
XLA Modules:
  0.0 749.1 jit_solution(13960202507398881650)
XLA Ops:
  7.2 3.0 collective-permute-start
  13.0 29.7 %exchange.1 = (bf16[1024,1024]{1,0:T(8,128)(2,1)}, bf16[1024,1024]{1,0:T(8,128)(2,1)}, bf16[1024,768]{1,0:T(8,128)(2,1)}, bf16[1024,2048]{1,0:T(8,128)(2,1)}, bf...) custom-call(bf16[1024,1024]{1,0:T(8,128)(2,1)} %in_mine.3, ...), custom_call_target="tpu_custom_call" | custom-call | flops 1000 | bytes 1000 | tf_op jit(solution)/shard_map/exchange/pallas_call | solution.py:518
  45.2 10.5 %project_block.2 = (bf16[2048,2048]{1,0:T(8,128)(2,1)}, bf16[512,2048]{1,0:T(8,128)(2,1)}, bf16[256,2048]{1,0:T(8,128)(2,1)}, bf16[2048,32]{1,0:T(8,128)(2,1)}, f32[2048,1]{1,0:T(8,128)}) custom-call(s32[10]{0:T(128)} %stack.105.place_ref, bf16[1024,1024]{1,0:T(8,128)(2,1)} %in_mine.3, bf16[1024,1024]{1,0:T(8,128)(2,1)} %get-tuple-element.158.other_ref.in_other, ...), custom_call_target="tpu_custom_call" | custom-call | flops 1000 | bytes 1000 | tf_op jit(solution)/shard_map/project_block/pallas_call | solution.py:620
  61.8 10.4 %project_block.3 = (bf16[2048,2048]{1,0:T(8,128)(2,1)}, bf16[512,2048]{1,0:T(8,128)(2,1)}, bf16[256,2048]{1,0:T(8,128)(2,1)}, bf16[2048,32]{1,0:T(8,128)(2,1)}, f32[2048,1]{1,0:T(8,128)}) custom-call(s32[10]{0:T(128)} %stack.105.place_ref, ...), custom_call_target="tpu_custom_call", output_to_operand_aliasing={{0}: (10, {}), {1}: (11, {}), {2}: (12, {}), {3}: (13, {}),... | custom-call | flops 1000 | bytes 1000 | tf_op jit(solution)/shard_map/project_block/pallas_call | solution.py:620
  74.1 19.4 %attention_forward.1 = (bf16[512,2048]{1,0:T(8,128)(2,1)S(1)}, f32[2,4,2048]{2,1,0:T(4,128)S(1)}) custom-call(s32[6]{0:T(128)S(1)} %pad_add_fusion.mark_ref, s32[1,1,2048]{2,1,0:T(1,128)S(1)} %bitcast.47, bf16[512,2048]{1,0:T(8,128)(2,1)S(1)} %copy-done.2, bf16[256,2176]{1,0:T(8,128)(2,1)S(1)} %pad.18.kt_ref.vt_ref, ...), custom_call_target="tpu_custom_call" | custom-call | flops 1000 | bytes 1000 | tf_op jit(solution)/shard_map/attention_forward/pallas_call | solution.py:293
  93.6 14.4 %hidden_grad.2.refs_0_ = bf16[2048,2048]{1,0:T(8,128)(2,1)} custom-call(s32[10]{0:T(128)} %stack.105.place_ref, bf16[1024,1024]{1,0:T(8,128)(2,1)} %grad_mine.1, bf16[1024,1024]{1,0:T(8,128)(2,1)} %get-tuple-element.174.other.refs_16_.refs_18_.refs_20_.refs_22_.refs_24_.refs_26_.refs_28_.refs_30_.grad_other, bf16[4096,1024]{1,0:T(8,128)(2,1)} %refs_1_.3, ...), custom_call_target="tpu_custom_call" | custom-call | flops 1000 | bytes 1000 | tf_op jit(solution)/shard_map/hidden_grad/pallas_call | solution.py:549
  108.8 3.9 collective-permute-done.3
  116.1 2.3 convolution_convert_fusion.3.at_mine
  119.7 2.3 convolution_convert_fusion.2.at_mine
  124.3 2.3 convolution_convert_fusion.at_mine
  129.2 14.3 %hidden_grad.3.dh_ref = bf16[2048,2048]{1,0:T(8,128)(2,1)} custom-call(s32[10]{0:T(128)} %stack.105.place_ref, bf16[1024,1024]{1,0:T(8,128)(2,1)} %collective-permute-done.2.mine.refs_1_.refs_3_.refs_5_.refs_7_.refs_9_.refs_11_.refs_13_.refs_15_.grad_mine, bf16[1024,1024]{1,0:T(8,128)(2,1)} %copy-done.24, ...), custom_call_target="tpu_custom_call", output_to_operand_aliasing={{}: (5, {})} | custom-call | flops 1000 | bytes 1000 | tf_op jit(solution)/shard_map/hidden_grad/pallas_call | solution.py:549
  148.7 20.3 %mlp_block.4 = (bf16[2048,2048]{1,0:T(8,128)(2,1)}, bf16[2048,2048]{1,0:T(8,128)(2,1)}, bf16[2048,2048]{1,0:T(8,128)(2,1)}, bf16[2048,2048]{1,0:T(8,128)(2,1)}, f32[2048,1]{1,0:T(8,128)}, /*index=5*/f32[1024,1024]{1,0:T(8,128)}) custom-call(s32[10]{0:T(128)} %stack.105.place_ref, bf16[1024,1024]{1,0:T(8,128)(2,1)} %in_mine.3, ...), custom_call_target="tpu_custom_call" | custom-call | flops 1000 | bytes 1000 | tf_op jit(solution)/shard_map/mlp_block/pallas_call | solution.py:743
  173.2 21.3 %mlp_block.5 = (bf16[2048,2048]{1,0:T(8,128)(2,1)}, bf16[2048,2048]{1,0:T(8,128)(2,1)}, bf16[2048,2048]{1,0:T(8,128)(2,1)}, bf16[2048,2048]{1,0:T(8,128)(2,1)}, f32[2048,1]{1,0:T(8,128)}, /*index=5*/f32[1024,1024]{1,0:T(8,128)}) custom-call(s32[10]{0:T(128)} %stack.105.place_ref, ...), custom_call_target="tpu_custom_call", output_to_operand_aliasing={{0}: (15, {}), {1}: (16, {}), {2}: (17, {}), {3}: (18, {}),... | custom-call | flops 1000 | bytes 1000 | tf_op jit(solution)/shard_map/mlp_block/pallas_call | solution.py:743
  198.9 19.7 %mlp_block.6 = (bf16[2048,2048]{1,0:T(8,128)(2,1)}, bf16[2048,2048]{1,0:T(8,128)(2,1)}, bf16[2048,2048]{1,0:T(8,128)(2,1)}, bf16[2048,2048]{1,0:T(8,128)(2,1)}, f32[2048,1]{1,0:T(8,128)}) custom-call(s32[10]{0:T(128)} %stack.105.place_ref, ...), custom_call_target="tpu_custom_call", output_to_operand_aliasing={{0}: (15, {}), {1}: (16, {}), {2}: (17, {}), {3}: (18, {}),... | custom-call | flops 1000 | bytes 1000 | tf_op jit(solution)/shard_map/mlp_block/pallas_call | solution.py:743
  220.9 2.6 collective-permute-done.17.far_other
  224.5 19.7 %mlp_block.7 = (bf16[2048,2048]{1,0:T(8,128)(2,1)}, bf16[2048,2048]{1,0:T(8,128)(2,1)}, bf16[2048,2048]{1,0:T(8,128)(2,1)}, bf16[2048,2048]{1,0:T(8,128)(2,1)}, f32[2048,1]{1,0:T(8,128)}) custom-call(s32[10]{0:T(128)} %stack.105.place_ref, ...), custom_call_target="tpu_custom_call", output_to_operand_aliasing={{0}: (15, {}), {1}: (16, {}), {2}: (17, {}), {3}: (18, {}),... | custom-call | flops 1000 | bytes 1000 | tf_op jit(solution)/shard_map/mlp_block/pallas_call | solution.py:743
  244.3 26.5 %gate_grad.1 = bf16[1024,4096]{1,0:T(8,128)(2,1)} custom-call(bf16[2048,2048]{1,0:T(8,128)(2,1)} %get-tuple-element.216.refs_0_.refs_1_.refs_2_.refs_3_.refs_4_.refs_5_.refs_6_.refs_7_.refs_8_.refs_9_.refs_10_.refs_11_.refs_12_.refs_13_.refs_14_.refs_15_.normed_ref, ...), custom_call_target="tpu_custom_call" | custom-call | flops 1000 | bytes 1000 | tf_op jit(solution)/shard_map/gate_grad/pallas_call | solution.py:1295
  270.9 29.2 %down_grad.1 = (bf16[512,2048]{1,0:T(8,128)(2,1)}, bf16[512,2048]{1,0:T(8,128)(2,1)}, bf16[512,2048]{1,0:T(8,128)(2,1)}, bf16[512,2048]{1,0:T(8,128)(2,1)}) custom-call(bf16[1024,1024]{1,0:T(8,128)(2,1)} %grad_mine.1, bf16[1024,1024]{1,0:T(8,128)(2,1)} %collective-permute-done.2.mine.refs_1_.refs_3_.refs_5_.refs_7_.refs_9_.refs_11_.refs_13_.refs_15_.grad_mine, ...), custom_call_target="tpu_custom_call" | custom-call | flops 1000 | bytes 1000 | tf_op jit(solution)/shard_map/down_grad/pallas_call | solution.py:1295
  303.3 26.0 %second_grad.2 = bf16[1024,1024]{1,0:T(8,128)(2,1)} custom-call(bf16[2048,2048]{1,0:T(8,128)(2,1)} %get-tuple-element.222.refs_16_.refs_0_, bf16[2048,2048]{1,0:T(8,128)(2,1)} %get-tuple-element.223.refs_1_.refs_16_, bf16[1024,4096]{1,0:T(8,128)(2,1)} %refs_2_.7, bf16[1024,2048]{1,0:T(8,128)(2,1)} %get-tuple-element.189.gate_got.refs_3_, ...), custom_call_target="tpu_custom_call" | custom-call | flops 1000 | bytes 1000 | tf_op jit(solution)/shard_map/second_grad/pallas_call | solution.py:905
  330.6 26.5 %second_grad.3 = bf16[1024,1024]{1,0:T(8,128)(2,1)} custom-call(bf16[2048,2048]{1,0:T(8,128)(2,1)} %get-tuple-element.222.refs_16_.refs_0_, bf16[2048,2048]{1,0:T(8,128)(2,1)} %get-tuple-element.223.refs_1_.refs_16_, bf16[1024,4096]{1,0:T(8,128)(2,1)} %refs_2_.7, bf16[1024,2048]{1,0:T(8,128)(2,1)} %get-tuple-element.189.gate_got.refs_3_, ...), custom_call_target="tpu_custom_call" | custom-call | flops 1000 | bytes 1000 | tf_op jit(solution)/shard_map/second_grad/pallas_call | solution.py:905
  358.0 26.4 %up_grad.1 = bf16[1024,4096]{1,0:T(8,128)(2,1)} custom-call(bf16[2048,2048]{1,0:T(8,128)(2,1)} %get-tuple-element.216.refs_0_.refs_1_.refs_2_.refs_3_.refs_4_.refs_5_.refs_6_.refs_7_.refs_8_.refs_9_.refs_10_.refs_11_.refs_12_.refs_13_.refs_14_.refs_15_.normed_ref, ...), custom_call_target="tpu_custom_call" | custom-call | flops 1000 | bytes 1000 | tf_op jit(solution)/shard_map/up_grad/pallas_call | solution.py:1295
  384.4 28.6 %down_product.1 = bf16[2048,1024]{1,0:T(8,128)(2,1)} custom-call(bf16[2048,2048]{1,0:T(8,128)(2,1)} %get-tuple-element.224.refs_32_.refs_0_, bf16[4096,1024]{1,0:T(8,128)(2,1)} %refs_1_.3, bf16[2048,1024]{1,0:T(8,128)(2,1)} %get-tuple-element.175.down_got.refs_2_), custom_call_target="tpu_custom_call" | custom-call | flops 1000 | bytes 1000 | tf_op jit(solution)/shard_map/down_product/pallas_call | solution.py:905
  413.1 3.6 add_convert_fusion.4
  418.8 4.0 add_convert_fusion.2.total_mine
  422.8 2.6 add_convert_fusion.1.total_mine
  426.6 2.3 constant_dynamic-slice_fusion.3.out_own
  429.9 13.8 %norm_back.2 = (bf16[512,2048]{1,0:T(8,128)(2,1)}, bf16[2048,1024]{1,0:T(8,128)(2,1)}, bf16[2048,128]{1,0:T(8,128)(2,1)}, f32[1,1024]{1,0:T(1,128)}, f32[1024,1024]{1,0:T(8,128)}) custom-call(s32[10]{0:T(128)} %stack.105.place_ref, bf16[1024,1024]{1,0:T(8,128)(2,1)} %add_convert_fusion.2.total_mine, bf16[1024,1024]{1,0:T(8,128)(2,1)} %collective-permute-done.23.total_other, ...), custom_call_target="tpu_custom_call" | custom-call | flops 1000 | bytes 1000 | tf_op jit(solution)/shard_map/norm_back/pallas_call | solution.py:848
  445.4 2.6 collective-permute-start.27
  448.2 13.0 %norm_back.3 = (bf16[512,2048]{1,0:T(8,128)(2,1)}, bf16[2048,1024]{1,0:T(8,128)(2,1)}, bf16[2048,128]{1,0:T(8,128)(2,1)}, f32[1,1024]{1,0:T(1,128)}) custom-call(s32[10]{0:T(128)} %stack.105.place_ref, bf16[1024,1024]{1,0:T(8,128)(2,1)} %copy-done.33, ...), custom_call_target="tpu_custom_call", output_to_operand_aliasing={{0}: (12, {}), {1}: (13, {}), {2}: (14, {})} | custom-call | flops 1000 | bytes 1000 | tf_op jit(solution)/shard_map/norm_back/pallas_call | solution.py:848
  461.2 2.4 fusion.12.refs_5_
  463.6 3.5 fusion.39.refs_3_
  467.1 9.9 %weight_grad.3 = (bf16[512,1024]{1,0:T(8,128)(2,1)}, bf16[512,1024]{1,0:T(8,128)(2,1)}) custom-call(s32[10]{0:T(128)} %stack.117.place_ref, bf16[1024,2048]{1,0:T(8,128)(2,1)} %copy-done.22, bf16[1024,2048]{1,0:T(8,128)(2,1)} %copy-done.22, bf16[1024,2048]{1,0:T(8,128)(2,1)} %copy-done.22, bf16[1024,2048]{1,0:T(8,128)(2,1)} %copy-done.22, ...), custom_call_target="tpu_custom_call" | custom-call | flops 1000 | bytes 1000 | tf_op jit(solution)/shard_map/weight_grad/pallas_call | solution.py:1173
  481.3 44.1 %attention_backward.1 = (bf16[512,2048]{1,0:T(8,128)(2,1)S(1)}, bf16[128,2048]{1,0:T(8,128)(2,1)S(1)}, bf16[128,2048]{1,0:T(8,128)(2,1)S(1)}, f32[8,32,128]{2,1,0:T(8,128)S(1)}, f32[2,32,128]{2,1,0:T(8,128)S(1)}) custom-call(s32[6]{0:T(128)S(1)} %copy-done.21, s32[1,1,2048]{2,1,0:T(1,128)S(1)} %bitcast.48, bf16[512,2048]{1,0:T(8,128)(2,1)} %get-tuple-element.169.qt_ref, ...), custom_call_target="tpu_custom_call" | custom-call | flops 1000 | bytes 1000 | tf_op jit(solution)/shard_map/attention_backward/pallas_call | solution.py:334
  527.7 2.6 add_convert_fusion.8
  530.3 2.6 add_convert_fusion.9
  535.8 2.7 collective-permute-start.34
  538.4 4.2 add_convert_fusion
  544.8 16.5 %first_back.1 = (bf16[1024,1024]{1,0:T(8,128)(2,1)}, f32[1024,1024]{1,0:T(8,128)}, bf16[2048,1536]{1,0:T(8,128)(2,1)}, f32[32,2048]{1,0:T(8,128)}, f32[1,1024]{1,0:T(1,128)}) custom-call(s32[10]{0:T(128)} %stack.105.place_ref, bf16[512,2048]{1,0:T(8,128)(2,1)} %copy-done.7, bf16[128,2048]{1,0:T(8,128)(2,1)} %copy-done.12, bf16[128,2048]{1,0:T(8,128)(2,1)} %copy-done.13, ...), custom_call_target="tpu_custom_call" | custom-call | flops 1000 | bytes 1000 | tf_op jit(solution)/shard_map/first_back/pallas_call | solution.py:1357
  564.4 2.5 fusion.2
  567.6 10.5 %weight_grad.4.refs_9_ = bf16[1024,768]{1,0:T(8,128)(2,1)} custom-call(s32[10]{0:T(128)} %stack.105.place_ref, bf16[2048,2048]{1,0:T(8,128)(2,1)} %get-tuple-element.261.refs_8_.refs_0_.refs_1_.refs_2_.refs_3_.refs_4_.refs_5_.refs_6_.refs_7_, bf16[2048,2048]{1,0:T(8,128)(2,1)} %get-tuple-element.261.refs_8_.refs_0_.refs_1_.refs_2_.refs_3_.refs_4_.refs_5_.refs_6_.refs_7_, ...), custom_call_target="tpu_custom_call" | custom-call | flops 1000 | bytes 1000 | tf_op jit(solution)/shard_map/weight_grad/pallas_call | solution.py:1173
  578.1 10.4 %weight_grad.5.refs_10_ = bf16[1024,768]{1,0:T(8,128)(2,1)} custom-call(s32[10]{0:T(128)} %stack.118.place_ref, bf16[2048,2048]{1,0:T(8,128)(2,1)} %get-tuple-element.261.refs_8_.refs_0_.refs_1_.refs_2_.refs_3_.refs_4_.refs_5_.refs_6_.refs_7_, bf16[2048,2048]{1,0:T(8,128)(2,1)} %get-tuple-element.261.refs_8_.refs_0_.refs_1_.refs_2_.refs_3_.refs_4_.refs_5_.refs_6_.refs_7_, ...), custom_call_target="tpu_custom_call" | custom-call | flops 1000 | bytes 1000 | tf_op jit(solution)/shard_map/weight_grad/pallas_call | solution.py:1173
  590.7 2.9 add.215
  593.7 3.5 multiply_reduce_fusion.1
  603.8 2.3 convert_add_fusion
  606.1 108.4 %finish.1 = (bf16[1024,1024]{1,0:T(8,128)(2,1)}, f32[1,1024]{1,0:T(1,128)}, f32[1,1024]{1,0:T(1,128)}, f32[8,1024]{1,0:T(8,128)}, f32[24,1024]{1,0:T(8,128)}, /*...) custom-call(bf16[1024,1024]{1,0:T(8,128)(2,1)} %get-tuple-element.27, ...), custom_call_target="tpu_custom_call" | custom-call | flops 1000 | bytes 1000 | tf_op jit(solution)/shard_map/finish/pallas_call | solution.py:1101
  714.6 2.8 multiply_reduce_fusion
  723.7 2.9 copy.118
  726.6 6.1 multiply_add_fusion
  (379 shorter events, 91.0 us)
Async XLA Ops:
  7.2 590.6 %reduce-scatter.3.cloned.1.call-start = ((), (), s32[]{:S(2)}) async-start(), calls=%async_computation.2 | async-start | bytes 9437184 | tf_op jit(solution)/shard_map/reduce_scatter | solution.py:1718
  7.2 49.0 %collective-permute-start = (bf16[1024,1024]{1,0:T(8,128)(2,1)}, bf16[1024,1024]{1,0:T(8,128)(2,1)}, u32[]{:S(2)}, u32[]{:S(2)}) collective-permute-start(bf16[1024,1024]{1,0:T(8,128)(2,1)} %in_mine.3), channel_id=1, source_target_pairs={{0,2},{2,0},{1,3},{3,1},{4,6},{6,4},{5,7},{7,5},{8,10},{10,8},{9,1... | collective-permute-start | bytes 6291464 | tf_op jit(solution)/shard_map/ppermute | solution.py:1386
  56.2 5.6 collective-permute-start.1
  56.2 51.9 %collective-permute-start.2 = (bf16[1024,1024]{1,0:T(8,128)(2,1)S(1)}, bf16[1024,1024]{1,0:T(8,128)(2,1)}, u32[]{:S(2)}, u32[]{:S(2)}) collective-permute-start(bf16[1024,1024]{1,0:T(8,128)(2,1)S(1)} %copy-done.23), channel_id=1, source_target_pairs={{0,2},{2,0},{1,3},{3,1},{4,6},{6,4},{5,7},{7,5},{8,10},{10,8},{9,1... | collective-permute-start | bytes 6291464 | tf_op jit(solution)/shard_map/ppermute | solution.py:1386
  108.0 4.7 collective-permute-start.3
  108.3 19.6 %collective-permute-start.6 = (bf16[1024,1024]{1,0:T(8,128)(2,1)}, bf16[1024,1024]{1,0:T(8,128)(2,1)S(1)}, u32[]{:S(2)}, u32[]{:S(2)}) collective-permute-start(bf16[1024,1024]{1,0:T(8,128)(2,1)} %collective-permute-done.2.mine.refs_1_.refs_3_.refs_5_.refs_7_.refs_9_.refs_11_.refs_13_.refs_15_.grad_mine), channel_id=1, source_target_pairs={{0,1},{1,0},{2,3},{3,2},{4,5},{5,4},{6,7},{7,6},{8,9},{9,8},{10,11... | collective-permute-start | bytes 6291464 | tf_op jit(solution)/shard_map/ppermute | solution.py:1386
  113.7 4.7 collective-permute-start.4
  118.4 25.5 %collective-permute-start.5 = (bf16[512,1024]{1,0:T(8,128)(2,1)}, bf16[512,1024]{1,0:T(8,128)(2,1)}, u32[]{:S(2)}, u32[]{:S(2)}) collective-permute-start(bf16[512,1024]{1,0:T(8,128)(2,1)} %convolution_convert_fusion.3.at_mine), channel_id=1, source_target_pairs={{0,2},{2,0},{1,3},{3,1},{4,6},{6,4},{5,7},{7,5},{8,10},{10,8},{9,1... | collective-permute-start | bytes 3145736 | tf_op jit(solution)/shard_map/ppermute | solution.py:1386
  124.3 23.4 %collective-permute-start.9 = (bf16[512,1024]{1,0:T(8,128)(2,1)}, bf16[512,1024]{1,0:T(8,128)(2,1)}, u32[]{:S(2)}, u32[]{:S(2)}) collective-permute-start(bf16[512,1024]{1,0:T(8,128)(2,1)} %convolution_convert_fusion.1.at_mine), channel_id=1, source_target_pairs={{0,1},{1,0},{2,3},{3,2},{4,5},{5,4},{6,7},{7,6},{8,9},{9,8},{10,11... | collective-permute-start | bytes 3145736 | tf_op jit(solution)/shard_map/ppermute | solution.py:1386
  143.9 3.8 collective-permute-start.10
  144.1 25.4 %collective-permute-start.8 = (bf16[512,1024]{1,0:T(8,128)(2,1)S(1)}, bf16[512,1024]{1,0:T(8,128)(2,1)S(1)}, u32[]{:S(2)}, u32[]{:S(2)}) collective-permute-start(bf16[512,1024]{1,0:T(8,128)(2,1)S(1)} %copy-done.38), channel_id=1, source_target_pairs={{0,2},{2,0},{1,3},{3,1},{4,6},{6,4},{5,7},{7,5},{8,10},{10,8},{9,1... | collective-permute-start | bytes 3145736 | tf_op jit(solution)/shard_map/ppermute | solution.py:1386
  147.4 23.6 %collective-permute-start.7 = (bf16[512,1024]{1,0:T(8,128)(2,1)S(1)}, bf16[512,1024]{1,0:T(8,128)(2,1)S(1)}, u32[]{:S(2)}, u32[]{:S(2)}) collective-permute-start(bf16[512,1024]{1,0:T(8,128)(2,1)S(1)} %copy-done.39), channel_id=1, source_target_pairs={{0,1},{1,0},{2,3},{3,2},{4,5},{5,4},{6,7},{7,6},{8,9},{9,8},{10,11... | collective-permute-start | bytes 3145736 | tf_op jit(solution)/shard_map/ppermute | solution.py:1386
  169.5 2.7 collective-permute-start.11
  169.5 25.8 %collective-permute-start.12 = (bf16[512,1024]{1,0:T(8,128)(2,1)}, bf16[512,1024]{1,0:T(8,128)(2,1)S(1)}, u32[]{:S(2)}, u32[]{:S(2)}) collective-permute-start(bf16[512,1024]{1,0:T(8,128)(2,1)} %convolution_convert_fusion.1.at_mine), channel_id=1, source_target_pairs={{0,2},{2,0},{1,3},{3,1},{4,6},{6,4},{5,7},{7,5},{8,10},{10,8},{9,1... | collective-permute-start | bytes 3145736 | tf_op jit(solution)/shard_map/ppermute | solution.py:1386
  170.8 26.0 %collective-permute-start.15 = (bf16[512,1024]{1,0:T(8,128)(2,1)}, bf16[512,1024]{1,0:T(8,128)(2,1)S(1)}, u32[]{:S(2)}, u32[]{:S(2)}) collective-permute-start(bf16[512,1024]{1,0:T(8,128)(2,1)} %convolution_convert_fusion.3.at_mine), channel_id=1, source_target_pairs={{0,1},{1,0},{2,3},{3,2},{4,5},{5,4},{6,7},{7,6},{8,9},{9,8},{10,11... | collective-permute-start | bytes 3145736 | tf_op jit(solution)/shard_map/ppermute | solution.py:1386
  195.3 2.7 collective-permute-start.16
  195.3 25.6 %collective-permute-start.14 = (bf16[512,1024]{1,0:T(8,128)(2,1)S(1)}, bf16[512,1024]{1,0:T(8,128)(2,1)S(1)}, u32[]{:S(2)}, u32[]{:S(2)}) collective-permute-start(bf16[512,1024]{1,0:T(8,128)(2,1)S(1)} %copy-done.40), channel_id=1, source_target_pairs={{0,2},{2,0},{1,3},{3,1},{4,6},{6,4},{5,7},{7,5},{8,10},{10,8},{9,1... | collective-permute-start | bytes 3145736 | tf_op jit(solution)/shard_map/ppermute | solution.py:1386
  196.7 24.2 %collective-permute-start.13 = (bf16[512,1024]{1,0:T(8,128)(2,1)S(1)}, bf16[512,1024]{1,0:T(8,128)(2,1)S(1)}, u32[]{:S(2)}, u32[]{:S(2)}) collective-permute-start(bf16[512,1024]{1,0:T(8,128)(2,1)S(1)} %copy-done.38), channel_id=1, source_target_pairs={{0,1},{1,0},{2,3},{3,2},{4,5},{5,4},{6,7},{7,6},{8,9},{9,8},{10,11... | collective-permute-start | bytes 3145736 | tf_op jit(solution)/shard_map/ppermute | solution.py:1386
  220.9 2.7 collective-permute-start.17
  270.8 463.6 %reduce-scatter.5.cloned.1.call-start = ((), (), s32[]{:S(2)}) async-start(), calls=%async_computation.3 | async-start | bytes 9437184 | tf_op jit(solution)/shard_map/reduce_scatter | solution.py:1718
  300.1 112.9 %collective-permute-start.21 = (bf16[512,2048]{1,0:T(8,128)(2,1)}, bf16[512,2048]{1,0:T(8,128)(2,1)}, u32[]{:S(2)}, u32[]{:S(2)}) collective-permute-start(bf16[512,2048]{1,0:T(8,128)(2,1)} %get-tuple-element.227), channel_id=1, source_target_pairs={{0,4},{4,0},{8,12},{12,8},{16,20},{20,16},{24,28},{28,24},{1,5},{5... | collective-permute-start | bytes 6291464 | tf_op jit(solution)/shard_map/ppermute | solution.py:1424
  301.7 114.9 %collective-permute-start.20 = (bf16[512,2048]{1,0:T(8,128)(2,1)}, bf16[512,2048]{1,0:T(8,128)(2,1)S(1)}, u32[]{:S(2)}, u32[]{:S(2)}) collective-permute-start(bf16[512,2048]{1,0:T(8,128)(2,1)} %get-tuple-element.226), channel_id=1, source_target_pairs={{0,8},{4,12},{8,0},{12,4},{16,24},{20,28},{24,16},{28,20},{1,9},{5... | collective-permute-start | bytes 6291464 | tf_op jit(solution)/shard_map/ppermute | solution.py:1424
  329.3 89.5 %collective-permute-start.19 = (bf16[1024,1024]{1,0:T(8,128)(2,1)}, bf16[1024,1024]{1,0:T(8,128)(2,1)}, u32[]{:S(2)}, u32[]{:S(2)}) collective-permute-start(bf16[1024,1024]{1,0:T(8,128)(2,1)} %second_grad.2), channel_id=1, source_target_pairs={{0,2},{2,0},{1,3},{3,1},{4,6},{6,4},{5,7},{7,5},{8,10},{10,8},{9,1... | collective-permute-start | bytes 6291464 | tf_op jit(solution)/shard_map/ppermute | solution.py:1386
  357.1 65.7 %collective-permute-start.18 = (bf16[1024,1024]{1,0:T(8,128)(2,1)}, bf16[1024,1024]{1,0:T(8,128)(2,1)}, u32[]{:S(2)}, u32[]{:S(2)}) collective-permute-start(bf16[1024,1024]{1,0:T(8,128)(2,1)} %second_grad.3), channel_id=1, source_target_pairs={{0,2},{2,0},{1,3},{3,1},{4,6},{6,4},{5,7},{7,5},{8,10},{10,8},{9,1... | collective-permute-start | bytes 6291464 | tf_op jit(solution)/shard_map/ppermute | solution.py:1386
  425.4 4.6 collective-permute-start.23
  443.8 4.4 collective-permute-start.22
  444.9 80.6 %collective-permute-start.26 = (bf16[256,2048]{1,0:T(8,128)(2,1)}, bf16[256,2048]{1,0:T(8,128)(2,1)}, u32[]{:S(2)}, u32[]{:S(2)}) collective-permute-start(bf16[256,2048]{1,0:T(8,128)(2,1)} %get-tuple-element.406), channel_id=1, source_target_pairs={{0,8},{4,12},{8,0},{12,4},{16,24},{20,28},{24,16},{28,20},{1,9},{5... | collective-permute-start | bytes 3145736 | tf_op jit(solution)/shard_map/ppermute | solution.py:1424
  445.4 80.0 %collective-permute-start.27 = (bf16[256,2048]{1,0:T(8,128)(2,1)}, bf16[256,2048]{1,0:T(8,128)(2,1)}, u32[]{:S(2)}, u32[]{:S(2)}) collective-permute-start(bf16[256,2048]{1,0:T(8,128)(2,1)} %get-tuple-element.404), channel_id=1, source_target_pairs={{0,16},{4,20},{8,24},{12,28},{16,0},{20,4},{24,8},{28,12},{1,17},{... | collective-permute-start | bytes 3145736 | tf_op jit(solution)/shard_map/ppermute | solution.py:1424
  477.0 48.5 %collective-permute-start.25 = (bf16[512,1024]{1,0:T(8,128)(2,1)}, bf16[512,1024]{1,0:T(8,128)(2,1)}, u32[]{:S(2)}, u32[]{:S(2)}) collective-permute-start(bf16[512,1024]{1,0:T(8,128)(2,1)} %get-tuple-element.250), channel_id=1, source_target_pairs={{0,4},{4,0},{8,12},{12,8},{16,20},{20,16},{24,28},{28,24},{1,5},{5... | collective-permute-start | bytes 3145736 | tf_op jit(solution)/shard_map/ppermute | solution.py:1424
  479.3 56.5 %collective-permute-start.24 = (bf16[1024,1024]{1,0:T(8,128)(2,1)}, bf16[1024,1024]{1,0:T(8,128)(2,1)}, u32[]{:S(2)}, u32[]{:S(2)}) collective-permute-start(bf16[1024,1024]{1,0:T(8,128)(2,1)} %slice.211), channel_id=1, source_target_pairs={{0,2},{2,0},{1,3},{3,1},{4,6},{6,4},{5,7},{7,5},{8,10},{10,8},{9,1... | collective-permute-start | bytes 6291464 | tf_op jit(solution)/shard_map/ppermute | solution.py:1386
  481.1 44.4 %copy-start.71 = (bf16[8,768]{1,0:T(8,128)(2,1)S(1)}, bf16[8,768]{1,0:T(8,128)(2,1)}, u32[]{:S(2)}) copy-start(bf16[8,768]{1,0:T(8,128)(2,1)} %copy-done.70) | copy-start | bytes 36868
  481.2 44.4 %copy-start.73 = (bf16[8,768]{1,0:T(8,128)(2,1)S(1)}, bf16[8,768]{1,0:T(8,128)(2,1)}, u32[]{:S(2)}) copy-start(bf16[8,768]{1,0:T(8,128)(2,1)} %copy-done.72) | copy-start | bytes 36868
  481.2 45.1 %copy-start.44 = (f32[2048,1]{1,0:T(8,128)S(1)}, f32[2048,1]{1,0:T(8,128)}, u32[]{:S(2)}) copy-start(f32[2048,1]{1,0:T(8,128)} %get-tuple-element.242) | copy-start | bytes 24580
  481.3 45.3 %copy-start.105 = (f32[1,1024]{1,0:T(1,128)S(1)}, f32[1,1024]{1,0:T(1,128)}, u32[]{:S(2)}) copy-start(f32[1,1024]{1,0:T(1,128)} %get-tuple-element.276) | copy-start | bytes 12292
  481.3 45.3 %copy-start.106 = (f32[1,1024]{1,0:T(1,128)S(1)}, f32[1,1024]{1,0:T(1,128)}, u32[]{:S(2)}) copy-start(f32[1,1024]{1,0:T(1,128)} %get-tuple-element.277) | copy-start | bytes 12292
  481.3 51.6 %copy-start.58 = (bf16[512,1024]{1,0:T(8,128)(2,1)S(1)}, bf16[512,1024]{1,0:T(8,128)(2,1)}, u32[]{:S(2)}) copy-start(bf16[512,1024]{1,0:T(8,128)(2,1)} %get-tuple-element.246) | copy-start | bytes 3145732
  525.5 17.8 %collective-permute-start.28 = (bf16[512,2048]{1,0:T(8,128)(2,1)S(1)}, bf16[512,2048]{1,0:T(8,128)(2,1)S(1)}, u32[]{:S(2)}, u32[]{:S(2)}) collective-permute-start(bf16[512,2048]{1,0:T(8,128)(2,1)S(1)} %get-tuple-element.255.refs_0_), channel_id=1, source_target_pairs={{0,1},{1,0},{2,3},{3,2},{4,5},{5,4},{6,7},{7,6},{8,9},{9,8},{10,11... | collective-permute-start | bytes 6291464 | tf_op jit(solution)/shard_map/ppermute | solution.py:1386
  527.2 15.5 %collective-permute-start.29 = (bf16[128,2048]{1,0:T(8,128)(2,1)S(1)}, bf16[128,2048]{1,0:T(8,128)(2,1)S(1)}, u32[]{:S(2)}, u32[]{:S(2)}) collective-permute-start(bf16[128,2048]{1,0:T(8,128)(2,1)S(1)} %get-tuple-element.258.refs_1_), channel_id=1, source_target_pairs={{0,1},{1,0},{2,3},{3,2},{4,5},{5,4},{6,7},{7,6},{8,9},{9,8},{10,11... | collective-permute-start | bytes 1572872 | tf_op jit(solution)/shard_map/ppermute | solution.py:1386
  527.6 15.7 %collective-permute-start.30 = (bf16[128,2048]{1,0:T(8,128)(2,1)S(1)}, bf16[128,2048]{1,0:T(8,128)(2,1)S(1)}, u32[]{:S(2)}, u32[]{:S(2)}) collective-permute-start(bf16[128,2048]{1,0:T(8,128)(2,1)S(1)} %get-tuple-element.259.refs_2_), channel_id=1, source_target_pairs={{0,1},{1,0},{2,3},{3,2},{4,5},{5,4},{6,7},{7,6},{8,9},{9,8},{10,11... | collective-permute-start | bytes 1572872 | tf_op jit(solution)/shard_map/ppermute | solution.py:1386
  534.5 69.3 %collective-permute-start.33 = (bf16[128,2048]{1,0:T(8,128)(2,1)}, bf16[128,2048]{1,0:T(8,128)(2,1)}, u32[]{:S(2)}, u32[]{:S(2)}) collective-permute-start(bf16[128,2048]{1,0:T(8,128)(2,1)} %get-tuple-element.412), channel_id=1, source_target_pairs={{0,4},{4,0},{8,12},{12,8},{16,20},{20,16},{24,28},{28,24},{1,5},{5... | collective-permute-start | bytes 1572872 | tf_op jit(solution)/shard_map/ppermute | solution.py:1424
  535.8 66.1 %collective-permute-start.34 = (bf16[128,2048]{1,0:T(8,128)(2,1)}, bf16[128,2048]{1,0:T(8,128)(2,1)S(1)}, u32[]{:S(2)}, u32[]{:S(2)}) collective-permute-start(bf16[128,2048]{1,0:T(8,128)(2,1)} %get-tuple-element.410), channel_id=1, source_target_pairs={{0,16},{4,20},{8,24},{12,28},{16,0},{20,4},{24,8},{28,12},{1,17},{... | collective-permute-start | bytes 1572872 | tf_op jit(solution)/shard_map/ppermute | solution.py:1424
  542.6 58.3 %collective-permute-start.35 = (bf16[256,1024]{1,0:T(8,128)(2,1)S(1)}, bf16[256,1024]{1,0:T(8,128)(2,1)S(1)}, u32[]{:S(2)}, u32[]{:S(2)}) collective-permute-start(bf16[256,1024]{1,0:T(8,128)(2,1)S(1)} %get-tuple-element.408), channel_id=1, source_target_pairs={{0,8},{4,12},{8,0},{12,4},{16,24},{20,28},{24,16},{28,20},{1,9},{5... | collective-permute-start | bytes 1572872 | tf_op jit(solution)/shard_map/ppermute | solution.py:1424
  562.4 26.1 %collective-permute-start.31 = (f32[32,2048]{1,0:T(8,128)S(1)}, f32[32,2048]{1,0:T(8,128)S(1)}, u32[]{:S(2)}, u32[]{:S(2)}) collective-permute-start(f32[32,2048]{1,0:T(8,128)S(1)} %pad_maximum_fusion.1), channel_id=1, source_target_pairs={{0,2},{2,0},{1,3},{3,1},{4,6},{6,4},{5,7},{7,5},{8,10},{10,8},{9,1... | collective-permute-start | bytes 786440 | tf_op jit(solution)/shard_map/ppermute | solution.py:1386
  563.2 25.2 %collective-permute-start.32 = (f32[1,1024]{1,0:T(1,128)}, f32[1,1024]{1,0:T(1,128)S(1)}, u32[]{:S(2)}, u32[]{:S(2)}) collective-permute-start(f32[1,1024]{1,0:T(1,128)} %get-tuple-element.264), channel_id=1, source_target_pairs={{0,2},{2,0},{1,3},{3,1},{4,6},{6,4},{5,7},{7,5},{8,10},{10,8},{9,1... | collective-permute-start | bytes 12296 | tf_op jit(solution)/shard_map/ppermute | solution.py:1386
  603.8 110.7 %copy-start.26 = (f32[1024,1024]{1,0:T(8,128)S(1)}, f32[1024,1024]{1,0:T(8,128)}, u32[]{:S(2)}) copy-start(f32[1024,1024]{1,0:T(8,128)} %add.215) | copy-start | bytes 12582916
  606.1 108.4 %copy-start.25 = (bf16[1024,1024]{1,0:T(8,128)(2,1)S(1)}, bf16[1024,1024]{1,0:T(8,128)(2,1)}, u32[]{:S(2)}) copy-start(bf16[1024,1024]{1,0:T(8,128)(2,1)} %in_mine.3) | copy-start | bytes 6291460
  717.3 9.3 %collective-permute-start.36 = (f32[1024]{0:T(1024)S(1)}, f32[1024]{0:T(1024)S(1)}, u32[]{:S(2)}, u32[]{:S(2)}) collective-permute-start(f32[1024]{0:T(1024)S(1)} %multiply_reduce_fusion), channel_id=1, source_target_pairs={{0,1},{1,0},{2,3},{3,2},{4,5},{5,4},{6,7},{7,6},{8,9},{9,8},{10,11... | collective-permute-start | bytes 12296 | tf_op jit(solution)/shard_map/ppermute | solution.py:1386
  717.5 15.2 %collective-permute-start.37 = (bf16[128,1024]{1,0:T(8,128)(2,1)}, bf16[128,1024]{1,0:T(8,128)(2,1)}, u32[]{:S(2)}, u32[]{:S(2)}) collective-permute-start(bf16[128,1024]{1,0:T(8,128)(2,1)} %get-tuple-element.416), channel_id=1, source_target_pairs={{0,16},{4,20},{8,24},{12,28},{16,0},{20,4},{24,8},{28,12},{1,17},{... | collective-permute-start | bytes 786440 | tf_op jit(solution)/shard_map/ppermute | solution.py:1424
  (103 other events, 1098.0 us)
Sparse Core Ops, SparseCore 0:
  271.0 218.9 reduce-scatter.2
  494.0 209.9 reduce-scatter.4

commit v4 on v3

--- a/solution.py
+++ b/solution.py
@@ -1870,6 +1870,11 @@
     grad_gate = sides(grad_gate_pair)
     clock = settle((grad_up, result, grad_gate), "output", "down_own", "down_got")
     d_first = d_first + contract(d_adapter[:, :half_rows], thin, 0, 0)
+    tied_down = None
+    if sums["down_own"].done and sums["down_got"].done:
+        whole_down = ordered(sums["down_own"].keep, sums["down_got"].keep, col, 1)
+        tied_down = jnp.transpose(whole_down)
+        clock += (tied_down,)
     d_first_far, totals, joined, reduced = finish(
         after(d_first_far, *clock),
         (
@@ -1925,7 +1930,10 @@
     ]
 
     grad_up_weight = sides(grad_up_pair)
-    grad_down_weight = ordered(sums["down_own"].keep, sums["down_got"].keep, col, 1)
+    grad_down_weight = tied_down
+    if tied_down is None:
+        whole_down = ordered(sums["down_own"].keep, sums["down_got"].keep, col, 1)
+        grad_down_weight = jnp.transpose(whole_down)
     return (
         result,
         grad_activations,
@@ -1947,7 +1955,7 @@
         totals[1][0],
         grad_gate,
         grad_up_weight,
-        jnp.transpose(grad_down_weight),
+        grad_down_weight,
     )
 
 

time: 758 us -> 757 us (level)
    unnamed x232 -> x230, local copies, waits for them, and re-layouts: 19.4 us -> 18.7 us
  transfers between devices with their start and end apart: 40 -> 40, of which waited for: 11 -> 10; matrix products, arithmetic and copies ran while one was open for 13% -> 13% of each run, Pallas kernels for 70% -> 70%
where the time goes in v4:
time: 757 us; the launch traced here: 748 us
  Pallas kernels  573 us (76%)
  other arithmetic  55.8 us (7%)
  local copies, waits for them, and re-layouts  36.1 us (5%)
  starting transfers between devices  30.8 us (4%)
  matrix products  22.4 us (3%)
  between operations  16.2 us (2%)
  waiting for transfers between devices  14.5 us (2%)
    pallas_call x1, Pallas kernels, finish(): pl.pallas_call(functools.partial(finish_kernel, orders, len(smalls), join...  111 us
    pallas_call x3, Pallas kernels, pair_grad(): pl.pallas_call(functools.partial(pair_grad_kernel, chunks, merged), grid=...  82.4 us
    pallas_call x3, Pallas kernels, pair_sum(): pl.pallas_call(functools.partial(pair_sum_kernel, products), grid=(2 * ti...  81.1 us
    pallas_call x4, Pallas kernels, mlp_block(): grid_call(functools.partial(mlp_kernel, len(shapes)), 'mlp_block', (tiles...  81.1 us
    pallas_call x1, Pallas kernels, attention_backward(): pl.pallas_call(backward_kernel, out_shape=(jax.ShapeDtypeStruct(qt.shape,...  44.1 us
    pallas_call x3, Pallas kernels, weight_grad(): grid_call(functools.partial(weight_grad_kernel, len(sets), chunks, pieces...  30.8 us
    pallas_call x1, Pallas kernels, exchange(): pl.pallas_call(functools.partial(exchange_kernel, query_cols, key_cols),...  29.7 us
    pallas_call x2, Pallas kernels, hidden_grad(): grid_call(hidden_grad_kernel, 'hidden_grad', (tiles,), jax.ShapeDtypeStru...  28.7 us
  transfers between devices with their start and end apart: 40, of which 10 were waited for; matrix products, arithmetic and copies ran while one was open for 13% of the time, Pallas kernels for 70%

profile of v4, /device:TPU:0, one launch (start us, length us, event | category | flops | bytes accessed | tf_op | source)
XLA Modules:
  0.0 748.3 jit_solution(11170350979990973805)
XLA Ops:
  7.2 3.0 collective-permute-start
  13.0 29.7 %exchange.1 = (bf16[1024,1024]{1,0:T(8,128)(2,1)}, bf16[1024,1024]{1,0:T(8,128)(2,1)}, bf16[1024,768]{1,0:T(8,128)(2,1)}, bf16[1024,2048]{1,0:T(8,128)(2,1)}, bf...) custom-call(bf16[1024,1024]{1,0:T(8,128)(2,1)} %in_mine.3, ...), custom_call_target="tpu_custom_call" | custom-call | flops 1000 | bytes 1000 | tf_op jit(solution)/shard_map/exchange/pallas_call | solution.py:518
  45.2 10.5 %project_block.2 = (bf16[2048,2048]{1,0:T(8,128)(2,1)}, bf16[512,2048]{1,0:T(8,128)(2,1)}, bf16[256,2048]{1,0:T(8,128)(2,1)}, bf16[2048,32]{1,0:T(8,128)(2,1)}, f32[2048,1]{1,0:T(8,128)}) custom-call(s32[10]{0:T(128)} %stack.105.place_ref, bf16[1024,1024]{1,0:T(8,128)(2,1)} %in_mine.3, bf16[1024,1024]{1,0:T(8,128)(2,1)} %get-tuple-element.158.other_ref.in_other, ...), custom_call_target="tpu_custom_call" | custom-call | flops 1000 | bytes 1000 | tf_op jit(solution)/shard_map/project_block/pallas_call | solution.py:620
  61.8 10.4 %project_block.3 = (bf16[2048,2048]{1,0:T(8,128)(2,1)}, bf16[512,2048]{1,0:T(8,128)(2,1)}, bf16[256,2048]{1,0:T(8,128)(2,1)}, bf16[2048,32]{1,0:T(8,128)(2,1)}, f32[2048,1]{1,0:T(8,128)}) custom-call(s32[10]{0:T(128)} %stack.105.place_ref, ...), custom_call_target="tpu_custom_call", output_to_operand_aliasing={{0}: (10, {}), {1}: (11, {}), {2}: (12, {}), {3}: (13, {}),... | custom-call | flops 1000 | bytes 1000 | tf_op jit(solution)/shard_map/project_block/pallas_call | solution.py:620
  74.1 19.4 %attention_forward.1 = (bf16[512,2048]{1,0:T(8,128)(2,1)S(1)}, f32[2,4,2048]{2,1,0:T(4,128)S(1)}) custom-call(s32[6]{0:T(128)S(1)} %pad_add_fusion.mark_ref, s32[1,1,2048]{2,1,0:T(1,128)S(1)} %bitcast.47, bf16[512,2048]{1,0:T(8,128)(2,1)S(1)} %copy-done.2, bf16[256,2176]{1,0:T(8,128)(2,1)S(1)} %pad.18.kt_ref.vt_ref, ...), custom_call_target="tpu_custom_call" | custom-call | flops 1000 | bytes 1000 | tf_op jit(solution)/shard_map/attention_forward/pallas_call | solution.py:293
  93.6 14.5 %hidden_grad.2.refs_0_ = bf16[2048,2048]{1,0:T(8,128)(2,1)} custom-call(s32[10]{0:T(128)} %stack.105.place_ref, bf16[1024,1024]{1,0:T(8,128)(2,1)} %grad_mine.1, bf16[1024,1024]{1,0:T(8,128)(2,1)} %get-tuple-element.174.other.refs_16_.refs_18_.refs_20_.refs_22_.refs_24_.refs_26_.refs_28_.refs_30_.grad_other, bf16[4096,1024]{1,0:T(8,128)(2,1)} %refs_1_.3, ...), custom_call_target="tpu_custom_call" | custom-call | flops 1000 | bytes 1000 | tf_op jit(solution)/shard_map/hidden_grad/pallas_call | solution.py:549
  108.8 3.9 collective-permute-done.3
  116.1 2.3 convolution_convert_fusion.3.at_mine
  119.7 2.3 convolution_convert_fusion.2.at_mine
  122.0 2.3 convolution_convert_fusion.1.at_mine
  124.3 2.3 convolution_convert_fusion.at_mine
  129.2 14.2 %hidden_grad.3.dh_ref = bf16[2048,2048]{1,0:T(8,128)(2,1)} custom-call(s32[10]{0:T(128)} %stack.105.place_ref, bf16[1024,1024]{1,0:T(8,128)(2,1)} %collective-permute-done.2.mine.refs_1_.refs_3_.refs_5_.refs_7_.refs_9_.refs_11_.refs_13_.refs_15_.grad_mine, bf16[1024,1024]{1,0:T(8,128)(2,1)} %copy-done.24, ...), custom_call_target="tpu_custom_call", output_to_operand_aliasing={{}: (5, {})} | custom-call | flops 1000 | bytes 1000 | tf_op jit(solution)/shard_map/hidden_grad/pallas_call | solution.py:549
  148.7 20.2 %mlp_block.4 = (bf16[2048,2048]{1,0:T(8,128)(2,1)}, bf16[2048,2048]{1,0:T(8,128)(2,1)}, bf16[2048,2048]{1,0:T(8,128)(2,1)}, bf16[2048,2048]{1,0:T(8,128)(2,1)}, f32[2048,1]{1,0:T(8,128)}, /*index=5*/f32[1024,1024]{1,0:T(8,128)}) custom-call(s32[10]{0:T(128)} %stack.105.place_ref, bf16[1024,1024]{1,0:T(8,128)(2,1)} %in_mine.3, ...), custom_call_target="tpu_custom_call" | custom-call | flops 1000 | bytes 1000 | tf_op jit(solution)/shard_map/mlp_block/pallas_call | solution.py:743
  173.2 21.2 %mlp_block.5 = (bf16[2048,2048]{1,0:T(8,128)(2,1)}, bf16[2048,2048]{1,0:T(8,128)(2,1)}, bf16[2048,2048]{1,0:T(8,128)(2,1)}, bf16[2048,2048]{1,0:T(8,128)(2,1)}, f32[2048,1]{1,0:T(8,128)}, /*index=5*/f32[1024,1024]{1,0:T(8,128)}) custom-call(s32[10]{0:T(128)} %stack.105.place_ref, ...), custom_call_target="tpu_custom_call", output_to_operand_aliasing={{0}: (15, {}), {1}: (16, {}), {2}: (17, {}), {3}: (18, {}),... | custom-call | flops 1000 | bytes 1000 | tf_op jit(solution)/shard_map/mlp_block/pallas_call | solution.py:743
  199.0 19.8 %mlp_block.6 = (bf16[2048,2048]{1,0:T(8,128)(2,1)}, bf16[2048,2048]{1,0:T(8,128)(2,1)}, bf16[2048,2048]{1,0:T(8,128)(2,1)}, bf16[2048,2048]{1,0:T(8,128)(2,1)}, f32[2048,1]{1,0:T(8,128)}) custom-call(s32[10]{0:T(128)} %stack.105.place_ref, ...), custom_call_target="tpu_custom_call", output_to_operand_aliasing={{0}: (15, {}), {1}: (16, {}), {2}: (17, {}), {3}: (18, {}),... | custom-call | flops 1000 | bytes 1000 | tf_op jit(solution)/shard_map/mlp_block/pallas_call | solution.py:743
  220.9 2.6 collective-permute-done.17.far_other
  224.5 19.9 %mlp_block.7 = (bf16[2048,2048]{1,0:T(8,128)(2,1)}, bf16[2048,2048]{1,0:T(8,128)(2,1)}, bf16[2048,2048]{1,0:T(8,128)(2,1)}, bf16[2048,2048]{1,0:T(8,128)(2,1)}, f32[2048,1]{1,0:T(8,128)}) custom-call(s32[10]{0:T(128)} %stack.105.place_ref, ...), custom_call_target="tpu_custom_call", output_to_operand_aliasing={{0}: (15, {}), {1}: (16, {}), {2}: (17, {}), {3}: (18, {}),... | custom-call | flops 1000 | bytes 1000 | tf_op jit(solution)/shard_map/mlp_block/pallas_call | solution.py:743
  244.4 26.5 %gate_grad.1 = bf16[1024,4096]{1,0:T(8,128)(2,1)} custom-call(bf16[2048,2048]{1,0:T(8,128)(2,1)} %get-tuple-element.216.refs_0_.refs_1_.refs_2_.refs_3_.refs_4_.refs_5_.refs_6_.refs_7_.refs_8_.refs_9_.refs_10_.refs_11_.refs_12_.refs_13_.refs_14_.refs_15_.normed_ref, ...), custom_call_target="tpu_custom_call" | custom-call | flops 1000 | bytes 1000 | tf_op jit(solution)/shard_map/gate_grad/pallas_call | solution.py:1295
  271.0 29.3 %down_grad.1 = (bf16[512,2048]{1,0:T(8,128)(2,1)}, bf16[512,2048]{1,0:T(8,128)(2,1)}, bf16[512,2048]{1,0:T(8,128)(2,1)}, bf16[512,2048]{1,0:T(8,128)(2,1)}) custom-call(bf16[1024,1024]{1,0:T(8,128)(2,1)} %grad_mine.1, bf16[1024,1024]{1,0:T(8,128)(2,1)} %collective-permute-done.2.mine.refs_1_.refs_3_.refs_5_.refs_7_.refs_9_.refs_11_.refs_13_.refs_15_.grad_mine, ...), custom_call_target="tpu_custom_call" | custom-call | flops 1000 | bytes 1000 | tf_op jit(solution)/shard_map/down_grad/pallas_call | solution.py:1295
  303.6 26.0 %second_grad.2 = bf16[1024,1024]{1,0:T(8,128)(2,1)} custom-call(bf16[2048,2048]{1,0:T(8,128)(2,1)} %get-tuple-element.222.refs_16_.refs_0_, bf16[2048,2048]{1,0:T(8,128)(2,1)} %get-tuple-element.223.refs_1_.refs_16_, bf16[1024,4096]{1,0:T(8,128)(2,1)} %refs_2_.7, bf16[1024,2048]{1,0:T(8,128)(2,1)} %get-tuple-element.189.gate_got.refs_3_, ...), custom_call_target="tpu_custom_call" | custom-call | flops 1000 | bytes 1000 | tf_op jit(solution)/shard_map/second_grad/pallas_call | solution.py:905
  330.9 26.5 %second_grad.3 = bf16[1024,1024]{1,0:T(8,128)(2,1)} custom-call(bf16[2048,2048]{1,0:T(8,128)(2,1)} %get-tuple-element.222.refs_16_.refs_0_, bf16[2048,2048]{1,0:T(8,128)(2,1)} %get-tuple-element.223.refs_1_.refs_16_, bf16[1024,4096]{1,0:T(8,128)(2,1)} %refs_2_.7, bf16[1024,2048]{1,0:T(8,128)(2,1)} %get-tuple-element.189.gate_got.refs_3_, ...), custom_call_target="tpu_custom_call" | custom-call | flops 1000 | bytes 1000 | tf_op jit(solution)/shard_map/second_grad/pallas_call | solution.py:905
  358.2 26.5 %up_grad.1 = bf16[1024,4096]{1,0:T(8,128)(2,1)} custom-call(bf16[2048,2048]{1,0:T(8,128)(2,1)} %get-tuple-element.216.refs_0_.refs_1_.refs_2_.refs_3_.refs_4_.refs_5_.refs_6_.refs_7_.refs_8_.refs_9_.refs_10_.refs_11_.refs_12_.refs_13_.refs_14_.refs_15_.normed_ref, ...), custom_call_target="tpu_custom_call" | custom-call | flops 1000 | bytes 1000 | tf_op jit(solution)/shard_map/up_grad/pallas_call | solution.py:1295
  384.7 28.6 %down_product.1 = bf16[2048,1024]{1,0:T(8,128)(2,1)} custom-call(bf16[2048,2048]{1,0:T(8,128)(2,1)} %get-tuple-element.224.refs_32_.refs_0_, bf16[4096,1024]{1,0:T(8,128)(2,1)} %refs_1_.3, bf16[2048,1024]{1,0:T(8,128)(2,1)} %get-tuple-element.175.down_got.refs_2_), custom_call_target="tpu_custom_call" | custom-call | flops 1000 | bytes 1000 | tf_op jit(solution)/shard_map/down_product/pallas_call | solution.py:905
  413.3 3.6 add_convert_fusion.4
  419.1 4.0 add_convert_fusion.2.total_mine
  423.1 2.6 add_convert_fusion.1.total_mine
  426.9 2.3 constant_dynamic-slice_fusion.3.out_own
  430.2 13.8 %norm_back.2 = (bf16[512,2048]{1,0:T(8,128)(2,1)}, bf16[2048,1024]{1,0:T(8,128)(2,1)}, bf16[2048,128]{1,0:T(8,128)(2,1)}, f32[1,1024]{1,0:T(1,128)}, f32[1024,1024]{1,0:T(8,128)}) custom-call(s32[10]{0:T(128)} %stack.105.place_ref, bf16[1024,1024]{1,0:T(8,128)(2,1)} %add_convert_fusion.2.total_mine, bf16[1024,1024]{1,0:T(8,128)(2,1)} %collective-permute-done.23.total_other, ...), custom_call_target="tpu_custom_call" | custom-call | flops 1000 | bytes 1000 | tf_op jit(solution)/shard_map/norm_back/pallas_call | solution.py:848
  445.8 2.6 collective-permute-start.27
  448.5 13.0 %norm_back.3 = (bf16[512,2048]{1,0:T(8,128)(2,1)}, bf16[2048,1024]{1,0:T(8,128)(2,1)}, bf16[2048,128]{1,0:T(8,128)(2,1)}, f32[1,1024]{1,0:T(1,128)}) custom-call(s32[10]{0:T(128)} %stack.105.place_ref, bf16[1024,1024]{1,0:T(8,128)(2,1)} %copy-done.33, ...), custom_call_target="tpu_custom_call", output_to_operand_aliasing={{0}: (12, {}), {1}: (13, {}), {2}: (14, {})} | custom-call | flops 1000 | bytes 1000 | tf_op jit(solution)/shard_map/norm_back/pallas_call | solution.py:848
  461.5 2.4 fusion.12.refs_5_
  463.8 3.5 fusion.39.refs_3_
  467.3 9.9 %weight_grad.3 = (bf16[512,1024]{1,0:T(8,128)(2,1)}, bf16[512,1024]{1,0:T(8,128)(2,1)}) custom-call(s32[10]{0:T(128)} %stack.117.place_ref, bf16[1024,2048]{1,0:T(8,128)(2,1)} %copy-done.22, bf16[1024,2048]{1,0:T(8,128)(2,1)} %copy-done.22, bf16[1024,2048]{1,0:T(8,128)(2,1)} %copy-done.22, bf16[1024,2048]{1,0:T(8,128)(2,1)} %copy-done.22, ...), custom_call_target="tpu_custom_call" | custom-call | flops 1000 | bytes 1000 | tf_op jit(solution)/shard_map/weight_grad/pallas_call | solution.py:1173
  481.6 44.1 %attention_backward.1 = (bf16[512,2048]{1,0:T(8,128)(2,1)S(1)}, bf16[128,2048]{1,0:T(8,128)(2,1)S(1)}, bf16[128,2048]{1,0:T(8,128)(2,1)S(1)}, f32[8,32,128]{2,1,0:T(8,128)S(1)}, f32[2,32,128]{2,1,0:T(8,128)S(1)}) custom-call(s32[6]{0:T(128)S(1)} %copy-done.21, s32[1,1,2048]{2,1,0:T(1,128)S(1)} %bitcast.48, bf16[512,2048]{1,0:T(8,128)(2,1)} %get-tuple-element.169.qt_ref, ...), custom_call_target="tpu_custom_call" | custom-call | flops 1000 | bytes 1000 | tf_op jit(solution)/shard_map/attention_backward/pallas_call | solution.py:334
  527.9 2.6 add_convert_fusion.8
  532.3 2.4 add_convert_fusion.7
  536.0 2.7 collective-permute-start.34
  538.7 4.2 add_convert_fusion
  545.0 16.7 %first_back.1 = (bf16[1024,1024]{1,0:T(8,128)(2,1)}, f32[1024,1024]{1,0:T(8,128)}, bf16[2048,1536]{1,0:T(8,128)(2,1)}, f32[32,2048]{1,0:T(8,128)}, f32[1,1024]{1,0:T(1,128)}) custom-call(s32[10]{0:T(128)} %stack.105.place_ref, bf16[512,2048]{1,0:T(8,128)(2,1)} %copy-done.7, bf16[128,2048]{1,0:T(8,128)(2,1)} %copy-done.12, bf16[128,2048]{1,0:T(8,128)(2,1)} %copy-done.13, ...), custom_call_target="tpu_custom_call" | custom-call | flops 1000 | bytes 1000 | tf_op jit(solution)/shard_map/first_back/pallas_call | solution.py:1357
  564.8 2.4 fusion.2
  567.9 10.5 %weight_grad.4.refs_9_ = bf16[1024,768]{1,0:T(8,128)(2,1)} custom-call(s32[10]{0:T(128)} %stack.105.place_ref, bf16[2048,2048]{1,0:T(8,128)(2,1)} %get-tuple-element.261.refs_8_.refs_0_.refs_1_.refs_2_.refs_3_.refs_4_.refs_5_.refs_6_.refs_7_, bf16[2048,2048]{1,0:T(8,128)(2,1)} %get-tuple-element.261.refs_8_.refs_0_.refs_1_.refs_2_.refs_3_.refs_4_.refs_5_.refs_6_.refs_7_, ...), custom_call_target="tpu_custom_call" | custom-call | flops 1000 | bytes 1000 | tf_op jit(solution)/shard_map/weight_grad/pallas_call | solution.py:1173
  578.4 10.4 %weight_grad.5.refs_10_ = bf16[1024,768]{1,0:T(8,128)(2,1)} custom-call(s32[10]{0:T(128)} %stack.118.place_ref, bf16[2048,2048]{1,0:T(8,128)(2,1)} %get-tuple-element.261.refs_8_.refs_0_.refs_1_.refs_2_.refs_3_.refs_4_.refs_5_.refs_6_.refs_7_, bf16[2048,2048]{1,0:T(8,128)(2,1)} %get-tuple-element.261.refs_8_.refs_0_.refs_1_.refs_2_.refs_3_.refs_4_.refs_5_.refs_6_.refs_7_, ...), custom_call_target="tpu_custom_call" | custom-call | flops 1000 | bytes 1000 | tf_op jit(solution)/shard_map/weight_grad/pallas_call | solution.py:1173
  591.2 2.9 add.215
  594.2 3.5 multiply_reduce_fusion.1
  605.3 110.9 %finish.1 = (bf16[1024,1024]{1,0:T(8,128)(2,1)}, f32[1,1024]{1,0:T(1,128)}, f32[1,1024]{1,0:T(1,128)}, f32[8,1024]{1,0:T(8,128)}, f32[24,1024]{1,0:T(8,128)}, /*...) custom-call(bf16[1024,1024]{1,0:T(8,128)(2,1)} %get-tuple-element.27, ...), custom_call_target="tpu_custom_call" | custom-call | flops 1000 | bytes 1000 | tf_op jit(solution)/shard_map/finish/pallas_call | solution.py:1101
  716.2 2.8 multiply_reduce_fusion
  723.8 2.9 copy.118
  726.7 6.1 multiply_add_fusion
  (377 shorter events, 87.4 us)
Async XLA Ops:
  7.2 591.1 %reduce-scatter.3.cloned.1.call-start = ((), (), s32[]{:S(2)}) async-start(), calls=%async_computation.2 | async-start | bytes 9437184 | tf_op jit(solution)/shard_map/reduce_scatter | solution.py:1718
  7.2 49.0 %collective-permute-start = (bf16[1024,1024]{1,0:T(8,128)(2,1)}, bf16[1024,1024]{1,0:T(8,128)(2,1)}, u32[]{:S(2)}, u32[]{:S(2)}) collective-permute-start(bf16[1024,1024]{1,0:T(8,128)(2,1)} %in_mine.3), channel_id=1, source_target_pairs={{0,2},{2,0},{1,3},{3,1},{4,6},{6,4},{5,7},{7,5},{8,10},{10,8},{9,1... | collective-permute-start | bytes 6291464 | tf_op jit(solution)/shard_map/ppermute | solution.py:1386
  56.2 5.6 collective-permute-start.1
  56.2 51.9 %collective-permute-start.2 = (bf16[1024,1024]{1,0:T(8,128)(2,1)S(1)}, bf16[1024,1024]{1,0:T(8,128)(2,1)}, u32[]{:S(2)}, u32[]{:S(2)}) collective-permute-start(bf16[1024,1024]{1,0:T(8,128)(2,1)S(1)} %copy-done.23), channel_id=1, source_target_pairs={{0,2},{2,0},{1,3},{3,1},{4,6},{6,4},{5,7},{7,5},{8,10},{10,8},{9,1... | collective-permute-start | bytes 6291464 | tf_op jit(solution)/shard_map/ppermute | solution.py:1386
  108.1 4.7 collective-permute-start.3
  108.3 19.6 %collective-permute-start.6 = (bf16[1024,1024]{1,0:T(8,128)(2,1)}, bf16[1024,1024]{1,0:T(8,128)(2,1)S(1)}, u32[]{:S(2)}, u32[]{:S(2)}) collective-permute-start(bf16[1024,1024]{1,0:T(8,128)(2,1)} %collective-permute-done.2.mine.refs_1_.refs_3_.refs_5_.refs_7_.refs_9_.refs_11_.refs_13_.refs_15_.grad_mine), channel_id=1, source_target_pairs={{0,1},{1,0},{2,3},{3,2},{4,5},{5,4},{6,7},{7,6},{8,9},{9,8},{10,11... | collective-permute-start | bytes 6291464 | tf_op jit(solution)/shard_map/ppermute | solution.py:1386
  113.7 4.7 collective-permute-start.4
  118.4 25.5 %collective-permute-start.5 = (bf16[512,1024]{1,0:T(8,128)(2,1)}, bf16[512,1024]{1,0:T(8,128)(2,1)}, u32[]{:S(2)}, u32[]{:S(2)}) collective-permute-start(bf16[512,1024]{1,0:T(8,128)(2,1)} %convolution_convert_fusion.3.at_mine), channel_id=1, source_target_pairs={{0,2},{2,0},{1,3},{3,1},{4,6},{6,4},{5,7},{7,5},{8,10},{10,8},{9,1... | collective-permute-start | bytes 3145736 | tf_op jit(solution)/shard_map/ppermute | solution.py:1386
  124.3 23.4 %collective-permute-start.9 = (bf16[512,1024]{1,0:T(8,128)(2,1)}, bf16[512,1024]{1,0:T(8,128)(2,1)}, u32[]{:S(2)}, u32[]{:S(2)}) collective-permute-start(bf16[512,1024]{1,0:T(8,128)(2,1)} %convolution_convert_fusion.1.at_mine), channel_id=1, source_target_pairs={{0,1},{1,0},{2,3},{3,2},{4,5},{5,4},{6,7},{7,6},{8,9},{9,8},{10,11... | collective-permute-start | bytes 3145736 | tf_op jit(solution)/shard_map/ppermute | solution.py:1386
  143.9 3.8 collective-permute-start.10
  144.1 25.5 %collective-permute-start.8 = (bf16[512,1024]{1,0:T(8,128)(2,1)S(1)}, bf16[512,1024]{1,0:T(8,128)(2,1)S(1)}, u32[]{:S(2)}, u32[]{:S(2)}) collective-permute-start(bf16[512,1024]{1,0:T(8,128)(2,1)S(1)} %copy-done.38), channel_id=1, source_target_pairs={{0,2},{2,0},{1,3},{3,1},{4,6},{6,4},{5,7},{7,5},{8,10},{10,8},{9,1... | collective-permute-start | bytes 3145736 | tf_op jit(solution)/shard_map/ppermute | solution.py:1386
  147.5 23.6 %collective-permute-start.7 = (bf16[512,1024]{1,0:T(8,128)(2,1)S(1)}, bf16[512,1024]{1,0:T(8,128)(2,1)S(1)}, u32[]{:S(2)}, u32[]{:S(2)}) collective-permute-start(bf16[512,1024]{1,0:T(8,128)(2,1)S(1)} %copy-done.39), channel_id=1, source_target_pairs={{0,1},{1,0},{2,3},{3,2},{4,5},{5,4},{6,7},{7,6},{8,9},{9,8},{10,11... | collective-permute-start | bytes 3145736 | tf_op jit(solution)/shard_map/ppermute | solution.py:1386
  169.5 2.7 collective-permute-start.11
  169.5 25.8 %collective-permute-start.12 = (bf16[512,1024]{1,0:T(8,128)(2,1)}, bf16[512,1024]{1,0:T(8,128)(2,1)S(1)}, u32[]{:S(2)}, u32[]{:S(2)}) collective-permute-start(bf16[512,1024]{1,0:T(8,128)(2,1)} %convolution_convert_fusion.1.at_mine), channel_id=1, source_target_pairs={{0,2},{2,0},{1,3},{3,1},{4,6},{6,4},{5,7},{7,5},{8,10},{10,8},{9,1... | collective-permute-start | bytes 3145736 | tf_op jit(solution)/shard_map/ppermute | solution.py:1386
  170.8 26.0 %collective-permute-start.15 = (bf16[512,1024]{1,0:T(8,128)(2,1)}, bf16[512,1024]{1,0:T(8,128)(2,1)S(1)}, u32[]{:S(2)}, u32[]{:S(2)}) collective-permute-start(bf16[512,1024]{1,0:T(8,128)(2,1)} %convolution_convert_fusion.3.at_mine), channel_id=1, source_target_pairs={{0,1},{1,0},{2,3},{3,2},{4,5},{5,4},{6,7},{7,6},{8,9},{9,8},{10,11... | collective-permute-start | bytes 3145736 | tf_op jit(solution)/shard_map/ppermute | solution.py:1386
  195.3 2.7 collective-permute-start.16
  195.3 25.6 %collective-permute-start.14 = (bf16[512,1024]{1,0:T(8,128)(2,1)S(1)}, bf16[512,1024]{1,0:T(8,128)(2,1)S(1)}, u32[]{:S(2)}, u32[]{:S(2)}) collective-permute-start(bf16[512,1024]{1,0:T(8,128)(2,1)S(1)} %copy-done.40), channel_id=1, source_target_pairs={{0,2},{2,0},{1,3},{3,1},{4,6},{6,4},{5,7},{7,5},{8,10},{10,8},{9,1... | collective-permute-start | bytes 3145736 | tf_op jit(solution)/shard_map/ppermute | solution.py:1386
  196.7 24.2 %collective-permute-start.13 = (bf16[512,1024]{1,0:T(8,128)(2,1)S(1)}, bf16[512,1024]{1,0:T(8,128)(2,1)S(1)}, u32[]{:S(2)}, u32[]{:S(2)}) collective-permute-start(bf16[512,1024]{1,0:T(8,128)(2,1)S(1)} %copy-done.38), channel_id=1, source_target_pairs={{0,1},{1,0},{2,3},{3,2},{4,5},{5,4},{6,7},{7,6},{8,9},{9,8},{10,11... | collective-permute-start | bytes 3145736 | tf_op jit(solution)/shard_map/ppermute | solution.py:1386
  220.9 2.7 collective-permute-start.17
  271.0 462.6 %reduce-scatter.5.cloned.1.call-start = ((), (), s32[]{:S(2)}) async-start(), calls=%async_computation.3 | async-start | bytes 9437184 | tf_op jit(solution)/shard_map/reduce_scatter | solution.py:1718
  300.4 113.0 %collective-permute-start.21 = (bf16[512,2048]{1,0:T(8,128)(2,1)}, bf16[512,2048]{1,0:T(8,128)(2,1)}, u32[]{:S(2)}, u32[]{:S(2)}) collective-permute-start(bf16[512,2048]{1,0:T(8,128)(2,1)} %get-tuple-element.227), channel_id=1, source_target_pairs={{0,4},{4,0},{8,12},{12,8},{16,20},{20,16},{24,28},{28,24},{1,5},{5... | collective-permute-start | bytes 6291464 | tf_op jit(solution)/shard_map/ppermute | solution.py:1424
  302.0 115.0 %collective-permute-start.20 = (bf16[512,2048]{1,0:T(8,128)(2,1)}, bf16[512,2048]{1,0:T(8,128)(2,1)S(1)}, u32[]{:S(2)}, u32[]{:S(2)}) collective-permute-start(bf16[512,2048]{1,0:T(8,128)(2,1)} %get-tuple-element.226), channel_id=1, source_target_pairs={{0,8},{4,12},{8,0},{12,4},{16,24},{20,28},{24,16},{28,20},{1,9},{5... | collective-permute-start | bytes 6291464 | tf_op jit(solution)/shard_map/ppermute | solution.py:1424
  329.5 89.5 %collective-permute-start.19 = (bf16[1024,1024]{1,0:T(8,128)(2,1)}, bf16[1024,1024]{1,0:T(8,128)(2,1)}, u32[]{:S(2)}, u32[]{:S(2)}) collective-permute-start(bf16[1024,1024]{1,0:T(8,128)(2,1)} %second_grad.2), channel_id=1, source_target_pairs={{0,2},{2,0},{1,3},{3,1},{4,6},{6,4},{5,7},{7,5},{8,10},{10,8},{9,1... | collective-permute-start | bytes 6291464 | tf_op jit(solution)/shard_map/ppermute | solution.py:1386
  357.4 65.7 %collective-permute-start.18 = (bf16[1024,1024]{1,0:T(8,128)(2,1)}, bf16[1024,1024]{1,0:T(8,128)(2,1)}, u32[]{:S(2)}, u32[]{:S(2)}) collective-permute-start(bf16[1024,1024]{1,0:T(8,128)(2,1)} %second_grad.3), channel_id=1, source_target_pairs={{0,2},{2,0},{1,3},{3,1},{4,6},{6,4},{5,7},{7,5},{8,10},{10,8},{9,1... | collective-permute-start | bytes 6291464 | tf_op jit(solution)/shard_map/ppermute | solution.py:1386
  425.7 4.6 collective-permute-start.23
  444.1 4.4 collective-permute-start.22
  445.2 80.5 %collective-permute-start.26 = (bf16[256,2048]{1,0:T(8,128)(2,1)}, bf16[256,2048]{1,0:T(8,128)(2,1)}, u32[]{:S(2)}, u32[]{:S(2)}) collective-permute-start(bf16[256,2048]{1,0:T(8,128)(2,1)} %get-tuple-element.406), channel_id=1, source_target_pairs={{0,8},{4,12},{8,0},{12,4},{16,24},{20,28},{24,16},{28,20},{1,9},{5... | collective-permute-start | bytes 3145736 | tf_op jit(solution)/shard_map/ppermute | solution.py:1424
  445.8 79.9 %collective-permute-start.27 = (bf16[256,2048]{1,0:T(8,128)(2,1)}, bf16[256,2048]{1,0:T(8,128)(2,1)}, u32[]{:S(2)}, u32[]{:S(2)}) collective-permute-start(bf16[256,2048]{1,0:T(8,128)(2,1)} %get-tuple-element.404), channel_id=1, source_target_pairs={{0,16},{4,20},{8,24},{12,28},{16,0},{20,4},{24,8},{28,12},{1,17},{... | collective-permute-start | bytes 3145736 | tf_op jit(solution)/shard_map/ppermute | solution.py:1424
  477.3 48.5 %collective-permute-start.25 = (bf16[512,1024]{1,0:T(8,128)(2,1)}, bf16[512,1024]{1,0:T(8,128)(2,1)}, u32[]{:S(2)}, u32[]{:S(2)}) collective-permute-start(bf16[512,1024]{1,0:T(8,128)(2,1)} %get-tuple-element.250), channel_id=1, source_target_pairs={{0,4},{4,0},{8,12},{12,8},{16,20},{20,16},{24,28},{28,24},{1,5},{5... | collective-permute-start | bytes 3145736 | tf_op jit(solution)/shard_map/ppermute | solution.py:1424
  479.5 56.5 %collective-permute-start.24 = (bf16[1024,1024]{1,0:T(8,128)(2,1)}, bf16[1024,1024]{1,0:T(8,128)(2,1)}, u32[]{:S(2)}, u32[]{:S(2)}) collective-permute-start(bf16[1024,1024]{1,0:T(8,128)(2,1)} %slice.211), channel_id=1, source_target_pairs={{0,2},{2,0},{1,3},{3,1},{4,6},{6,4},{5,7},{7,5},{8,10},{10,8},{9,1... | collective-permute-start | bytes 6291464 | tf_op jit(solution)/shard_map/ppermute | solution.py:1386
  481.4 44.4 %copy-start.70 = (bf16[8,768]{1,0:T(8,128)(2,1)S(1)}, bf16[8,768]{1,0:T(8,128)(2,1)}, u32[]{:S(2)}) copy-start(bf16[8,768]{1,0:T(8,128)(2,1)} %copy-done.69) | copy-start | bytes 36868
  481.4 44.4 %copy-start.72 = (bf16[8,768]{1,0:T(8,128)(2,1)S(1)}, bf16[8,768]{1,0:T(8,128)(2,1)}, u32[]{:S(2)}) copy-start(bf16[8,768]{1,0:T(8,128)(2,1)} %copy-done.71) | copy-start | bytes 36868
  481.5 45.1 %copy-start.43 = (f32[2048,1]{1,0:T(8,128)S(1)}, f32[2048,1]{1,0:T(8,128)}, u32[]{:S(2)}) copy-start(f32[2048,1]{1,0:T(8,128)} %get-tuple-element.242) | copy-start | bytes 24580
  481.5 45.3 %copy-start.104 = (f32[1,1024]{1,0:T(1,128)S(1)}, f32[1,1024]{1,0:T(1,128)}, u32[]{:S(2)}) copy-start(f32[1,1024]{1,0:T(1,128)} %get-tuple-element.276) | copy-start | bytes 12292
  481.5 45.3 %copy-start.105 = (f32[1,1024]{1,0:T(1,128)S(1)}, f32[1,1024]{1,0:T(1,128)}, u32[]{:S(2)}) copy-start(f32[1,1024]{1,0:T(1,128)} %get-tuple-element.277) | copy-start | bytes 12292
  481.5 50.8 %copy-start.57 = (bf16[512,1024]{1,0:T(8,128)(2,1)S(1)}, bf16[512,1024]{1,0:T(8,128)(2,1)}, u32[]{:S(2)}) copy-start(bf16[512,1024]{1,0:T(8,128)(2,1)} %get-tuple-element.246) | copy-start | bytes 3145732
  525.8 17.7 %collective-permute-start.28 = (bf16[512,2048]{1,0:T(8,128)(2,1)S(1)}, bf16[512,2048]{1,0:T(8,128)(2,1)S(1)}, u32[]{:S(2)}, u32[]{:S(2)}) collective-permute-start(bf16[512,2048]{1,0:T(8,128)(2,1)S(1)} %get-tuple-element.255.refs_0_), channel_id=1, source_target_pairs={{0,1},{1,0},{2,3},{3,2},{4,5},{5,4},{6,7},{7,6},{8,9},{9,8},{10,11... | collective-permute-start | bytes 6291464 | tf_op jit(solution)/shard_map/ppermute | solution.py:1386
  527.4 15.5 %collective-permute-start.29 = (bf16[128,2048]{1,0:T(8,128)(2,1)S(1)}, bf16[128,2048]{1,0:T(8,128)(2,1)S(1)}, u32[]{:S(2)}, u32[]{:S(2)}) collective-permute-start(bf16[128,2048]{1,0:T(8,128)(2,1)S(1)} %get-tuple-element.258.refs_1_), channel_id=1, source_target_pairs={{0,1},{1,0},{2,3},{3,2},{4,5},{5,4},{6,7},{7,6},{8,9},{9,8},{10,11... | collective-permute-start | bytes 1572872 | tf_op jit(solution)/shard_map/ppermute | solution.py:1386
  527.9 15.6 %collective-permute-start.30 = (bf16[128,2048]{1,0:T(8,128)(2,1)S(1)}, bf16[128,2048]{1,0:T(8,128)(2,1)S(1)}, u32[]{:S(2)}, u32[]{:S(2)}) collective-permute-start(bf16[128,2048]{1,0:T(8,128)(2,1)S(1)} %get-tuple-element.259.refs_2_), channel_id=1, source_target_pairs={{0,1},{1,0},{2,3},{3,2},{4,5},{5,4},{6,7},{7,6},{8,9},{9,8},{10,11... | collective-permute-start | bytes 1572872 | tf_op jit(solution)/shard_map/ppermute | solution.py:1386
  534.8 68.8 %collective-permute-start.33 = (bf16[128,2048]{1,0:T(8,128)(2,1)S(1)}, bf16[128,2048]{1,0:T(8,128)(2,1)S(1)}, u32[]{:S(2)}, u32[]{:S(2)}) collective-permute-start(bf16[128,2048]{1,0:T(8,128)(2,1)S(1)} %get-tuple-element.412), channel_id=1, source_target_pairs={{0,4},{4,0},{8,12},{12,8},{16,20},{20,16},{24,28},{28,24},{1,5},{5... | collective-permute-start | bytes 1572872 | tf_op jit(solution)/shard_map/ppermute | solution.py:1424
  536.0 66.4 %collective-permute-start.34 = (bf16[128,2048]{1,0:T(8,128)(2,1)}, bf16[128,2048]{1,0:T(8,128)(2,1)}, u32[]{:S(2)}, u32[]{:S(2)}) collective-permute-start(bf16[128,2048]{1,0:T(8,128)(2,1)} %get-tuple-element.410), channel_id=1, source_target_pairs={{0,16},{4,20},{8,24},{12,28},{16,0},{20,4},{24,8},{28,12},{1,17},{... | collective-permute-start | bytes 1572872 | tf_op jit(solution)/shard_map/ppermute | solution.py:1424
  542.9 58.6 %collective-permute-start.35 = (bf16[256,1024]{1,0:T(8,128)(2,1)}, bf16[256,1024]{1,0:T(8,128)(2,1)S(1)}, u32[]{:S(2)}, u32[]{:S(2)}) collective-permute-start(bf16[256,1024]{1,0:T(8,128)(2,1)} %get-tuple-element.408), channel_id=1, source_target_pairs={{0,8},{4,12},{8,0},{12,4},{16,24},{20,28},{24,16},{28,20},{1,9},{5... | collective-permute-start | bytes 1572872 | tf_op jit(solution)/shard_map/ppermute | solution.py:1424
  562.7 26.2 %collective-permute-start.31 = (f32[32,2048]{1,0:T(8,128)S(1)}, f32[32,2048]{1,0:T(8,128)S(1)}, u32[]{:S(2)}, u32[]{:S(2)}) collective-permute-start(f32[32,2048]{1,0:T(8,128)S(1)} %pad_maximum_fusion.1), channel_id=1, source_target_pairs={{0,2},{2,0},{1,3},{3,1},{4,6},{6,4},{5,7},{7,5},{8,10},{10,8},{9,1... | collective-permute-start | bytes 786440 | tf_op jit(solution)/shard_map/ppermute | solution.py:1386
  563.5 25.4 %collective-permute-start.32 = (f32[1,1024]{1,0:T(1,128)}, f32[1,1024]{1,0:T(1,128)S(1)}, u32[]{:S(2)}, u32[]{:S(2)}) collective-permute-start(f32[1,1024]{1,0:T(1,128)} %get-tuple-element.264), channel_id=1, source_target_pairs={{0,2},{2,0},{1,3},{3,1},{4,6},{6,4},{5,7},{7,5},{8,10},{10,8},{9,1... | collective-permute-start | bytes 12296 | tf_op jit(solution)/shard_map/ppermute | solution.py:1386
  603.7 112.4 %copy-start.26 = (f32[1024,1024]{1,0:T(8,128)S(1)}, f32[1024,1024]{1,0:T(8,128)}, u32[]{:S(2)}) copy-start(f32[1024,1024]{1,0:T(8,128)} %add.215) | copy-start | bytes 12582916
  605.3 110.9 %copy-start.25 = (bf16[1024,1024]{1,0:T(8,128)(2,1)S(1)}, bf16[1024,1024]{1,0:T(8,128)(2,1)}, u32[]{:S(2)}) copy-start(bf16[1024,1024]{1,0:T(8,128)(2,1)} %in_mine.3) | copy-start | bytes 6291460
  719.0 7.7 %collective-permute-start.36 = (f32[1024]{0:T(1024)S(1)}, f32[1024]{0:T(1024)S(1)}, u32[]{:S(2)}, u32[]{:S(2)}) collective-permute-start(f32[1024]{0:T(1024)S(1)} %multiply_reduce_fusion), channel_id=1, source_target_pairs={{0,1},{1,0},{2,3},{3,2},{4,5},{5,4},{6,7},{7,6},{8,9},{9,8},{10,11... | collective-permute-start | bytes 12296 | tf_op jit(solution)/shard_map/ppermute | solution.py:1386
  719.1 13.6 %collective-permute-start.37 = (bf16[128,1024]{1,0:T(8,128)(2,1)S(1)}, bf16[128,1024]{1,0:T(8,128)(2,1)S(1)}, u32[]{:S(2)}, u32[]{:S(2)}) collective-permute-start(bf16[128,1024]{1,0:T(8,128)(2,1)S(1)} %copy-done.66), channel_id=1, source_target_pairs={{0,16},{4,20},{8,24},{12,28},{16,0},{20,4},{24,8},{28,12},{1,17},{... | collective-permute-start | bytes 786440 | tf_op jit(solution)/shard_map/ppermute | solution.py:1424
  (102 other events, 1093.0 us)
Sparse Core Ops, SparseCore 0:
  271.1 218.8 reduce-scatter.2
  494.1 208.2 reduce-scatter.4
